TPU v7x, 128 devices: a whole 4x4x4 slice. The times are simulated.
128 devices in a mesh: seq: 16 (over x, z), shard: 8 (over y, core).
Axes of the slice: x: 4, y: 4, z: 4, core: 2. Of those that a mesh axis runs over, the one named last changes fastest.
Arguments:
- stream: bfloat16 [8, 4096, 1152], P('shard', 'seq'), may hold values from -9 to 9
- doc_starts: int32 [8, 8], P('shard'), may hold values from 0 to 4095, as said below
- cotangent: bfloat16 [8, 4096, 1152], P('shard', 'seq'), may hold values from -6 to 6
- attention_norm: bfloat16 [1152], P(('seq', 'shard')), may hold values from 0.25 to 1.75
- query_weight: bfloat16 [1152, 1024], P(('seq', 'shard')), may hold values from -0.1875 to 0.1875
- key_weight: bfloat16 [1152, 256], P(('seq', 'shard')), may hold values from -0.1875 to 0.1875
- value_weight: bfloat16 [1152, 256], P(('seq', 'shard')), may hold values from -0.1875 to 0.1875
- query_norm: bfloat16 [256], P(('seq', 'shard')), may hold values from 0.25 to 1.75
- key_norm: bfloat16 [256], P(('seq', 'shard')), may hold values from 0.25 to 1.75
- output_weight: bfloat16 [1024, 1152], P(('seq', 'shard')), may hold values from -0.1875 to 0.1875
- attention_post_norm: bfloat16 [1152], P(('seq', 'shard')), may hold values from 0.25 to 1.75
- mlp_norm: bfloat16 [1152], P(('seq', 'shard')), may hold values from 0.25 to 1.75
- gate_weight: bfloat16 [1152, 6912], P(('seq', 'shard')), may hold values from -0.1875 to 0.1875
- up_weight: bfloat16 [1152, 6912], P(('seq', 'shard')), may hold values from -0.1875 to 0.1875
- down_weight: bfloat16 [6912, 1152], P(('seq', 'shard')), may hold values from -0.078125 to 0.078125
- mlp_post_norm: bfloat16 [1152], P(('seq', 'shard')), may hold values from 0.25 to 1.75
Outputs:
- block_output: bfloat16 [8, 4096, 1152], P('shard', 'seq')
- stream_grad: bfloat16 [8, 4096, 1152], P('shard', 'seq')
- attention_norm_grad: float32 [1152], P(('seq', 'shard'))
- query_weight_grad: float32 [1152, 1024], P(('seq', 'shard'))
- key_weight_grad: float32 [1152, 256], P(('seq', 'shard'))
- value_weight_grad: float32 [1152, 256], P(('seq', 'shard'))
- query_norm_grad: float32 [256], P(('seq', 'shard'))
- key_norm_grad: float32 [256], P(('seq', 'shard'))
- output_weight_grad: float32 [1024, 1152], P(('seq', 'shard'))
- attention_post_norm_grad: float32 [1152], P(('seq', 'shard'))
- mlp_norm_grad: float32 [1152], P(('seq', 'shard'))
- gate_weight_grad: float32 [1152, 6912], P(('seq', 'shard'))
- up_weight_grad: float32 [1152, 6912], P(('seq', 'shard'))
- down_weight_grad: float32 [6912, 1152], P(('seq', 'shard'))
- mlp_post_norm_grad: float32 [1152], P(('seq', 'shard'))
- stream_rms: float32 [3], replicated
Inputs may be any that keep to these rules, and one draw needn't show every extreme that they name: `doc_starts`: each row is non-decreasing and begins with 0. In every draw one sequence, drawn from the seed, has all entries 0: it is one document.
All inputs are finite; a program needn't handle non-finite values.
Results may differ from a plain program's by a relative error of at most 0.025.
Values may be sent and summed in bfloat16 or wider, within the bound.
A program may use at most 192 MiB of HBM per device.

v0:
```python
import math

import jax
import jax.numpy as jnp
from jax import lax
from jax.sharding import PartitionSpec as P

D = 1152
HEADS = 4
HEAD_DIM = 256
WINDOW = 512


EPSILON = 1e-06
NEGATIVE = -1e30


def from_behind(value, axis, by):
    length = lax.axis_size(axis)
    pairs = [(i, i + by) for i in range(length) if 0 <= i + by < length]
    return lax.ppermute(value, axis, pairs)


def norm_rows(values, weight):
    return values * lax.rsqrt(jnp.mean(values * values, axis=-1, keepdims=True) + EPSILON) * weight


def rotate(values, angles):
    middle = values.shape[-1] // 2
    leading = values[..., :middle]
    trailing = values[..., middle:]
    cosine = jnp.cos(angles)
    sine_part = jnp.sin(angles)
    return jnp.concatenate(
        [leading * cosine - trailing * sine_part, trailing * cosine + leading * sine_part], axis=-1
    )


def head_prep(values, weight, angles):
    return rotate(norm_rows(values, weight), angles)


def geglu(gate_part, up_part):
    return jax.nn.gelu(gate_part, approximate=True) * up_part


def frequencies(width):
    return jnp.exp(jnp.arange(width // 2, dtype=jnp.float32) * (-2.0 * math.log(10000.0) / width))


def block_scores(query_part, key_part, query_place, key_place, query_begin, scale):
    allowed = (
        (key_place[None, :] <= query_place[:, None])
        & (key_place[None, :] > query_place[:, None] - WINDOW)
        & (key_place[None, :] >= query_begin[:, None])
    )
    raw = jnp.einsum("qhd,kd->hqk", query_part, key_part, preferred_element_type=jnp.float32)
    return jnp.where(allowed[None], raw * scale, NEGATIVE)


def as_float(gathered):
    return tuple((piece.astype(jnp.float32) if piece.ndim == 1 else piece for piece in gathered))


def gather_attention(
    query_weight,
    key_weight,
    value_weight,
    output_weight,
    attention_norm,
    query_norm,
    key_norm,
    attention_post_norm,
    mlp_norm,
    mlp_post_norm,
):
    return as_float(
        (
            lax.all_gather(query_weight, ("seq", "shard"), axis=0, tiled=True),
            lax.all_gather(key_weight, ("seq", "shard"), axis=0, tiled=True),
            lax.all_gather(value_weight, ("seq", "shard"), axis=0, tiled=True),
            lax.all_gather(output_weight, ("seq", "shard"), axis=0, tiled=True),
            lax.all_gather(attention_norm, ("seq", "shard"), axis=0, tiled=True),
            lax.all_gather(query_norm, ("seq", "shard"), axis=0, tiled=True),
            lax.all_gather(key_norm, ("seq", "shard"), axis=0, tiled=True),
            lax.all_gather(attention_post_norm, ("seq", "shard"), axis=0, tiled=True),
            lax.all_gather(mlp_norm, ("seq", "shard"), axis=0, tiled=True),
            lax.all_gather(mlp_post_norm, ("seq", "shard"), axis=0, tiled=True),
        )
    )


def local(
    stream,
    doc_starts,
    cotangent,
    attention_norm,
    query_weight,
    key_weight,
    value_weight,
    query_norm,
    key_norm,
    output_weight,
    attention_post_norm,
    mlp_norm,
    gate_weight,
    up_weight,
    down_weight,
    mlp_post_norm,
):
    tokens = stream.shape[1]
    seq_count = lax.axis_size("seq")
    shard_count = lax.axis_size("shard")
    rows_local = gate_weight.shape[0]
    ff_piece = gate_weight.shape[1] // (seq_count * shard_count)
    halo_blocks = max(1, WINDOW // tokens)
    query_rows = min(tokens, 512)
    key_span = query_rows + WINDOW
    scale = HEAD_DIM ** (-0.5)
    inputs = stream[0].astype(jnp.float32)
    offset = lax.axis_index("seq") * tokens
    positions = offset + jnp.arange(tokens, dtype=jnp.int32)
    starts_row = doc_starts[0]
    beginning = jnp.max(
        jnp.where(starts_row[None, :] <= positions[:, None], starts_row[None, :], 0), axis=1
    )
    angles = (positions - beginning).astype(jnp.float32)[:, None] * frequencies(HEAD_DIM)[None, :]
    attention_set = gather_attention(
        query_weight,
        key_weight,
        value_weight,
        output_weight,
        attention_norm,
        query_norm,
        key_norm,
        attention_post_norm,
        mlp_norm,
        mlp_post_norm,
    )
    (
        full_query,
        full_key,
        full_value,
        full_output,
        gain_input,
        gain_query,
        gain_key,
        gain_post,
        gain_mlp,
        gain_mlp_post,
    ) = attention_set
    normed = norm_rows(inputs, gain_input).astype(jnp.bfloat16)
    query_proj = jnp.dot(normed, full_query, preferred_element_type=jnp.float32).reshape(
        tokens, HEADS, HEAD_DIM
    )
    key_proj = jnp.dot(normed, full_key, preferred_element_type=jnp.float32)
    values_low = jnp.dot(normed, full_value, preferred_element_type=jnp.float32).astype(
        jnp.bfloat16
    )
    query_rot = head_prep(query_proj, gain_query, angles[:, None, :]).astype(jnp.bfloat16)
    key_rot = head_prep(key_proj, gain_key, angles).astype(jnp.bfloat16)
    far_keys = []
    far_values = []
    for distance in range(halo_blocks, 0, -1):
        received = from_behind((key_rot, values_low), "seq", distance)
        far_keys.append(received[0])
        far_values.append(received[1])
    keys_all = jnp.concatenate(far_keys + [key_rot], axis=0)
    values_all = jnp.concatenate(far_values + [values_low], axis=0)
    key_base = offset - halo_blocks * tokens

    def scores_of(number):
        query_low = number * query_rows
        key_low = halo_blocks * tokens + query_low - WINDOW
        key_place = key_base + key_low + jnp.arange(key_span, dtype=jnp.int32)
        scores = block_scores(query_rot, keys_all, positions, key_place, beginning, scale)
        return (scores, query_low, key_low)

    number = 0
    scores, query_low, key_low = scores_of(number)
    highest = jnp.max(scores, axis=-1, keepdims=True)
    exponent = jnp.exp(scores - highest)
    totals = jnp.sum(exponent, axis=-1, keepdims=True)
    probability = (exponent / totals).astype(jnp.bfloat16)
    mixed_parts = jnp.einsum(
        "hqk,kd->qhd", probability, values_all, preferred_element_type=jnp.float32
    )
    log_totals = [highest + jnp.log(totals)]
    mixed = mixed_parts.reshape(tokens, HEADS * HEAD_DIM).astype(jnp.bfloat16)
    branch = jnp.dot(mixed, full_output, preferred_element_type=jnp.float32)
    hidden = inputs + norm_rows(branch, gain_post)
    feed = norm_rows(hidden, gain_mlp).astype(jnp.bfloat16)
    gate_split = gate_weight.reshape(rows_local, seq_count, shard_count, ff_piece)
    up_split = up_weight.reshape(rows_local, seq_count, shard_count, ff_piece)
    column_parts = (
        lax.all_to_all(gate_split, "shard", split_axis=2, concat_axis=0, tiled=True),
        lax.all_to_all(up_split, "shard", split_axis=2, concat_axis=0, tiled=True),
    )
    row_sets = (
        lax.all_gather(column_parts[0], "seq", axis=0, tiled=True),
        lax.all_gather(column_parts[1], "seq", axis=0, tiled=True),
        lax.all_gather(down_weight, "seq", axis=0, tiled=True),
    )
    full_gate = row_sets[0].reshape(D, seq_count * ff_piece)
    full_up = row_sets[1].reshape(D, seq_count * ff_piece)
    full_down = row_sets[2]
    feed_all = lax.all_gather(feed, "shard", axis=0, tiled=True)
    gate_out = jnp.dot(feed_all, full_gate, preferred_element_type=jnp.float32)
    up_out = jnp.dot(feed_all, full_up, preferred_element_type=jnp.float32)
    active = geglu(gate_out, up_out).astype(jnp.bfloat16)
    down_out = lax.psum_scatter(
        jnp.dot(active, full_down, preferred_element_type=jnp.float32),
        "shard",
        scatter_dimension=0,
        tiled=True,
    )
    result = hidden + norm_rows(down_out, gain_mlp_post)
    square_sums = lax.psum(
        (jnp.sum(inputs * inputs), jnp.sum(hidden * hidden), jnp.sum(result * result)),
        ("seq", "shard"),
    )
    element_count = tokens * seq_count * shard_count * D
    stream_rms = jnp.sqrt(jnp.stack(square_sums) / element_count)
    upstream = cotangent[0].astype(jnp.float32)
    result_back = jax.vjp(norm_rows, down_out, gain_mlp_post)[1]
    down_grad, gain_mlp_post_grad = result_back(upstream)
    down_low = down_grad.astype(jnp.bfloat16)
    down_all = lax.all_gather(down_low, "shard", axis=0, tiled=True)
    active_grad = jnp.einsum("td,fd->tf", down_all, full_down, preferred_element_type=jnp.float32)
    down_weight_term = jnp.einsum("tf,td->fd", active, down_all, preferred_element_type=jnp.float32)
    gate_grad, up_grad = jax.vjp(geglu, gate_out, up_out)[1](active_grad)
    gate_low = gate_grad.astype(jnp.bfloat16)
    up_low = up_grad.astype(jnp.bfloat16)
    gate_weight_term = jnp.einsum(
        "td,tf->df", feed_all, gate_low, preferred_element_type=jnp.float32
    )
    up_weight_term = jnp.einsum("td,tf->df", feed_all, up_low, preferred_element_type=jnp.float32)
    feed_grad = lax.psum_scatter(
        jnp.einsum("tf,df->td", gate_low, full_gate, preferred_element_type=jnp.float32)
        + jnp.einsum("tf,df->td", up_low, full_up, preferred_element_type=jnp.float32),
        "shard",
        scatter_dimension=0,
        tiled=True,
    )
    hidden_extra, gain_mlp_grad = jax.vjp(norm_rows, hidden, gain_mlp)[1](feed_grad)
    hidden_grad = upstream + hidden_extra
    branch_grad, gain_post_grad = jax.vjp(norm_rows, branch, gain_post)[1](hidden_grad)
    branch_low = branch_grad.astype(jnp.bfloat16)
    output_weight_term = jnp.einsum(
        "tn,td->nd", mixed, branch_low, preferred_element_type=jnp.float32
    )
    mixed_grad = (
        jnp.einsum("td,nd->tn", branch_low, full_output, preferred_element_type=jnp.float32)
        .astype(jnp.bfloat16)
        .reshape(tokens, HEADS, HEAD_DIM)
    )
    key_grads = jnp.zeros((keys_all.shape[0], HEAD_DIM), jnp.float32)
    value_grads = jnp.zeros((keys_all.shape[0], HEAD_DIM), jnp.float32)
    number = 0
    scores, query_low, key_low = scores_of(number)
    probability = jnp.exp(scores - log_totals[number])
    probability_low = probability.astype(jnp.bfloat16)
    prob_grad = jnp.einsum(
        "qhd,kd->hqk", mixed_grad, values_all, preferred_element_type=jnp.float32
    )
    inner_sum = jnp.sum(probability * prob_grad, axis=-1, keepdims=True)
    score_low = (probability * (prob_grad - inner_sum) * scale).astype(jnp.bfloat16)
    query_grad_parts = jnp.einsum(
        "hqk,kd->qhd", score_low, keys_all, preferred_element_type=jnp.float32
    )
    key_grads = key_grads.at[key_low : key_low + key_span].add(
        jnp.einsum("hqk,qhd->kd", score_low, query_rot, preferred_element_type=jnp.float32)
    )
    value_grads = value_grads.at[key_low : key_low + key_span].add(
        jnp.einsum("hqk,qhd->kd", probability_low, mixed_grad, preferred_element_type=jnp.float32)
    )
    own_key_grad = key_grads[halo_blocks * tokens :]
    own_value_grad = value_grads[halo_blocks * tokens :]
    for distance in range(1, halo_blocks + 1):
        piece_low = (halo_blocks - distance) * tokens
        returned = (
            from_behind(
                key_grads[piece_low : piece_low + tokens].astype(jnp.bfloat16), "seq", -distance
            ).astype(jnp.float32),
            from_behind(
                value_grads[piece_low : piece_low + tokens].astype(jnp.bfloat16), "seq", -distance
            ).astype(jnp.float32),
        )
        own_key_grad = own_key_grad + returned[0]
        own_value_grad = own_value_grad + returned[1]
    query_back = jax.vjp(
        lambda values, weight: head_prep(values, weight, angles[:, None, :]), query_proj, gain_query
    )[1]
    query_grad, gain_query_grad = query_back(query_grad_parts)
    key_back = jax.vjp(
        lambda values, weight: head_prep(values, weight, angles), key_proj, gain_key
    )[1]
    key_grad, gain_key_grad = key_back(own_key_grad)
    query_low_grad = query_grad.reshape(tokens, HEADS * HEAD_DIM).astype(jnp.bfloat16)
    key_low_grad = key_grad.astype(jnp.bfloat16)
    value_low_grad = own_value_grad.astype(jnp.bfloat16)
    query_weight_term = jnp.einsum(
        "td,tn->dn", normed, query_low_grad, preferred_element_type=jnp.float32
    )
    key_weight_term = jnp.einsum(
        "td,tn->dn", normed, key_low_grad, preferred_element_type=jnp.float32
    )
    value_weight_term = jnp.einsum(
        "td,tn->dn", normed, value_low_grad, preferred_element_type=jnp.float32
    )
    normed_grad = (
        jnp.einsum("tn,dn->td", query_low_grad, full_query, preferred_element_type=jnp.float32)
        + jnp.einsum("tn,dn->td", key_low_grad, full_key, preferred_element_type=jnp.float32)
        + jnp.einsum("tn,dn->td", value_low_grad, full_value, preferred_element_type=jnp.float32)
    )
    input_extra, gain_input_grad = jax.vjp(norm_rows, inputs, gain_input)[1](normed_grad)
    stream_grad = (hidden_grad + input_extra).astype(jnp.bfloat16)
    attention_shares = (
        lax.psum_scatter(query_weight_term, ("seq", "shard"), scatter_dimension=0, tiled=True),
        lax.psum_scatter(key_weight_term, ("seq", "shard"), scatter_dimension=0, tiled=True),
        lax.psum_scatter(value_weight_term, ("seq", "shard"), scatter_dimension=0, tiled=True),
        lax.psum_scatter(output_weight_term, ("seq", "shard"), scatter_dimension=0, tiled=True),
        lax.psum_scatter(gain_input_grad, ("seq", "shard"), scatter_dimension=0, tiled=True),
        lax.psum_scatter(gain_query_grad, ("seq", "shard"), scatter_dimension=0, tiled=True),
        lax.psum_scatter(gain_key_grad, ("seq", "shard"), scatter_dimension=0, tiled=True),
        lax.psum_scatter(gain_post_grad, ("seq", "shard"), scatter_dimension=0, tiled=True),
        lax.psum_scatter(gain_mlp_grad, ("seq", "shard"), scatter_dimension=0, tiled=True),
        lax.psum_scatter(gain_mlp_post_grad, ("seq", "shard"), scatter_dimension=0, tiled=True),
    )
    block_sums = (
        lax.psum_scatter(
            gate_weight_term.reshape(D, seq_count, 1, ff_piece).astype(jnp.bfloat16),
            "seq",
            scatter_dimension=0,
            tiled=True,
        ).astype(jnp.float32),
        lax.psum_scatter(
            up_weight_term.reshape(D, seq_count, 1, ff_piece).astype(jnp.bfloat16),
            "seq",
            scatter_dimension=0,
            tiled=True,
        ).astype(jnp.float32),
        lax.psum_scatter(
            down_weight_term.astype(jnp.bfloat16), "seq", scatter_dimension=0, tiled=True
        ).astype(jnp.float32),
    )
    returned_rows = (
        lax.all_to_all(
            block_sums[0].astype(jnp.bfloat16), "shard", split_axis=0, concat_axis=2, tiled=True
        ).astype(jnp.float32),
        lax.all_to_all(
            block_sums[1].astype(jnp.bfloat16), "shard", split_axis=0, concat_axis=2, tiled=True
        ).astype(jnp.float32),
    )
    gate_share = returned_rows[0].reshape(rows_local, seq_count * shard_count * ff_piece)
    up_share = returned_rows[1].reshape(rows_local, seq_count * shard_count * ff_piece)
    down_share = block_sums[2]
    block_output = result.astype(jnp.bfloat16)[None]
    return (
        block_output,
        stream_grad[None],
        attention_shares[4],
        attention_shares[0],
        attention_shares[1],
        attention_shares[2],
        attention_shares[5],
        attention_shares[6],
        attention_shares[3],
        attention_shares[7],
        attention_shares[8],
        gate_share,
        up_share,
        down_share,
        attention_shares[9],
        stream_rms,
    )


def solution(mesh):
    placed = (
        P("shard", "seq", None),
        P("shard", None),
        P("shard", "seq", None),
        P(("seq", "shard")),
        P(("seq", "shard"), None),
        P(("seq", "shard"), None),
        P(("seq", "shard"), None),
        P(("seq", "shard")),
        P(("seq", "shard")),
        P(("seq", "shard"), None),
        P(("seq", "shard")),
        P(("seq", "shard")),
        P(("seq", "shard"), None),
        P(("seq", "shard"), None),
        P(("seq", "shard"), None),
        P(("seq", "shard")),
    )
    return jax.shard_map(
        local,
        mesh=mesh,
        in_specs=placed,
        out_specs=(
            P("shard", "seq", None),
            P("shard", "seq", None),
            P(("seq", "shard")),
            P(("seq", "shard"), None),
            P(("seq", "shard"), None),
            P(("seq", "shard"), None),
            P(("seq", "shard")),
            P(("seq", "shard")),
            P(("seq", "shard"), None),
            P(("seq", "shard")),
            P(("seq", "shard")),
            P(("seq", "shard"), None),
            P(("seq", "shard"), None),
            P(("seq", "shard"), None),
            P(("seq", "shard")),
            P(),
        ),
        check_vma=False,
    )
```

profile of v0, /device:TPU:1, one launch (start us, length us, event | category | flops | bytes accessed | tf_op | source)
XLA Modules:
  0.0 863.6 jit_solution(18017608271514179657)
XLA Ops:
  9.5 1.7 reshape.461
  11.7 11.0 %all_to_all.54 = bf16[8,2,3888]{2,1,0:T(2,128)(2,1)S(1)} all-to-all(bf16[8,2,3888]{2,1,0:T(2,128)(2,1)S(1)} %reshape.510), channel_id=1, replica_groups=mesh['seq'=16,'shard'=8] {'shard'}, dimensions={0} | all-to-all | bytes 248832 | tf_op jit(solution)/shard_map/all_to_all | solution.py:196
  25.4 66.7 %all-reduce.26 = (bf16[1152]{0:T(1024)(128)(2,1)S(1)}, bf16[256]{0:T(256)(128)(2,1)S(1)}, bf16[256]{0:T(256)(128)(2,1)S(1)}, bf16[1152]{0:T(1024)(128)(2,1)S(1)}...) all-reduce(bf16[1152]{0:T(1024)(128)(2,1)S(1)} %dynamic-update-slic, ...), channel_id=1, replica_groups=mesh['seq'=16,'shard'=8] {'seq','shard'}, use_global_device_ids=true, to_apply=%add.4 | all-reduce | flops 5120 | bytes 20480
  92.1 34.6 %all-gather.1 = bf16[128,9,256]{2,1,0:T(8,128)(2,1)S(1)} all-gather(bf16[1,9,256]{2,1,0:T(8,128)(2,1)S(1)} %bitcast.259), channel_id=1, replica_groups=mesh['seq'=16,'shard'=8] {'seq','shard'}, dimensions={0}, use_global_device_ids=true | all-gather | bytes 594432 | tf_op jit(solution)/shard_map/all_gather | solution.py:80
  129.8 4.1 collective-permute-start.2
  133.9 3.6 collective-permute-start.3
  137.5 35.7 %all-gather = bf16[128,9,256]{2,1,0:T(8,128)(2,1)S(1)} all-gather(bf16[1,9,256]{2,1,0:T(8,128)(2,1)S(1)} %bitcast.260), channel_id=1, replica_groups=mesh['seq'=16,'shard'=8] {'seq','shard'}, dimensions={0}, use_global_device_ids=true | all-gather | bytes 594432 | tf_op jit(solution)/shard_map/all_gather | solution.py:81
  174.6 3.7 collective-permute-start
  178.3 2.0 collective-permute-start.1
  182.3 4.9 all-to-all-start.1
  188.7 3.7 all-to-all-done.1
  193.6 4.2 reshape.489
  197.8 2.8 copy.104
  200.6 2.6 multiply_reduce_fusion.11
  204.6 1.7 fusion.108
  207.9 1.8 fusion.33
  209.7 2.8 multiply_reduce_fusion.6
  214.7 2.8 reshape.491
  217.5 34.8 %all-gather.16.cloned.1.call-done = bf16[1152,16,1,54]{3,1,2,0:T(8,128)(2,1)} async-done(((bf16[72,16,1,54]{3,1,2,0:T(8,128)(2,1)}), bf16[1152,16,1,54]{3,1,2,0:T(8,128)(2,1)}) %all-gather.16.cloned.1.call-update) | async-done | bytes 1990672 | tf_op jit(solution)/shard_map/all_gather | solution.py:200
  252.3 8.0 reshape.499
  260.3 48.3 %all-gather.18.cloned.1.call-done = bf16[1152,16,1,54]{3,1,2,0:T(8,128)(2,1)} async-done(((bf16[72,16,1,54]{3,1,2,0:T(8,128)(2,1)}), bf16[1152,16,1,54]{3,1,2,0:T(8,128)(2,1)}) %all-gather.18.cloned.1.call-update) | async-done | bytes 1990672 | tf_op jit(solution)/shard_map/all_gather | solution.py:201
  308.6 8.1 reshape.500
  316.7 28.4 %all-gather.14.cloned.1.call-done = bf16[2048,1152]{1,0:T(8,128)(2,1)} async-done(((bf16[256,1152]{1,0:T(8,128)(2,1)}), bf16[2048,1152]{1,0:T(8,128)(2,1)}) %all-gather.14.cloned.1.call-update) | async-done | bytes 4718608 | tf_op jit(solution)/shard_map/all_gather | solution.py:207
  345.1 7.6 fusion.111
  352.7 8.6 multiply_convert_fusion.1
  361.4 1.9 copy-done.94
  363.2 8.1 fusion.112
  372.8 55.0 %reduce-scatter.7.cloned.1.call-done = f32[256,1152]{1,0:T(8,128)} async-done(((f32[2048,1152]{1,0:T(8,128)}), f32[256,1152]{1,0:T(8,128)}) %reduce-scatter.7.cloned.1.call-update) | async-done | bytes 1179664 | tf_op jit(solution)/shard_map/reduce_scatter | solution.py:211
  427.9 1.5 multiply_reduce_fusion.5
  429.4 3.5 fusion.48
  434.1 35.0 %all-gather.20.cloned.1.call-done = bf16[2048,1152]{1,0:T(8,128)(2,1)} async-done(((bf16[256,1152]{1,0:T(8,128)(2,1)}), bf16[2048,1152]{1,0:T(8,128)(2,1)}) %all-gather.20.cloned.1.call-update) | async-done | bytes 4718608 | tf_op jit(solution)/shard_map/all_gather | solution.py:228
  469.1 14.8 %multiply_convert_fusion = (bf16[2048,864]{0,1:T(8,128)(2,1)S(1)}, bf16[2048,864]{0,1:T(8,128)(2,1)S(1)}) fusion(f32[2048,864]{0,1:T(8,128)} %copy-done.92, f32[2048,864]{0,1:T(8,128)} %get-tuple-element.123, bf16[2048,1152]{1,0:T(8,128)(2,1)} %all-gather.20.cloned.1.call-done, bf16[864,1152]{1,0:T(8,128)(2,1)} %reshape.491), kind=kOutput, calls=%fused_computation.11 | convolution fusion | flops 4119330816 | bytes 27942912 | tf_op jit(solution)/shard_map/td,fd->tf/dot_general | solution.py:229
  484.0 5.8 fusion.113
  489.8 8.6 convolution_add_fusion
  499.8 9.4 %convolution_convert_fusion.1 = bf16[1152,864]{0,1:T(8,128)(2,1)} fusion(bf16[2048,864]{0,1:T(8,128)(2,1)} %copy-done.95, bf16[2048,1152]{1,0:T(8,128)(2,1)} %all-gather.14.cloned.1.call-done), kind=kOutput, calls=%fused_computation.15 | convolution fusion | flops 4077858816 | bytes 10248192 | tf_op jit(solution)/shard_map/td,tf->df/dot_general | solution.py:234
  509.2 2.8 convert_element_type.233
  512.0 9.6 %convolution_convert_fusion = bf16[1152,864]{0,1:T(8,128)(2,1)} fusion(bf16[2048,864]{0,1:T(8,128)(2,1)} %copy-done.93, bf16[2048,1152]{1,0:T(8,128)(2,1)} %all-gather.14.cloned.1.call-done), kind=kOutput, calls=%fused_computation.14 | convolution fusion | flops 4077858816 | bytes 10248192 | tf_op jit(solution)/shard_map/td,tf->df/dot_general | solution.py:237
  521.6 2.8 convert_element_type.239
  524.5 30.5 %reduce-scatter.9.cloned.1.call-done = f32[256,1152]{1,0:T(8,128)} async-done(((f32[2048,1152]{1,0:T(8,128)}), f32[256,1152]{1,0:T(8,128)}) %reduce-scatter.9.cloned.1.call-update) | async-done | bytes 1179664 | tf_op jit(solution)/shard_map/reduce_scatter | solution.py:238
  555.0 2.2 multiply_reduce_fusion.1
  559.0 1.8 copy-done.18
  566.6 3.5 fusion.56
  570.1 7.2 fusion.109
  579.3 1.6 collective-permute-start.5
  580.9 6.4 fusion.32
  589.6 3.0 fusion.115
  592.7 3.1 fusion.53
  600.5 1.5 fusion.99
  602.0 8.1 convolution_convert_fusion.2
  610.2 59.4 %fusion = bf16[64,1152]{1,0:T(8,128)(2,1)S(1)} fusion(bf16[864,1152]{1,0:T(8,128)(2,1)S(1)} %convolution_convert_fusion.2), kind=kCustom, calls=%all-reduce-scatter | all-reduce-scatter fusion | flops 1179649 | bytes 2138624
  669.5 2.4 collective-permute-start.8
  672.0 4.0 collective-permute-start.9
  676.1 2.4 collective-permute-start.10
  684.3 9.4 %all-to-all-start.2 = ((bf16[8,2,3888]{2,1,0:T(2,128)(2,1)}), bf16[8,2,3888]{2,1,0:T(2,128)(2,1)S(1)}, u32[]{:S(2)}, u32[]{:S(2)}) async-start(bf16[8,2,3888]{2,1,0:T(2,128)(2,1)} %reshape.512), calls=%async_computation.4 | async-start | bytes 253952 | tf_op jit(solution)/shard_map/all_to_all | solution.py:348
  695.8 3.2 all-to-all-done.2
  699.0 4.9 all-to-all-start.3
  705.3 2.4 reshape.468
  707.7 2.0 all-to-all-done.3
  709.7 2.0 reshape.515
  713.7 2.3 reshape.469
  719.4 67.1 %all-reduce.24 = (f32[1152]{0:T(1024)S(1)}, f32[256]{0:T(256)S(1)}, f32[256]{0:T(256)S(1)}, f32[1152]{0:T(1024)S(1)}, f32[1152]{0:T(1024)S(1)}, /*index=5*/f32[1...) all-reduce(f32[1152]{0:T(1024)S(1)} %get-tuple-element.64, ...), channel_id=4, replica_groups=mesh['seq'=16,'shard'=8] {'seq','shard'}, use_global_device_ids=true, to_apply=%region_19.20.clone | all-reduce | flops 5123 | bytes 40984
  790.1 2.5 fusion.87
  793.8 58.7 %all-reduce.31.cloned.1.call-done = (f32[1152,1024]{1,0:T(8,128)}, f32[1152,256]{1,0:T(8,128)}, f32[1152,256]{1,0:T(8,128)}, f32[1024,1152]{1,0:T(8,128)}) async-done(((f32[1152,1024]{1,0:T(8,128)}, f32[1152,256]{1,0:T(8,128)}, f32[1152,256]{1,0:T(8,128)}, f32[1024,1152]{1,0:T(8,128)}), (f32[1152,1024]{1,0:T(8,128)}, f32[1152,256]{1,0:T(8,128)}, f32[1152,256]{1,0:T(8,128)}, ...) | async-done | bytes 11796496
  852.5 1.5 constant_dynamic-slice_fusion.5
  (330 shorter events, 60.5 us)
Async XLA Ops:
  7.2 16.7 %copy-start.86 = (bf16[9]{0:T(256)(128)(2,1)S(1)}, bf16[9]{0:T(256)(128)(2,1)}, u32[]{:S(2)}) copy-start(bf16[9]{0:T(256)(128)(2,1)} %param.27) | copy-start | bytes 58
  7.2 16.9 %copy-start.87 = (bf16[9]{0:T(256)(128)(2,1)S(1)}, bf16[9]{0:T(256)(128)(2,1)}, u32[]{:S(2)}) copy-start(bf16[9]{0:T(256)(128)(2,1)} %param.34) | copy-start | bytes 58
  7.2 17.2 %copy-start.88 = (bf16[9]{0:T(256)(128)(2,1)S(1)}, bf16[9]{0:T(256)(128)(2,1)}, u32[]{:S(2)}) copy-start(bf16[9]{0:T(256)(128)(2,1)} %param.35) | copy-start | bytes 58
  7.2 17.4 %copy-start.89 = (bf16[9]{0:T(256)(128)(2,1)S(1)}, bf16[9]{0:T(256)(128)(2,1)}, u32[]{:S(2)}) copy-start(bf16[9]{0:T(256)(128)(2,1)} %param.39) | copy-start | bytes 58
  7.2 17.6 %copy-start.90 = (bf16[2]{0:T(256)(128)(2,1)S(1)}, bf16[2]{0:T(256)(128)(2,1)}, u32[]{:S(2)}) copy-start(bf16[2]{0:T(256)(128)(2,1)} %param.32) | copy-start | bytes 16
  7.2 17.9 %copy-start.91 = (bf16[2]{0:T(256)(128)(2,1)S(1)}, bf16[2]{0:T(256)(128)(2,1)}, u32[]{:S(2)}) copy-start(bf16[2]{0:T(256)(128)(2,1)} %param.31) | copy-start | bytes 16
  7.2 84.8 %copy-start.77 = (bf16[9,256]{1,0:T(8,128)(2,1)S(1)}, bf16[9,256]{1,0:T(8,128)(2,1)}, u32[]{:S(2)}) copy-start(bf16[9,256]{1,0:T(8,128)(2,1)} %param.29) | copy-start | bytes 13828
  7.3 186.4 %all-gather.22.cloned.1.call-start = ((), (), s32[]{:S(2)}) async-start(), calls=%async_computation.13 | async-start | bytes 4227072 | tf_op jit(solution)/shard_map/all_gather | solution.py:79
  8.0 201.7 %all-gather.12.cloned.1.call-start = ((), (), s32[]{:S(2)}) async-start(), calls=%async_computation.6 | async-start | bytes 2377728 | tf_op jit(solution)/shard_map/all_gather | solution.py:82
  8.7 205.9 %all-gather.24.cloned.1.call-start = ((), (), s32[]{:S(2)}) async-start(), calls=%async_computation.14 | async-start | bytes 2193408 | tf_op jit(solution)/shard_map/all_gather | solution.py:202
  9.5 242.8 %all-gather.16.cloned.1.call-start = ((), (), s32[]{:S(2)}) async-start(), calls=%async_computation.8 | async-start | bytes 5013504 | tf_op jit(solution)/shard_map/all_gather | solution.py:200
  11.2 115.9 %copy-start.84 = (s32[1,8]{1,0:T(1,128)S(1)}, s32[1,8]{1,0:T(1,128)}, u32[]{:S(2)}) copy-start(s32[1,8]{1,0:T(1,128)} %param.25) | copy-start | bytes 100
  11.2 116.0 %copy-start = (bf16[1,256,1152]{2,1,0:T(8,128)(2,1)S(1)}, bf16[1,256,1152]{2,1,0:T(8,128)(2,1)}, u32[]{:S(2)}) copy-start(bf16[1,256,1152]{2,1,0:T(8,128)(2,1)} %param.24) | copy-start | bytes 1769476
  126.7 10.8 %copy-start.78 = (bf16[9,256]{1,0:T(8,128)(2,1)S(1)}, bf16[9,256]{1,0:T(8,128)(2,1)}, u32[]{:S(2)}) copy-start(bf16[9,256]{1,0:T(8,128)(2,1)} %param.30) | copy-start | bytes 13828
  127.0 10.5 %copy-start.19 = (bf16[1152,256]{1,0:T(8,128)(2,1)}, bf16[1152,256]{1,0:T(8,128)(2,1)S(1)}, u32[]{:S(2)}) copy-start(bf16[1152,256]{1,0:T(8,128)(2,1)S(1)} %reshape.487) | copy-start | bytes 1769476
  127.0 46.3 %copy-start.69 = (f32[256]{0:T(256)}, f32[256]{0:T(256)S(1)}, u32[]{:S(2)}) copy-start(f32[256]{0:T(256)S(1)} %convert_element_type.198) | copy-start | bytes 3076
  127.0 46.2 %copy-start.82 = (f32[128]{0:T(128)}, f32[128]{0:T(128)S(1)}, u32[]{:S(2)}) copy-start(f32[128]{0:T(128)S(1)} %multiply_exponential_fusion) | copy-start | bytes 1540
  127.4 73.3 %copy-start.49 = (f32[256]{0:T(256)}, f32[256]{0:T(256)S(1)}, u32[]{:S(2)}) copy-start(f32[256]{0:T(256)S(1)} %fusion.81) | copy-start | bytes 3076
  127.9 9.6 %copy-start.16 = (f32[256,256]{0,1:T(8,128)}, f32[256,256]{0,1:T(8,128)S(1)}, u32[]{:S(2)}) copy-start(f32[256,256]{0,1:T(8,128)S(1)} %get-tuple-element.117) | copy-start | bytes 786436
  128.4 46.2 %copy-start.56 = (f32[256]{0:T(256)}, f32[256]{0:T(256)S(1)}, u32[]{:S(2)}) copy-start(f32[256]{0:T(256)S(1)} %fusion.83) | copy-start | bytes 3076
  128.4 46.2 %copy-start.71 = (f32[256]{0:T(256)}, f32[256]{0:T(256)S(1)}, u32[]{:S(2)}) copy-start(f32[256]{0:T(256)S(1)} %subtract_convert_fusion.1) | copy-start | bytes 3076
  129.1 45.5 %copy-start.39 = (bf16[256,128]{0,1:T(8,128)(2,1)}, bf16[256,128]{0,1:T(8,128)(2,1)S(1)}, u32[]{:S(2)}) copy-start(bf16[256,128]{0,1:T(8,128)(2,1)S(1)} %get-tuple-element.109) | copy-start | bytes 196612
  129.1 74.8 %copy-start.25 = (f32[256,128]{0,1:T(8,128)}, f32[256,128]{0,1:T(8,128)S(1)}, u32[]{:S(2)}) copy-start(f32[256,128]{0,1:T(8,128)S(1)} %get-tuple-element.110) | copy-start | bytes 393220
  129.1 74.8 %copy-start.27 = (f32[256,128]{0,1:T(8,128)}, f32[256,128]{0,1:T(8,128)S(1)}, u32[]{:S(2)}) copy-start(f32[256,128]{0,1:T(8,128)S(1)} %get-tuple-element.111) | copy-start | bytes 393220
  129.1 75.1 %copy-start.37 = (bf16[256,128]{0,1:T(8,128)(2,1)}, bf16[256,128]{0,1:T(8,128)(2,1)S(1)}, u32[]{:S(2)}) copy-start(bf16[256,128]{0,1:T(8,128)(2,1)S(1)} %get-tuple-element.108) | copy-start | bytes 196612
  129.1 51.1 %copy-start.42 = (bf16[9,6912]{1,0:T(8,128)(2,1)S(1)}, bf16[9,6912]{1,0:T(8,128)(2,1)}, u32[]{:S(2)}) copy-start(bf16[9,6912]{1,0:T(8,128)(2,1)} %param.37) | copy-start | bytes 373252
  129.8 74.3 %collective-permute-start.2 = (bf16[256,256]{0,1:T(8,128)(2,1)}, bf16[256,256]{0,1:T(8,128)(2,1)}, u32[]{:S(2)}, u32[]{:S(2)}) collective-permute-start(bf16[256,256]{0,1:T(8,128)(2,1)} %pad_maximum_fusion.3), channel_id=1, source_target_pairs={{0,16},{8,24},{16,32},{24,40},{32,48},{40,56},{48,64},{56,72},{64,... | collective-permute-start | bytes 393224 | tf_op jit(solution)/shard_map/ppermute | solution.py:21
  133.9 70.2 %collective-permute-start.3 = (bf16[256,256]{0,1:T(8,128)(2,1)}, bf16[256,256]{0,1:T(8,128)(2,1)}, u32[]{:S(2)}, u32[]{:S(2)}) collective-permute-start(bf16[256,256]{0,1:T(8,128)(2,1)} %pad_maximum_fusion.3), channel_id=1, source_target_pairs={{0,8},{8,16},{16,24},{24,32},{32,40},{40,48},{48,56},{56,64},{64,7... | collective-permute-start | bytes 393224 | tf_op jit(solution)/shard_map/ppermute | solution.py:21
  173.5 20.1 %copy-start.14 = (bf16[1152,256]{1,0:T(8,128)(2,1)}, bf16[1152,256]{1,0:T(8,128)(2,1)S(1)}, u32[]{:S(2)}) copy-start(bf16[1152,256]{1,0:T(8,128)(2,1)S(1)} %reshape.485) | copy-start | bytes 1769476
  174.6 32.1 %collective-permute-start = (bf16[256,256]{1,0:T(8,128)(2,1)}, bf16[256,256]{1,0:T(8,128)(2,1)}, u32[]{:S(2)}, u32[]{:S(2)}) collective-permute-start(bf16[256,256]{1,0:T(8,128)(2,1)} %convolution_convert_fusion.4), channel_id=1, source_target_pairs={{0,16},{8,24},{16,32},{24,40},{32,48},{40,56},{48,64},{56,72},{64,... | collective-permute-start | bytes 393224 | tf_op jit(solution)/shard_map/ppermute | solution.py:21
  178.3 28.4 %collective-permute-start.1 = (bf16[256,256]{1,0:T(8,128)(2,1)}, bf16[256,256]{1,0:T(8,128)(2,1)}, u32[]{:S(2)}, u32[]{:S(2)}) collective-permute-start(bf16[256,256]{1,0:T(8,128)(2,1)} %convolution_convert_fusion.4), channel_id=1, source_target_pairs={{0,8},{8,16},{16,24},{24,32},{32,40},{40,48},{48,56},{56,64},{64,7... | collective-permute-start | bytes 393224 | tf_op jit(solution)/shard_map/ppermute | solution.py:21
  182.3 10.2 %all-to-all-start.1 = ((bf16[8,2,3888]{2,1,0:T(2,128)(2,1)}), bf16[8,2,3888]{2,1,0:T(2,128)(2,1)S(1)}, u32[]{:S(2)}, u32[]{:S(2)}) async-start(bf16[8,2,3888]{2,1,0:T(2,128)(2,1)} %reshape.508), calls=%async_computation.1 | async-start | bytes 253952 | tf_op jit(solution)/shard_map/all_to_all | solution.py:197
  187.1 121.5 %all-gather.18.cloned.1.call-start = ((), (), s32[]{:S(2)}) async-start(), calls=%async_computation.9 | async-start | bytes 5013504 | tf_op jit(solution)/shard_map/all_gather | solution.py:201
  188.1 15.2 %copy-start.65 = (f32[256]{0:T(256)}, f32[256]{0:T(256)S(1)}, u32[]{:S(2)}) copy-start(f32[256]{0:T(256)S(1)} %convert_element_type.203) | copy-start | bytes 3076
  193.5 151.6 %all-gather.14.cloned.1.call-start = ((), (), s32[]{:S(2)}) async-start(), calls=%async_computation.7 | async-start | bytes 5308416 | tf_op jit(solution)/shard_map/all_gather | solution.py:207
  214.2 213.7 %reduce-scatter.7.cloned.1.call-start = ((), (), s32[]{:S(2)}) async-start(), calls=%async_computation.10 | async-start | bytes 10616832 | tf_op jit(solution)/shard_map/reduce_scatter | solution.py:211
  345.1 7.6 copy-start.22
  345.1 7.6 copy-start.85
  352.7 8.6 %copy-start.92 = (f32[2048,864]{0,1:T(8,128)}, f32[2048,864]{0,1:T(8,128)S(1)}, u32[]{:S(2)}) copy-start(f32[2048,864]{0,1:T(8,128)S(1)} %fusion.111) | copy-start | bytes 21233668
  352.7 10.5 %copy-start.24 = (bf16[864,1152]{1,0:T(8,128)(2,1)S(1)}, bf16[864,1152]{1,0:T(8,128)(2,1)}, u32[]{:S(2)}) copy-start(bf16[864,1152]{1,0:T(8,128)(2,1)} %reshape.491) | copy-start | bytes 5971972
  371.3 58.1 %copy-start.10 = (bf16[1,256,1152]{2,1,0:T(8,128)(2,1)S(1)}, bf16[1,256,1152]{2,1,0:T(8,128)(2,1)}, u32[]{:S(2)}) copy-start(bf16[1,256,1152]{2,1,0:T(8,128)(2,1)} %param.26) | copy-start | bytes 1769476
  371.3 97.8 %all-gather.20.cloned.1.call-start = ((), (), s32[]{:S(2)}) async-start(), calls=%async_computation.11 | async-start | bytes 5308416 | tf_op jit(solution)/shard_map/all_gather | solution.py:228
  434.1 120.9 %reduce-scatter.9.cloned.1.call-start = ((), (), s32[]{:S(2)}) async-start(), calls=%async_computation.12 | async-start | bytes 10616832 | tf_op jit(solution)/shard_map/reduce_scatter | solution.py:238
  469.1 14.8 %copy-start.21 = (bf16[1152,864]{1,0:T(8,128)(2,1)S(1)}, bf16[1152,864]{1,0:T(8,128)(2,1)}, u32[]{:S(2)}) copy-start(bf16[1152,864]{1,0:T(8,128)(2,1)} %reshape.499) | copy-start | bytes 5971972
  498.4 183.1 %all-reduce.33.cloned.1.call-start = ((), (), s32[]{:S(2)}) async-start(), calls=%async_computation.16 | async-start | bytes 8257536
  524.5 328.0 %all-reduce.31.cloned.1.call-start = ((), (), s32[]{:S(2)}) async-start(), calls=%async_computation.15 | async-start | bytes 23592960
  563.2 6.8 copy-start.34
  564.0 33.9 %collective-permute-start.6 = (bf16[256,256]{1,0:T(8,128)(2,1)}, bf16[256,256]{1,0:T(8,128)(2,1)}, u32[]{:S(2)}, u32[]{:S(2)}) collective-permute-start(bf16[256,256]{1,0:T(8,128)(2,1)} %get-tuple-element.102), channel_id=1, source_target_pairs={{8,0},{16,8},{24,16},{32,24},{40,32},{48,40},{56,48},{64,56},{72,6... | collective-permute-start | bytes 393224 | tf_op jit(solution)/shard_map/ppermute | solution.py:21
  565.3 32.6 %collective-permute-start.7 = (bf16[256,256]{1,0:T(8,128)(2,1)}, bf16[256,256]{1,0:T(8,128)(2,1)}, u32[]{:S(2)}, u32[]{:S(2)}) collective-permute-start(bf16[256,256]{1,0:T(8,128)(2,1)} %get-tuple-element.103), channel_id=1, source_target_pairs={{16,0},{24,8},{32,16},{40,24},{48,32},{56,40},{64,48},{72,56},{80,... | collective-permute-start | bytes 393224 | tf_op jit(solution)/shard_map/ppermute | solution.py:21
  570.1 10.8 %copy-start.38 = (bf16[256,128]{0,1:T(8,128)(2,1)S(1)}, bf16[256,128]{0,1:T(8,128)(2,1)}, u32[]{:S(2)}) copy-start(bf16[256,128]{0,1:T(8,128)(2,1)} %copy-done.37) | copy-start | bytes 196612
  570.1 10.8 %copy-start.41 = (bf16[256,128]{0,1:T(8,128)(2,1)S(1)}, bf16[256,128]{0,1:T(8,128)(2,1)}, u32[]{:S(2)}) copy-start(bf16[256,128]{0,1:T(8,128)(2,1)} %copy-done.39) | copy-start | bytes 196612
  578.0 17.8 %collective-permute-start.4 = (bf16[256,256]{0,1:T(8,128)(2,1)}, bf16[256,256]{0,1:T(8,128)(2,1)}, u32[]{:S(2)}, u32[]{:S(2)}) collective-permute-start(bf16[256,256]{0,1:T(8,128)(2,1)} %get-tuple-element.104), channel_id=1, source_target_pairs={{8,0},{16,8},{24,16},{32,24},{40,32},{48,40},{56,48},{64,56},{72,6... | collective-permute-start | bytes 393224 | tf_op jit(solution)/shard_map/ppermute | solution.py:21
  579.3 8.1 copy-start.26
  579.3 8.1 copy-start.28
  579.3 16.5 %collective-permute-start.5 = (bf16[256,256]{0,1:T(8,128)(2,1)}, bf16[256,256]{0,1:T(8,128)(2,1)}, u32[]{:S(2)}, u32[]{:S(2)}) collective-permute-start(bf16[256,256]{0,1:T(8,128)(2,1)} %get-tuple-element.105), channel_id=1, source_target_pairs={{16,0},{24,8},{32,16},{40,24},{48,32},{56,40},{64,48},{72,56},{80,... | collective-permute-start | bytes 393224 | tf_op jit(solution)/shard_map/ppermute | solution.py:21
  602.0 76.5 %copy-start.81 = (u32[128]{0:T(128)S(1)}, u32[128]{0:T(128)}, u32[]{:S(2)}) copy-start(u32[128]{0:T(128)} %constant.213) | copy-start | bytes 1540
  669.5 10.9 %collective-permute-start.8 = (bf16[64,1152]{1,0:T(8,128)(2,1)S(1)}, bf16[64,1152]{1,0:T(8,128)(2,1)S(1)}, u32[]{:S(2)}, u32[]{:S(2)}) collective-permute-start(bf16[64,1152]{1,0:T(8,128)(2,1)S(1)} %fusion), channel_id=1, source_target_pairs={{0,8},{8,16},{16,24},{24,32},{32,40},{40,48},{48,56},{56,64},{64,7... | collective-permute-start | bytes 442376
  672.0 8.5 collective-permute-start.9
  676.1 4.4 collective-permute-start.10
  684.3 14.7 %all-to-all-start.2 = ((bf16[8,2,3888]{2,1,0:T(2,128)(2,1)}), bf16[8,2,3888]{2,1,0:T(2,128)(2,1)S(1)}, u32[]{:S(2)}, u32[]{:S(2)}) async-start(bf16[8,2,3888]{2,1,0:T(2,128)(2,1)} %reshape.512), calls=%async_computation.4 | async-start | bytes 253952 | tf_op jit(solution)/shard_map/all_to_all | solution.py:348
  699.0 10.7 %all-to-all-start.3 = ((bf16[8,2,3888]{2,1,0:T(2,128)(2,1)}), bf16[8,2,3888]{2,1,0:T(2,128)(2,1)}, u32[]{:S(2)}, u32[]{:S(2)}) async-start(bf16[8,2,3888]{2,1,0:T(2,128)(2,1)} %reshape.514), calls=%async_computation.5 | async-start | bytes 253952 | tf_op jit(solution)/shard_map/all_to_all | solution.py:351
  705.3 10.7 %copy-start.2 = (bf16[1152,1024]{1,0:T(8,128)(2,1)S(1)}, bf16[1152,1024]{1,0:T(8,128)(2,1)}, u32[]{:S(2)}) copy-start(bf16[1152,1024]{1,0:T(8,128)(2,1)} %copy-done.1) | copy-start | bytes 7077892
  718.2 74.4 %copy-start.74 = (f32[256]{0:T(256)S(1)}, f32[256]{0:T(256)}, u32[]{:S(2)}) copy-start(f32[256]{0:T(256)} %copy-done.73) | copy-start | bytes 3076
  718.2 74.4 %copy-start.6 = (f32[256,1152]{1,0:T(8,128)S(1)}, f32[256,1152]{1,0:T(8,128)}, u32[]{:S(2)}) copy-start(f32[256,1152]{1,0:T(8,128)} %copy-done.5) | copy-start | bytes 3538948
  (57 other events, 145.6 us)
Sparse Core Ops, SparseCore 0:
  11.2 70.5 all-gather.21
  84.8 64.8 all-gather.11
  152.0 44.4 all-gather.23
  199.0 53.2 all-gather.15
  254.9 53.6 all-gather.17
  310.7 34.3 all-gather.13
  371.4 56.3 reduce-scatter.6
  434.2 34.8 all-gather.19
  498.5 56.3 reduce-scatter.8
  558.3 119.2 all-reduce.32
  684.1 168.3 all-reduce.30
where the time goes:
time: 873 us; the launch traced here: 864 us
  waiting for transfers between devices  302 us (35%)
  blocking collectives  275 us (32%)
  matrix products  121 us (14%)
  local copies, waits for them, and re-layouts  74.1 us (8%)
  starting transfers between devices  47.9 us (5%)
  other arithmetic  27.2 us (3%)
  between operations  16.8 us (2%)
    unnamed x3, blocking collectives  193 us
    unnamed x16, waiting for transfers between devices  60.9 us
    reduce_scatter x1, waiting for transfers between devices, local(): lax.psum_scatter(jnp.dot(active, full_down, preferred_element_type=jnp.fl...  55 us
    all_gather x1, waiting for transfers between devices, local(): lax.all_gather(column_parts[1], 'seq', axis=0, tiled=True)  48.3 us
    unnamed x229, local copies, waits for them, and re-layouts  38.3 us
    all_gather x1, blocking collectives, gather_attention(): lax.all_gather(value_weight, ('seq', 'shard'), axis=0, tiled=True)  35.7 us
    all_gather x1, waiting for transfers between devices, local(): down_all = lax.all_gather(down_low, 'shard', axis=0, tiled=True)  35 us
    all_gather x1, waiting for transfers between devices, local(): lax.all_gather(column_parts[0], 'seq', axis=0, tiled=True)  34.8 us
  transfers between devices with their start and end apart: 25, of which 10 were waited for; matrix products, arithmetic and copies ran while one was open for 24% of the time, Pallas kernels for 0%

commit v1 on v0

v1 whole, which is shorter than its diff:
```python
import functools
import math

import jax
import jax.numpy as jnp
from jax import lax
from jax.experimental import pallas as pl
from jax.experimental.pallas import tpu as pltpu
from jax.sharding import PartitionSpec as P

D = 1152
HEADS = 4
HEAD_DIM = 256
WINDOW = 512
FF = 6912
PIECE = 54
SLOT = 56
WIDE = 16 * SLOT

EPSILON = 1e-06
NEGATIVE = -1e30
MESH = pl.DeviceIdType.MESH
MIB = 2**20


def place():
    q, s = lax.axis_index("seq"), lax.axis_index("shard")
    return q // 4, s // 2, q % 4, s % 2


def device(x, y, z, c):
    return {"seq": x % 4 * 4 + z % 4, "shard": y % 4 * 2 + c}


def greet(targets):
    barrier = pltpu.get_barrier_semaphore()
    for target in targets:
        pl.semaphore_signal(barrier, inc=1, device_id=target, device_id_type=MESH)
    pl.semaphore_wait(barrier, len(targets))


class Sems:
    def __init__(self, send, recv):
        self.send, self.recv, self.used = send, recv, 0

    def take(self):
        self.used += 1
        return self.send.at[self.used - 1], self.recv.at[self.used - 1]


class Push:
    def __init__(self, src, dst, sems, to, lands=None):
        send, recv = sems.take()
        self.out = pltpu.make_async_remote_copy(
            src_ref=src, dst_ref=dst, send_sem=send, recv_sem=recv, device_id=to, device_id_type=MESH
        )
        lands = dst if lands is None else lands
        self.back = pltpu.make_async_remote_copy(
            src_ref=lands, dst_ref=lands, send_sem=send, recv_sem=recv, device_id=to, device_id_type=MESH
        )

    def start(self):
        self.out.start()

    def arrived(self):
        self.back.wait_recv()

    def sent(self):
        self.out.wait_send()


class RingGather:
    def __init__(self, own, slot, half, me, peer, sems):
        up, down, far = (me + 1) % 4, (me + 3) % 4, (me + 2) % 4
        self.right = Push(own, slot(me), sems, peer(up), slot(down))
        self.left = Push(own, slot(me), sems, peer(down), slot(up))
        self.right2 = Push(half(down, 0), half(down, 0), sems, peer(up), half(far, 0))
        split = half(up, 1)
        self.left2 = None if split is None else Push(split, split, sems, peer(down), half(far, 1))

    def first(self):
        self.right.start()
        self.left.start()

    def relay(self):
        self.right.arrived()
        self.right2.start()
        self.left.arrived()
        if self.left2 is not None:
            self.left2.start()

    def last(self):
        self.right2.arrived()
        if self.left2 is not None:
            self.left2.arrived()

    def close(self):
        for push in (self.right, self.left, self.right2, self.left2):
            if push is not None:
                push.sent()


class RingSum:
    def __init__(self, chunk, half, inbox, me, peer, sems, add):
        up, down, far = (me + 1) % 4, (me + 3) % 4, (me + 2) % 4
        self.chunk, self.half, self.inbox, self.add = chunk, half, inbox, add
        self.me, self.up, self.down = me, up, down
        near_a, near_b, right, left = inbox
        self.far_a = Push(half(far, 0), near_a, sems, peer(up))
        split = half(far, 1)
        self.far_b = None if split is None else Push(split, near_b, sems, peer(down))
        self.right = Push(chunk(up), right, sems, peer(up))
        self.left = Push(chunk(down), left, sems, peer(down))

    def first(self):
        self.far_a.start()
        if self.far_b is not None:
            self.far_b.start()

    def second(self):
        self.far_a.arrived()
        self.add(self.half(self.up, 0), self.inbox[0])
        self.right.start()
        if self.far_b is not None:
            self.far_b.arrived()
            self.add(self.half(self.down, 1), self.inbox[1])
        self.left.start()

    def third(self):
        self.right.arrived()
        self.add(self.chunk(self.me), self.inbox[2])
        self.left.arrived()
        self.add(self.chunk(self.me), self.inbox[3])

    def close(self):
        for push in (self.far_a, self.far_b, self.right, self.left):
            if push is not None:
                push.sent()


def add_into(total, extra):
    if len(total.shape) == 2:
        summed = total[...].astype(jnp.float32) + extra[...].astype(jnp.float32)
        total[...] = summed.astype(total.dtype)
        return

    @pl.loop(0, total.shape[0])
    def _(step):
        add_into(total.at[step], extra.at[step])


ANY = pl.BlockSpec(memory_space=pl.ANY)
VMEM = pl.BlockSpec(memory_space=pltpu.VMEM)


def call(kernel, name, number, outs, ins, scratch, copies, in_specs=None, out_specs=None, local=0):
    outs = [jax.ShapeDtypeStruct(shape, dtype) for shape, dtype in outs]
    scratch = list(scratch) + [pltpu.SemaphoreType.DMA((copies,)), pltpu.SemaphoreType.DMA((copies,))]
    if local:
        scratch.append(pltpu.SemaphoreType.DMA((local,)))
    return pl.pallas_call(
        kernel,
        name=name,
        out_shape=outs,
        in_specs=in_specs or [ANY] * len(ins),
        out_specs=out_specs or [ANY] * len(outs),
        scratch_shapes=scratch,
        compiler_params=pltpu.CompilerParams(
            collective_id=number, has_side_effects=True, vmem_limit_bytes=56 * MIB
        ),
    )(*ins)


SHARD_STEPS = [(dy, dc) for dy in range(4) for dc in range(2) if dy or dc]


def exchange_shard(name, number, shared, spread):
    n_shared, n = len(shared), len(shared) + len(spread)

    def kernel(*refs):
        ins, outs, (send, recv, here) = refs[:n], refs[n : 2 * n], refs[2 * n :]
        x, y, z, c = place()
        mine = y * 2 + c
        sems = Sems(send, recv)
        greet([device(x, y + dy, z, (c + dc) % 2) for dy, dc in SHARD_STEPS])
        pushes = []
        for dy, dc in SHARD_STEPS:
            to_y, to_c = (y + dy) % 4, (c + dc) % 2
            from_y, from_c = (y + 4 - dy) % 4, (c + 2 - dc) % 2
            for at in range(n):
                src = ins[at] if at < n_shared else ins[at].at[to_y * 2 + to_c]
                push = Push(
                    src, outs[at].at[mine], sems, device(x, to_y, z, to_c), outs[at].at[from_y * 2 + from_c]
                )
                push.start()
                pushes.append(push)
        own = []
        for at in range(n):
            src = ins[at] if at < n_shared else ins[at].at[mine]
            own.append(pltpu.make_async_copy(src, outs[at].at[mine], here.at[at]))
            own[-1].start()
        for copy in own:
            copy.wait()
        for push in pushes:
            push.arrived()
            push.sent()

    outs = [((8,) + a.shape, a.dtype) for a in shared] + [(a.shape, a.dtype) for a in spread]
    return call(kernel, name, number, outs, list(shared) + list(spread), [], 7 * n, local=n)


def lane_halves(width):
    low = width // 256 * 128 if width % 256 == 0 else (width // 128 + 1) // 2 * 128
    return ((0, low), (low, width - low)) if width > 128 else ((0, width), None)


def gather_seq(name, number, z_first, x_first, shared):
    ins = list(z_first) + list(x_first) + list(shared)
    n = len(ins)
    copies = 8 * n + 4 * len(shared)

    def kernel(*refs):
        sources, outs, (send, recv, here) = refs[:n], refs[n : 2 * n], refs[2 * n :]
        x, y, z, c = place()
        sems = Sems(send, recv)
        greet(
            [device(x, y, z + 1, c), device(x, y, z + 3, c), device(x + 1, y, z, c), device(x + 3, y, z, c)]
            + ([device(x, y, z, 1 - c)] if shared else [])
        )

        def z_peer(k):
            return device(x, y, k, c)

        def x_peer(k):
            return device(k, y, z, c)

        jobs, own = [], []
        for at in range(n):
            source, out = sources[at], outs[at]
            rows, width = source.shape
            is_shared, by_rows = at >= len(z_first) + len(x_first), rows % 32 == 0
            part = lambda ref: ref
            if is_shared and by_rows:
                share = pl.ds(pl.multiple_of(c * (rows // 2), 16), rows // 2)
                part = lambda ref, share=share: ref.at[(slice(None),) * (len(ref.shape) - 2) + (share,)]
            elif is_shared:
                width //= 2
                share = pl.ds(pl.multiple_of(c * width, 128), width)
                part = lambda ref, share=share: ref.at[(slice(None),) * (len(ref.shape) - 1) + (share,)]
            halves = lane_halves(width)

            def lanes(ref, h, halves=halves, part=part):
                return None if halves[h] is None else part(ref).at[:, pl.ds(*halves[h])]

            mine = part(source)
            own.append(pltpu.make_async_copy(mine, part(out.at[x, z]), here.at[at]))
            own[-1].start()
            if at < len(z_first):
                one = RingGather(
                    mine,
                    lambda k, out=out, part=part: part(out.at[x, k]),
                    lambda k, h, out=out, lanes=lanes: lanes(out.at[x, k], h),
                    z, z_peer, sems,
                )
                two = RingGather(
                    part(out.at[x]),
                    lambda k, out=out, part=part: part(out.at[k]),
                    lambda k, h, out=out, part=part: part(out.at[k, pl.ds(2 * h, 2)]),
                    x, x_peer, sems,
                )
                piece = lambda k, out=out, part=part: part(out.at[k])
                me = x
            else:
                one = RingGather(
                    mine,
                    lambda k, out=out, part=part: part(out.at[k, z]),
                    lambda k, h, out=out, lanes=lanes: lanes(out.at[k, z], h),
                    x, x_peer, sems,
                )
                two = RingGather(
                    part(out.at[:, z]),
                    lambda k, out=out, part=part: part(out.at[:, k]),
                    lambda k, h, out=out, part=part: part(out.at[pl.ds(2 * h, 2), k]),
                    z, z_peer, sems,
                )
                piece = lambda k, out=out, part=part: part(out.at[:, k])
                me = z
            crossings = []
            if is_shared:
                half = rows // 2 if by_rows else width
                theirs = pl.ds(pl.multiple_of((1 - c) * half, 16 if by_rows else 128), half)
                for k in (me, (me + 3) % 4, (me + 1) % 4, (me + 2) % 4):
                    lands = out.at[:, k, theirs] if by_rows else out.at[:, k, :, theirs]
                    crossings.append(Push(piece(k), piece(k), sems, device(x, y, z, 1 - c), lands))
            jobs.append((one, two, crossings))
        for one, _, _ in jobs:
            one.first()
        for one, _, _ in jobs:
            one.relay()
        for copy in own:
            copy.wait()
        for one, two, crossings in jobs:
            one.last()
            two.first()
            if crossings:
                crossings[0].start()
        for _, two, crossings in jobs:
            two.relay()
            if crossings:
                crossings[1].start()
                crossings[2].start()
        for one, two, crossings in jobs:
            two.last()
            if crossings:
                crossings[3].start()
        for one, two, crossings in jobs:
            for push in crossings:
                push.arrived()
                push.sent()
            one.close()
            two.close()

    outs = [((4, 4) + a.shape, a.dtype) for a in ins]
    return call(kernel, name, number, outs, ins, [], copies, local=n)


def halo(name, number, steps, value):
    def kernel(src, out, send, recv):
        q, s = lax.axis_index("seq"), lax.axis_index("shard")
        sems = Sems(send, recv)
        there = [{"seq": (q + 16 + d) % 16, "shard": s} for d in steps]
        back = [{"seq": (q + 16 - d) % 16, "shard": s} for d in steps]
        greet(there + back)
        pushes = []
        for at in range(len(steps)):
            piece = src if len(src.shape) == 2 else src.at[at]
            pushes.append(Push(piece, out.at[at], sems, there[at]))
            pushes[-1].start()
        for push in pushes:
            push.arrived()
            push.sent()

    shape = (len(steps),) + value.shape[-2:]
    return call(kernel, name, number, [(shape, value.dtype)], [value], [], len(steps))[0]


def gather_tokens(name, number, value):
    rows, width = value.shape

    def kernel(src, out, send, recv, here):
        x, y, z, c = place()
        sems = Sems(send, recv)
        other = device(x, y, z, 1 - c)
        greet([device(x, y + 1, z, c), device(x, y + 3, z, c), other])
        slot = lambda k: out.at[k * 2 + c]
        ring = RingGather(
            src, slot, lambda k, h: out.at[k * 2 + c, pl.ds(h * (rows // 2), rows // 2)],
            y, lambda k: device(x, k, z, c), sems,
        )
        there = lambda k: out.at[k * 2 + 1 - c]
        cross = [
            Push(src if i == 0 else slot((y + i) % 4), slot((y + i) % 4), sems, other, there((y + i) % 4))
            for i in range(4)
        ]
        ring.first()
        cross[0].start()
        own = pltpu.make_async_copy(src, slot(y), here.at[0])
        own.start()
        ring.relay()
        cross[3].start()
        cross[1].start()
        ring.last()
        cross[2].start()
        own.wait()
        for push in cross:
            push.arrived()
            push.sent()
        ring.close()

    return call(kernel, name, number, [((8, rows, width), value.dtype)], [value], [], 8, local=1)[0]


def sum_tokens(name, number, value):
    _, rows, width = value.shape
    half = rows // 2

    def kernel(src, out, chunks, inbox, near_a, near_b, right, left, send, recv, here):
        x, y, z, c = place()
        sems = Sems(send, recv)
        other = device(x, y, z, 1 - c)
        greet([device(x, y + 1, z, c), device(x, y + 3, z, c), other])
        order = [(y + 2) % 4, (y + 1) % 4, (y + 3) % 4, y]
        cross = [Push(src.at[k * 2 + 1 - c], inbox.at[i], sems, other) for i, k in enumerate(order)]
        for push in cross:
            push.start()
        loads = [pltpu.make_async_copy(src.at[k * 2 + c], chunks.at[i], here.at[i]) for i, k in enumerate(order)]
        for load in loads:
            load.start()
        at = {2: 0, 1: 1, 3: 2, 0: 3}
        to = lambda d: device(x, y + d, z, c)
        far_a = Push(chunks.at[0, pl.ds(0, half)], near_a, sems, to(1))
        far_b = Push(chunks.at[0, pl.ds(half, half)], near_b, sems, to(3))
        go_right = Push(chunks.at[1], right, sems, to(1))
        go_left = Push(chunks.at[2], left, sems, to(3))
        for i in range(4):
            loads[i].wait()
            cross[i].arrived()
            if i < 3:
                add_into(chunks.at[i], inbox.at[i])
            if i == 0:
                far_a.start()
                far_b.start()
        far_a.arrived()
        add_into(chunks.at[1, pl.ds(0, half)], near_a)
        go_right.start()
        far_b.arrived()
        add_into(chunks.at[2, pl.ds(half, half)], near_b)
        go_left.start()
        out[...] = chunks[3].astype(jnp.float32) + inbox[3].astype(jnp.float32)
        go_right.arrived()
        out[...] += right[...].astype(jnp.float32)
        go_left.arrived()
        out[...] += left[...].astype(jnp.float32)
        for push in cross + [far_a, far_b, go_right, go_left]:
            push.sent()

    kind = value.dtype
    scratch = [
        pltpu.VMEM((4, rows, width), kind),
        pltpu.VMEM((4, rows, width), kind),
        pltpu.VMEM((half, width), kind),
        pltpu.VMEM((half, width), kind),
        pltpu.VMEM((rows, width), kind),
        pltpu.VMEM((rows, width), kind),
    ]
    return call(
        kernel, name, number, [((rows, width), jnp.float32)], [value], scratch, 8, out_specs=[VMEM], local=4
    )[0]


def sum_seq(name, number, z_first, x_first, shared):
    ins = list(z_first) + list(x_first) + [a for a, _, _ in shared]
    n, plain = len(ins), len(z_first) + len(x_first)
    shapes = [a.shape for a in z_first + x_first] + [a.shape[:3] + (size,) for a, _, size in shared]
    kinds = [a.dtype for a in ins]
    copies = 8 * n + len(shared)

    def boxes(shape, kind, first_axis):
        rows, width = shape[2:]
        lanes = lane_halves(width)
        out = [pltpu.VMEM((2, rows, width), kind)] * 2 + [pltpu.VMEM((4, rows, width), kind)] * 2
        out += [pltpu.VMEM((rows, lanes[0][1]), kind)]
        out += [pltpu.VMEM((rows, (lanes[1] or lanes[0])[1]), kind)]
        out += [pltpu.VMEM((rows, width), kind)] * 2
        return out

    scratch = []
    for at in range(n):
        scratch.append(pltpu.VMEM(shapes[at], kinds[at]))
        scratch += boxes(shapes[at], kinds[at], 0)
    for at in range(plain, n):
        scratch.append(pltpu.VMEM(shapes[at], kinds[at]))

    def kernel(*refs):
        sources, outs = refs[:n], refs[n : 2 * n]
        room = refs[2 * n : 2 * n + 9 * n]
        extra = refs[11 * n : 11 * n + len(shared)]
        send, recv, here = refs[11 * n + len(shared) :]
        x, y, z, c = place()
        sems = Sems(send, recv)
        greet(
            [device(x, y, z + 1, c), device(x, y, z + 3, c), device(x + 1, y, z, c), device(x + 3, y, z, c)]
            + ([device(x, y, z, 1 - c)] if shared else [])
        )
        z_peer = lambda k: device(x, y, k, c)
        x_peer = lambda k: device(k, y, z, c)
        loads, cross, jobs = [], [], []
        for at in range(n):
            total = room[9 * at]
            source = sources[at]
            if at >= plain:
                _, step, size = shared[at - plain]
                theirs = source.at[:, :, :, pl.ds(pl.multiple_of((1 - c) * step, 128), size)]
                cross.append(Push(theirs, extra[at - plain], sems, device(x, y, z, 1 - c)))
                cross[-1].start()
                source = source.at[:, :, :, pl.ds(pl.multiple_of(c * step, 128), size)]
            loads.append(pltpu.make_async_copy(source, total, here.at[at]))
            loads[-1].start()
            halves = lane_halves(shapes[at][3])

            def lanes(ref, h, halves=halves):
                return None if halves[h] is None else ref.at[:, pl.ds(*halves[h])]

            inbox1, inbox2 = room[9 * at + 1 : 9 * at + 5], room[9 * at + 5 : 9 * at + 9]
            if at < len(z_first):
                one = RingSum(
                    lambda k, t=total: t.at[:, k],
                    lambda k, h, t=total: t.at[pl.ds(2 * h, 2), k],
                    inbox1, z, z_peer, sems, add_into,
                )
                two = RingSum(
                    lambda k, t=total: t.at[k, z],
                    lambda k, h, t=total, lanes=lanes: lanes(t.at[k, z], h),
                    inbox2, x, x_peer, sems, add_into,
                )
            else:
                one = RingSum(
                    lambda k, t=total: t.at[k],
                    lambda k, h, t=total: t.at[k, pl.ds(2 * h, 2)],
                    inbox1, x, x_peer, sems, add_into,
                )
                two = RingSum(
                    lambda k, t=total: t.at[x, k],
                    lambda k, h, t=total, lanes=lanes: lanes(t.at[x, k], h),
                    inbox2, z, z_peer, sems, add_into,
                )
            jobs.append((one, two))
        for at in range(n):
            loads[at].wait()
            if at >= plain:
                cross[at - plain].arrived()
                add_into(room[9 * at], extra[at - plain])
            jobs[at][0].first()
        for one, _ in jobs:
            one.second()
        for one, two in jobs:
            one.third()
            two.first()
        for _, two in jobs:
            two.second()
        for at, (one, two) in enumerate(jobs):
            two.third()
            outs[at][...] = room[9 * at][x, z].astype(outs[at].dtype)
        for one, two in jobs:
            one.close()
            two.close()
        for push in cross:
            push.sent()

    outs = [(shape[2:], kind) for shape, kind in zip(shapes, kinds)]
    return call(kernel, name, number, outs, ins, scratch, copies, out_specs=[VMEM] * n, local=n)


def norm_rows(values, weight):
    return values * lax.rsqrt(jnp.mean(values * values, axis=-1, keepdims=True) + EPSILON) * weight


def rotate(values, angles):
    middle = values.shape[-1] // 2
    leading = values[..., :middle]
    trailing = values[..., middle:]
    cosine = jnp.cos(angles)
    sine_part = jnp.sin(angles)
    return jnp.concatenate(
        [leading * cosine - trailing * sine_part, trailing * cosine + leading * sine_part], axis=-1
    )


def head_prep(values, weight, angles):
    return rotate(norm_rows(values, weight), angles)


def geglu(gate_part, up_part):
    return jax.nn.gelu(gate_part, approximate=True) * up_part


def frequencies(width):
    return jnp.exp(jnp.arange(width // 2, dtype=jnp.float32) * (-2.0 * math.log(10000.0) / width))


def matmul(a, b):
    return jnp.dot(a, b, preferred_element_type=jnp.float32)


def matmul_tn(a, b):
    return lax.dot_general(a, b, (((0,), (0,)), ((), ())), preferred_element_type=jnp.float32)


def matmul_nt(a, b):
    return lax.dot_general(a, b, (((1,), (1,)), ((), ())), preferred_element_type=jnp.float32)


def heads_first(values):
    return jnp.concatenate([values[:, h * HEAD_DIM : (h + 1) * HEAD_DIM] for h in range(HEADS)], axis=0)


def heads_last(values):
    rows = values.shape[0] // HEADS
    return jnp.concatenate([values[h * rows : (h + 1) * rows] for h in range(HEADS)], axis=1)


def pad_rows(values, rows):
    return jnp.pad(values, ((0, rows - values.shape[0]), (0, 128 - values.shape[1])))


def split_hidden(weight):
    parts = weight.reshape(9, 16, 8, PIECE).transpose(2, 0, 1, 3)
    return jnp.pad(parts, ((0, 0), (0, 0), (0, 0), (0, SLOT - PIECE))).reshape(8, 9, WIDE)


def local(
    stream, doc_starts, cotangent, attention_norm, query_weight, key_weight, value_weight, query_norm, key_norm,
    output_weight, attention_post_norm, mlp_norm, gate_weight, up_weight, down_weight, mlp_post_norm,
):
    tokens = stream.shape[1]
    scale = HEAD_DIM ** (-0.5)
    inputs = stream[0].astype(jnp.float32)
    upstream = cotangent[0].astype(jnp.float32)
    offset = lax.axis_index("seq") * tokens
    positions = offset + jnp.arange(tokens, dtype=jnp.int32)
    starts_row = doc_starts[0]
    beginning = jnp.max(
        jnp.where(starts_row[None, :] <= positions[:, None], starts_row[None, :], 0), axis=1
    )
    angles = (positions - beginning).astype(jnp.float32)[:, None] * frequencies(HEAD_DIM)[None, :]
    angles_q = jnp.concatenate([angles] * HEADS, axis=0)

    own_qkv = jnp.concatenate([query_weight, key_weight, value_weight], axis=1)
    own_gains = jnp.stack(
        [jnp.pad(g, (0, 9 - g.shape[0])) for g in (attention_norm, attention_post_norm, mlp_norm, mlp_post_norm, query_norm, key_norm)]
    )
    own_both = jnp.concatenate([split_hidden(gate_weight), split_hidden(up_weight)], axis=2)
    qkv8, out8, gains8, both8 = exchange_shard(
        "exchange_weights", 0, [own_qkv, output_weight, pad_rows(own_gains, 16)], [own_both]
    )
    gains_row = gains8[:, :6, :9].transpose(1, 0, 2).reshape(6, 72)
    both16, gains16, down16, qkv16, out16 = gather_seq(
        "gather_weights", 1, [both8.reshape(72, 2 * WIDE), pad_rows(gains_row, 16)], [down_weight],
        [qkv8.reshape(72, 1536), out8.reshape(64, D)],
    )
    full_both = both16.reshape(D, 2 * WIDE)
    full_gate, full_up = full_both[:, :WIDE], full_both[:, WIDE:]
    full_down = jnp.pad(down16.reshape(16, PIECE, D), ((0, 0), (0, SLOT - PIECE), (0, 0))).reshape(WIDE, D)
    full_qkv = qkv16.reshape(D, 1536)
    full_output = out16.reshape(HEADS * HEAD_DIM, D)
    gains = gains16.reshape(16, 16, 128).astype(jnp.float32)
    gain_input, gain_post, gain_mlp, gain_mlp_post = (gains[:, i, :72].reshape(D) for i in range(4))
    gain_query, gain_key = (gains[:, i, :72].reshape(16, 8, 9)[:, :, :2].reshape(HEAD_DIM) for i in (4, 5))

    normed = norm_rows(inputs, gain_input).astype(jnp.bfloat16)
    projected = matmul(normed, full_qkv)
    query_proj = heads_first(projected[:, :1024])
    key_proj = projected[:, 1024:1280]
    values_low = projected[:, 1280:].astype(jnp.bfloat16)
    query_rot = head_prep(query_proj, gain_query, angles_q).astype(jnp.bfloat16)
    key_rot = head_prep(key_proj, gain_key, angles).astype(jnp.bfloat16)
    own_kv = jnp.concatenate([key_rot, values_low], axis=1)
    far_kv = halo("halo", 2, (2, 1), own_kv)
    kv = jnp.concatenate([far_kv.reshape(2 * tokens, 2 * HEAD_DIM), own_kv], axis=0)
    keys_all, values_all = kv[:, :HEAD_DIM], kv[:, HEAD_DIM:]
    key_place = offset - WINDOW + jnp.arange(tokens + WINDOW, dtype=jnp.int32)
    allowed = (
        (key_place[None, :] <= positions[:, None])
        & (key_place[None, :] > positions[:, None] - WINDOW)
        & (key_place[None, :] >= beginning[:, None])
    )
    allowed = jnp.concatenate([allowed] * HEADS, axis=0)
    scores = jnp.where(allowed, matmul_nt(query_rot, keys_all) * scale, NEGATIVE)
    highest = jnp.max(scores, axis=-1, keepdims=True)
    exponent = jnp.exp(scores - highest)
    totals = jnp.sum(exponent, axis=-1, keepdims=True)
    probability = exponent / totals
    probability_low = probability.astype(jnp.bfloat16)
    mixed = heads_last(matmul(probability_low, values_all).astype(jnp.bfloat16))
    branch = matmul(mixed, full_output)
    hidden = inputs + norm_rows(branch, gain_post)
    feed = norm_rows(hidden, gain_mlp).astype(jnp.bfloat16)

    feed_all = gather_tokens("gather_feed", 3, feed).reshape(8 * tokens, D)
    gate_out = matmul(feed_all, full_gate)
    up_out = matmul(feed_all, full_up)
    active = geglu(gate_out, up_out).astype(jnp.bfloat16)
    down_part = matmul(active, full_down).astype(jnp.bfloat16)
    down_out = sum_tokens("sum_down", 4, down_part.reshape(8, tokens, D))
    result = hidden + norm_rows(down_out, gain_mlp_post)
    down_grad, gain_mlp_post_grad = jax.vjp(norm_rows, down_out, gain_mlp_post)[1](upstream)
    down_all = gather_tokens("gather_down", 5, down_grad.astype(jnp.bfloat16)).reshape(8 * tokens, D)
    active_grad = matmul_nt(down_all, full_down)
    down_term = matmul_tn(active, down_all).astype(jnp.bfloat16)
    gate_grad, up_grad = jax.vjp(geglu, gate_out, up_out)[1](active_grad)
    both_low = jnp.concatenate([gate_grad.astype(jnp.bfloat16), up_grad.astype(jnp.bfloat16)], axis=1)
    both_term = matmul_tn(feed_all, both_low).astype(jnp.bfloat16)
    feed_part = matmul_nt(both_low, full_both).astype(jnp.bfloat16)
    feed_grad = sum_tokens("sum_feed", 6, feed_part.reshape(8, tokens, D))

    hidden_extra, gain_mlp_grad = jax.vjp(norm_rows, hidden, gain_mlp)[1](feed_grad)
    hidden_grad = upstream + hidden_extra
    branch_grad, gain_post_grad = jax.vjp(norm_rows, branch, gain_post)[1](hidden_grad)
    branch_low = branch_grad.astype(jnp.bfloat16)
    output_term = matmul_tn(mixed, branch_low).astype(jnp.bfloat16)
    mixed_grad = heads_first(matmul_nt(branch_low, full_output).astype(jnp.bfloat16))
    prob_grad = matmul_nt(mixed_grad, values_all)
    inner_sum = jnp.sum(probability * prob_grad, axis=-1, keepdims=True)
    score_low = (probability * (prob_grad - inner_sum) * scale).astype(jnp.bfloat16)
    query_grad_rot = matmul(score_low, keys_all)
    key_grads = matmul_tn(score_low, query_rot)
    value_grads = matmul_tn(probability_low, mixed_grad)
    kv_grads = jnp.concatenate([key_grads, value_grads], axis=1)
    returned = halo(
        "halo_back", 7, (-2, -1), kv_grads[:WINDOW].astype(jnp.bfloat16).reshape(2, tokens, 2 * HEAD_DIM)
    )
    kv_own = kv_grads[WINDOW:] + returned[0].astype(jnp.float32) + returned[1].astype(jnp.float32)
    query_grad, gain_query_grad = jax.vjp(lambda v, w: head_prep(v, w, angles_q), query_proj, gain_query)[1](
        query_grad_rot
    )
    key_grad, gain_key_grad = jax.vjp(lambda v, w: head_prep(v, w, angles), key_proj, gain_key)[1](
        kv_own[:, :HEAD_DIM]
    )
    qkv_low = jnp.concatenate([heads_last(query_grad), key_grad, kv_own[:, HEAD_DIM:]], axis=1).astype(jnp.bfloat16)
    qkv_term = matmul_tn(normed, qkv_low).astype(jnp.bfloat16)
    normed_grad = matmul_nt(qkv_low, full_qkv)
    input_extra, gain_input_grad = jax.vjp(norm_rows, inputs, gain_input)[1](normed_grad)
    stream_grad = (hidden_grad + input_extra).astype(jnp.bfloat16)

    squares = jnp.stack([jnp.sum(inputs * inputs), jnp.sum(hidden * hidden), jnp.sum(result * result)])
    small = [g.reshape(16, 72) for g in (gain_input_grad, gain_post_grad, gain_mlp_grad, gain_mlp_post_grad)]
    small += [jnp.pad(g.reshape(16, 16), ((0, 0), (0, 56))) for g in (gain_query_grad, gain_key_grad)]
    small.append(jnp.pad(jnp.broadcast_to(squares[None], (16, 3)), ((0, 0), (0, 69))))
    small = jnp.pad(jnp.stack(small, axis=1), ((0, 0), (0, 1), (0, 56))).reshape(4, 4, 8, 128)
    down_blocks = down_term.reshape(16, SLOT, D)[:, :PIECE].reshape(4, 4, PIECE, D)
    both_sum, small_sum, down_sum, qkv_sum, output_sum = sum_seq(
        "sum_weights", 8, [both_term.reshape(4, 4, 72, 2 * WIDE), small], [down_blocks],
        [(qkv_term.reshape(4, 4, 72, 1536), 768, 768), (output_term.reshape(4, 4, 64, D), 512, 640)],
    )
    small_all, both_rows, qkv_rows, output_rows = exchange_shard(
        "exchange_grads", 9, [small_sum],
        [both_sum.reshape(8, 9, 2 * WIDE), qkv_sum.reshape(8, 9, 768), output_sum.reshape(8, 8, 640)],
    )

    def whole(rows):
        parts = rows.reshape(8, 9, 16, SLOT)[..., :PIECE]
        return parts.transpose(1, 2, 0, 3).reshape(9, FF).astype(jnp.float32)

    qkv_grad = jnp.sum(qkv_rows.reshape(4, 2, 9, 768).astype(jnp.float32), axis=0)
    qkv_grad = jnp.concatenate([qkv_grad[0], qkv_grad[1]], axis=1)
    output_grad = jnp.sum(output_rows.reshape(4, 2, 8, 640).astype(jnp.float32), axis=0)
    output_grad = jnp.concatenate([output_grad[0][:, :512], output_grad[1]], axis=1)
    small_sum = jnp.sum(small_all, axis=0)
    shard = lax.axis_index("shard")
    gain_grads = lax.dynamic_slice_in_dim(small_sum, shard * 9, 9, 1)
    head_grads = lax.dynamic_slice_in_dim(small_sum, shard * 2, 2, 1)
    stream_rms = jnp.sqrt(small_sum[6, :3] / (32768 * D))
    return (
        result.astype(jnp.bfloat16)[None],
        stream_grad[None],
        gain_grads[0],
        qkv_grad[:, :1024],
        qkv_grad[:, 1024:1280],
        qkv_grad[:, 1280:],
        head_grads[4],
        head_grads[5],
        output_grad,
        gain_grads[1],
        gain_grads[2],
        whole(both_rows[:, :, :WIDE]),
        whole(both_rows[:, :, WIDE:]),
        down_sum.astype(jnp.float32),
        gain_grads[3],
        stream_rms,
    )


def solution(mesh):
    rows = P(("seq", "shard"))
    tokens = P("shard", "seq", None)
    table = P(("seq", "shard"), None)
    return jax.shard_map(
        local,
        mesh=mesh,
        in_specs=(
            tokens, P("shard", None), tokens, rows, table, table, table, rows, rows, table, rows, rows, table, table,
            table, rows,
        ),
        out_specs=(
            tokens, tokens, rows, table, table, table, rows, rows, table, rows, rows, table, table, table, rows, P(),
        ),
        check_vma=False,
    )
```

time: 873 us -> 478 us (0.55)
  Pallas kernels: 0 us -> 305 us
  waiting for transfers between devices: 302 us -> 0 us
  blocking collectives: 275 us -> 0 us
  starting transfers between devices: 47.9 us -> 0 us
  local copies, waits for them, and re-layouts: 74.1 us -> 34.2 us
  matrix products: 121 us -> 87.3 us
  other arithmetic: 27.2 us -> 43 us
  between operations: 16.8 us -> 2.29 us
    pallas_call x0 -> x10, Pallas kernels: none -> 305 us  [call(): pl.pallas_call(kernel, name=name, out_shape=outs, in_specs=in_specs or [A...]
    unnamed x3 -> x0, blocking collectives: 193 us -> none
    all_gather x7 -> x0, waiting for transfers between devices: 147 us -> none  [the longest x1 48.3 us: local(): lax.all_gather(column_parts[1], 'seq', axis=0, tiled=True)]
    reduce_scatter x2 -> x0, waiting for transfers between devices: 85.5 us -> none  [the longest x1 55 us: local(): lax.psum_scatter(jnp.dot(active, full_down, preferred_element_type=jnp.fl...]
    all_gather x2 -> x0, blocking collectives: 70.4 us -> none  [the longest x1 35.7 us: gather_attention(): lax.all_gather(value_weight, ('seq', 'shard'), axis=0, tiled=True)]
    unnamed x16 -> x0, waiting for transfers between devices: 60.9 us -> none
    dot_general x27 -> x19, matrix products: 121 us -> 87.3 us  [the longest x7 29.9 us: matmul(): return jnp.dot(a, b, preferred_element_type=jnp.float32)]
    unnamed x229 -> x148, local copies, waits for them, and re-layouts: 38.3 us -> 7.78 us
  transfers between devices with their start and end apart: 25 -> 0, of which waited for: 10 -> 0; matrix products, arithmetic and copies ran while one was open for 24% -> 0% of each run, Pallas kernels for 0% -> 0%
where the time goes in v1:
time: 478 us; the launch traced here: 472 us
  Pallas kernels  305 us (64%)
  matrix products  87.3 us (18%)
  other arithmetic  43 us (9%)
  local copies, waits for them, and re-layouts  34.2 us (7%)
    pallas_call x10, Pallas kernels, call(): pl.pallas_call(kernel, name=name, out_shape=outs, in_specs=in_specs or [A...  305 us
    dot_general x7, matrix products, matmul(): return jnp.dot(a, b, preferred_element_type=jnp.float32)  29.9 us
    dot_general x6, matrix products, matmul_nt(): lax.dot_general(a, b, (((1,), (1,)), ((), ())), preferred_element_type=jn...  29.3 us
    dot_general x6, matrix products, matmul_tn(): lax.dot_general(a, b, (((0,), (0,)), ((), ())), preferred_element_type=jn...  28.1 us

profile of v1, /device:TPU:1, one launch (start us, length us, event | category | flops | bytes accessed | tf_op | source)
XLA Modules:
  0.0 472.3 jit_solution(15791045863821139062)
XLA Ops:
  1.4 0.7 stack.51
  2.7 1.7 reshape.322
  4.8 1.7 reshape.324
  7.0 0.8 pad_maximum_fusion.9.refs_3_
  8.5 18.2 %exchange_weights.1 = (bf16[8,9,1536]{2,1,0:T(8,128)(2,1)}, bf16[8,8,1152]{2,1,0:T(8,128)(2,1)}, bf16[8,16,128]{2,1,0:T(8,128)(2,1)}, bf16[8,9,1792]{2,1,0:T(8,128)(2,1)}) custom-call(bf16[9,1536]{1,0:T(8,128)(2,1)} %pad_maximum_fusion.18.refs_0_, bf16[8,1152]{1,0:T(8,128)(2,1)} %refs_1_.1, bf16[16,128]{1,0:T(8,128)(2,1)} %pad.55.refs_2_, ...), custom_call_target="tpu_custom_call" | custom-call | tf_op jit(solution)/shard_map/exchange_weights/pallas_call | solution.py:161
  26.7 1.8 reshape.326.refs_0_
  28.5 1.8 reshape.328.refs_3_
  31.7 69.4 %gather_weights.1 = (bf16[4,4,72,1792]{3,2,1,0:T(8,128)(2,1)}, bf16[4,4,16,128]{3,2,1,0:T(8,128)(2,1)}, bf16[4,4,54,1152]{3,2,1,0:T(8,128)(2,1)}, bf16[4,4,72,15...) custom-call(bf16[72,1792]{1,0:T(8,128)(2,1)} %reshape.326.refs_0_, bf16[16,128]{1,0:T(8,128)(2,1)} %pad.58.refs_1_, ...), custom_call_target="tpu_custom_call" | custom-call | tf_op jit(solution)/shard_map/gather_weights/pallas_call | solution.py:161
  101.1 0.9 bitcast_convert_fusion
  102.4 3.2 fusion.42
  105.7 1.2 copy-done.13
  107.2 1.4 fusion.83
  110.1 3.5 subtract_convert_fusion
  113.6 1.1 slice.367
  115.4 17.4 %halo.1 = bf16[2,256,512]{2,1,0:T(8,128)(2,1)} custom-call(bf16[256,512]{1,0:T(8,128)(2,1)} %pad_maximum_fusion.12.src), custom_call_target="tpu_custom_call" | custom-call | tf_op jit(solution)/shard_map/halo/pallas_call | solution.py:161
  132.8 1.1 maximum_maximum_fusion
  135.4 0.8 convolution_convert_fusion.7
  136.7 1.1 copy-done.63
  137.8 1.0 multiply_reduce_fusion.7
  140.0 1.0 multiply_convert_fusion.3.src
  141.0 26.3 %gather_feed.1 = bf16[8,256,1152]{2,1,0:T(8,128)(2,1)} custom-call(bf16[256,1152]{1,0:T(8,128)(2,1)} %multiply_convert_fusion.3.src), custom_call_target="tpu_custom_call" | custom-call | tf_op jit(solution)/shard_map/gather_feed/pallas_call | solution.py:161
  167.3 7.2 %fusion.11 = f32[2048,896]{0,1:T(8,128)S(1)} fusion(bf16[2048,1152]{1,0:T(8,128)(2,1)} %bitcast.178, bf16[1152,1792]{1,0:T(8,128)(2,1)S(1)} %bitcast.211), kind=kOutput, calls=%fused_computation.27 | convolution fusion | flops 4227858432 | bytes 14123008 | tf_op jit(solution)/shard_map/dot_general | solution.py:572
  174.5 9.6 %multiply_convert_fusion.1 = (bf16[2048,896]{0,1:T(8,128)(2,1)}, f32[2048,896]{0,1:T(8,128)}) fusion(f32[2048,896]{0,1:T(8,128)S(1)} %fusion.11, bf16[2048,1152]{1,0:T(8,128)(2,1)S(1)} %bitcast.180, bf16[1152,1792]{1,0:T(8,128)(2,1)S(1)} %bitcast.212), kind=kOutput, calls=%fused_computation.15 | convolution fusion | flops 4246208512 | bytes 25133056 | tf_op jit(solution)/shard_map/dot_general | solution.py:572
  184.3 2.6 copy-done.66
  186.9 7.5 %convolution_convert_fusion = bf16[2048,1152]{1,0:T(8,128)(2,1)} fusion(bf16[2048,896]{0,1:T(8,128)(2,1)S(1)} %copy-done.66, bf16[896,1152]{1,0:T(8,128)(2,1)S(1)} %bitcast.190), kind=kOutput, calls=%fused_computation.2 | convolution fusion | flops 4230217728 | bytes 10452992 | tf_op jit(solution)/shard_map/dot_general | solution.py:572
  194.4 28.2 %sum_down.1 = f32[256,1152]{1,0:T(8,128)} custom-call(bf16[8,256,1152]{2,1,0:T(8,128)(2,1)} %bitcast.177), custom_call_target="tpu_custom_call" | custom-call | tf_op jit(solution)/shard_map/sum_down/pallas_call | solution.py:161
  222.6 1.5 multiply_reduce_fusion.6
  224.8 3.8 fusion.34
  228.6 1.1 fusion.30.src
  229.7 27.6 %gather_down.1 = bf16[8,256,1152]{2,1,0:T(8,128)(2,1)} custom-call(bf16[256,1152]{1,0:T(8,128)(2,1)} %fusion.30.src), custom_call_target="tpu_custom_call" | custom-call | tf_op jit(solution)/shard_map/gather_down/pallas_call | solution.py:161
  257.4 13.6 %fusion.6 = (bf16[2048,896]{0,1:T(8,128)(2,1)S(1)}, bf16[2048,896]{0,1:T(8,128)(2,1)S(1)}) fusion(f32[2048,896]{0,1:T(8,128)} %copy-done.65, f32[2048,896]{0,1:T(8,128)} %get-tuple-element.120, bf16[2048,1152]{1,0:T(8,128)(2,1)} %bitcast.181, bf16[896,1152]{1,0:T(8,128)(2,1)S(1)} %bitcast.191), kind=kOutput, calls=%fused_computation.12 | convolution fusion | flops 4271898624 | bytes 28803072 | tf_op jit(solution)/shard_map/dot_general | solution.py:580
  271.0 11.6 %convolution_convert_fusion.2 = bf16[2048,1152]{1,0:T(8,128)(2,1)} fusion(bf16[1152,1792]{1,0:T(8,128)(2,1)S(1)} %bitcast.213, bf16[2048,896]{0,1:T(8,128)(2,1)S(1)} %get-tuple-element.75, bf16[2048,896]{0,1:T(8,128)(2,1)S(1)} %get-tuple-element.74), kind=kOutput, calls=%fused_computation.4 | convolution fusion | flops 8472756224 | bytes 16187392 | tf_op jit(solution)/shard_map/dot_general | solution.py:580
  282.6 26.2 %sum_feed.1 = f32[256,1152]{1,0:T(8,128)} custom-call(bf16[8,256,1152]{2,1,0:T(8,128)(2,1)} %bitcast.176), custom_call_target="tpu_custom_call" | custom-call | tf_op jit(solution)/shard_map/sum_feed/pallas_call | solution.py:161
  308.9 2.2 multiply_reduce_fusion.2
  311.2 1.3 multiply_reduce_fusion.3
  312.9 2.3 convolution_convert_fusion.4
  315.2 0.9 convolution_convert_fusion.6
  316.1 1.0 copy-done.3
  318.2 0.8 multiply_reduce_fusion
  319.0 0.9 multiply_convert_fusion.2
  320.6 0.8 fusion.36
  321.5 13.0 %halo_back.1 = bf16[2,256,512]{2,1,0:T(8,128)(2,1)} custom-call(bf16[2,256,512]{2,1,0:T(8,128)(2,1)} %bitcast.188), custom_call_target="tpu_custom_call" | custom-call | tf_op jit(solution)/shard_map/halo_back/pallas_call | solution.py:161
  334.5 1.1 fusion.51
  336.2 1.7 multiply_reduce_fusion.13
  338.6 2.3 multiply_add_fusion.2
  341.9 1.3 fusion.63
  343.3 3.1 convolution_convert_fusion.1
  346.4 6.5 %convolution_convert_fusion.5 = bf16[896,1152]{1,0:T(8,128)(2,1)} fusion(bf16[2048,896]{0,1:T(8,128)(2,1)S(1)} %copy-done.67, bf16[2048,1152]{1,0:T(8,128)(2,1)S(1)} %bitcast.184), kind=kOutput, calls=%fused_computation.18 | convolution fusion | flops 4228890624 | bytes 10452992 | tf_op jit(solution)/shard_map/dot_general | solution.py:576
  352.9 1.9 fusion.25
  354.7 2.0 select_maximum_fusion
  358.1 15.1 %convolution_convert_fusion.3 = bf16[1152,1792]{1,0:T(8,128)(2,1)} fusion(bf16[2048,1152]{1,0:T(8,128)(2,1)} %bitcast.179, bf16[2048,896]{0,1:T(8,128)(2,1)} %copy-done.69, bf16[2048,896]{0,1:T(8,128)(2,1)} %copy-done.68), kind=kOutput, calls=%fused_computation.5 | convolution fusion | flops 8472461312 | bytes 16187392 | tf_op jit(solution)/shard_map/dot_general | solution.py:576
  373.1 62.2 %sum_weights.1 = (bf16[72,1792]{1,0:T(8,128)(2,1)}, f32[8,128]{1,0:T(8,128)}, bf16[54,1152]{1,0:T(8,128)(2,1)}, bf16[72,768]{1,0:T(8,128)(2,1)}, bf16[64,640]{1,0:T(8,128)(2,1)}) custom-call(bf16[4,4,72,1792]{3,2,1,0:T(8,128)(2,1)} %bitcast.185, f32[4,4,8,128]{3,2,1,0:T(8,128)} %bitcast.195, bf16[4,4,54,1152]{3,2,1,0:T(8,128)(2,1)} %bitcast.192, ...), custom_call_target="tpu_custom_call" | custom-call | tf_op jit(solution)/shard_map/sum_weights/pallas_call | solution.py:161
  435.4 1.8 reshape.349.refs_1_
  437.2 1.6 reshape.350.refs_2_
  438.8 17.0 %exchange_grads.1 = (f32[8,8,128]{2,1,0:T(8,128)}, bf16[8,9,1792]{2,1,0:T(8,128)(2,1)}, bf16[8,9,768]{2,1,0:T(8,128)(2,1)}, bf16[8,8,640]{2,1,0:T(8,128)(2,1)}) custom-call(f32[8,128]{1,0:T(8,128)} %get-tuple-element.43.refs_0_, bf16[8,9,1792]{2,1,0:T(8,128)(2,1)} %reshape.349.refs_1_, bf16[8,9,768]{2,1,0:T(8,128)(2,1)} %reshape.350.refs_2_, ...), custom_call_target="tpu_custom_call" | custom-call | tf_op jit(solution)/shard_map/exchange_grads/pallas_call | solution.py:161
  455.8 1.8 fusion.86
  458.4 1.2 reshape.361
  459.5 1.0 copy.82
  461.2 1.2 reshape.362
  462.4 0.9 convert_reduce_fusion.1
  464.0 1.0 convert_reduce_fusion
  466.2 0.8 reduce_sum.267
  468.7 1.6 convert_element_type.202
  471.0 1.2 fusion.40
  (236 shorter events, 22.2 us)
Async XLA Ops:
  0.6 7.2 %copy-start.35 = (bf16[9,1024]{1,0:T(8,128)(2,1)S(1)}, bf16[9,1024]{1,0:T(8,128)(2,1)}, u32[]{:S(2)}) copy-start(bf16[9,1024]{1,0:T(8,128)(2,1)} %param.20) | copy-start | bytes 55300
  0.7 7.2 %copy-start.53 = (bf16[9,256]{1,0:T(8,128)(2,1)S(1)}, bf16[9,256]{1,0:T(8,128)(2,1)}, u32[]{:S(2)}) copy-start(bf16[9,256]{1,0:T(8,128)(2,1)} %param.21) | copy-start | bytes 13828
  0.7 7.2 %copy-start.52 = (bf16[9,256]{1,0:T(8,128)(2,1)S(1)}, bf16[9,256]{1,0:T(8,128)(2,1)}, u32[]{:S(2)}) copy-start(bf16[9,256]{1,0:T(8,128)(2,1)} %param.22) | copy-start | bytes 13828
  4.8 97.3 %copy-start.1 = (bf16[1,256,1152]{2,1,0:T(8,128)(2,1)S(1)}, bf16[1,256,1152]{2,1,0:T(8,128)(2,1)}, u32[]{:S(2)}) copy-start(bf16[1,256,1152]{2,1,0:T(8,128)(2,1)} %param.16) | copy-start | bytes 1769476
  102.4 4.7 copy-start.46
  102.4 3.3 copy-start.38
  106.8 2.5 copy-start.59
  107.0 3.1 copy-start.48
  107.0 1.7 copy-start.36
  108.6 6.8 %copy-start.7 = (f32[256,256]{1,0:T(8,128)}, f32[256,256]{1,0:T(8,128)S(1)}, u32[]{:S(2)}) copy-start(f32[256,256]{1,0:T(8,128)S(1)} %get-tuple-element.80) | copy-start | bytes 786436
  108.6 6.8 %copy-start.9 = (f32[256,256]{1,0:T(8,128)}, f32[256,256]{1,0:T(8,128)S(1)}, u32[]{:S(2)}) copy-start(f32[256,256]{1,0:T(8,128)S(1)} %get-tuple-element.81) | copy-start | bytes 786436
  109.4 24.5 %copy-start.43 = (f32[256]{0:T(256)}, f32[256]{0:T(256)S(1)}, u32[]{:S(2)}) copy-start(f32[256]{0:T(256)S(1)} %get-tuple-element.126) | copy-start | bytes 3076
  109.5 25.4 %copy-start.57 = (f32[128]{0:T(128)}, f32[128]{0:T(128)S(1)}, u32[]{:S(2)}) copy-start(f32[128]{0:T(128)S(1)} %multiply_exponential_fusion) | copy-start | bytes 1540
  110.1 3.5 copy-start.17
  113.6 21.3 %copy-start.21 = (bf16[1024,128]{1,0:T(8,128)(2,1)}, bf16[1024,128]{1,0:T(8,128)(2,1)S(1)}, u32[]{:S(2)}) copy-start(bf16[1024,128]{1,0:T(8,128)(2,1)S(1)} %get-tuple-element.84) | copy-start | bytes 786436
  113.6 20.6 %copy-start.23 = (bf16[1024,128]{1,0:T(8,128)(2,1)S(1)}, bf16[1024,128]{1,0:T(8,128)(2,1)}, u32[]{:S(2)}) copy-start(bf16[1024,128]{1,0:T(8,128)(2,1)} %get-tuple-element.85) | copy-start | bytes 786436
  133.9 1.5 copy-start.19
  134.9 1.7 copy-start.2
  135.4 2.4 copy-start.63
  136.7 2.1 copy-start.25
  136.7 2.1 copy-start.27
  136.7 2.1 copy-start.29
  136.7 2.1 copy-start.31
  138.8 28.5 %copy-start.4 = (f32[256,1152]{1,0:T(8,128)}, f32[256,1152]{1,0:T(8,128)S(1)}, u32[]{:S(2)}) copy-start(f32[256,1152]{1,0:T(8,128)S(1)} %get-tuple-element.118) | copy-start | bytes 3538948
  140.0 27.3 %copy-start.60 = (bf16[4,4,72,1792]{3,2,1,0:T(8,128)(2,1)S(1)}, bf16[4,4,72,1792]{3,2,1,0:T(8,128)(2,1)}, u32[]{:S(2)}) copy-start(bf16[4,4,72,1792]{3,2,1,0:T(8,128)(2,1)} %get-tuple-element.41) | copy-start | bytes 12386308
  167.3 7.2 %copy-start.12 = (bf16[8,256,1152]{2,1,0:T(8,128)(2,1)S(1)}, bf16[8,256,1152]{2,1,0:T(8,128)(2,1)}, u32[]{:S(2)}) copy-start(bf16[8,256,1152]{2,1,0:T(8,128)(2,1)} %gather_feed.1) | copy-start | bytes 14155780
  174.5 9.6 %copy-start.65 = (f32[2048,896]{0,1:T(8,128)}, f32[2048,896]{0,1:T(8,128)S(1)}, u32[]{:S(2)}) copy-start(f32[2048,896]{0,1:T(8,128)S(1)} %fusion.11) | copy-start | bytes 22020100
  174.5 9.6 %copy-start.14 = (bf16[4,4,54,1152]{3,2,1,0:T(8,128)(2,1)S(1)}, bf16[4,4,54,1152]{3,2,1,0:T(8,128)(2,1)}, u32[]{:S(2)}) copy-start(bf16[4,4,54,1152]{3,2,1,0:T(8,128)(2,1)} %get-tuple-element.42) | copy-start | bytes 5971972
  184.2 2.8 copy-start.66
  184.3 10.1 %copy-start.15 = (bf16[16,56,1152]{2,1,0:T(8,128)(2,1)}, bf16[16,56,1152]{2,1,0:T(8,128)(2,1)S(1)}, u32[]{:S(2)}) copy-start(bf16[16,56,1152]{2,1,0:T(8,128)(2,1)S(1)} %pad.59) | copy-start | bytes 6193156
  222.6 6.0 %copy-start = (f32[256,1152]{1,0:T(8,128)S(1)}, f32[256,1152]{1,0:T(8,128)}, u32[]{:S(2)}) copy-start(f32[256,1152]{1,0:T(8,128)} %sum_down.1) | copy-start | bytes 3538948
  224.8 3.8 copy-start.51
  224.8 3.8 copy-start.11
  224.8 3.8 copy-start.45
  229.7 27.6 %copy-start.16 = (bf16[16,56,1152]{2,1,0:T(8,128)(2,1)S(1)}, bf16[16,56,1152]{2,1,0:T(8,128)(2,1)}, u32[]{:S(2)}) copy-start(bf16[16,56,1152]{2,1,0:T(8,128)(2,1)} %copy-done.15) | copy-start | bytes 6193156
  257.4 13.6 %copy-start.61 = (bf16[4,4,72,1792]{3,2,1,0:T(8,128)(2,1)S(1)}, bf16[4,4,72,1792]{3,2,1,0:T(8,128)(2,1)}, u32[]{:S(2)}) copy-start(bf16[4,4,72,1792]{3,2,1,0:T(8,128)(2,1)} %get-tuple-element.41) | copy-start | bytes 12386308
  271.0 11.6 %copy-start.68 = (bf16[2048,896]{0,1:T(8,128)(2,1)}, bf16[2048,896]{0,1:T(8,128)(2,1)S(1)}, u32[]{:S(2)}) copy-start(bf16[2048,896]{0,1:T(8,128)(2,1)S(1)} %get-tuple-element.74) | copy-start | bytes 11010052
  271.0 11.6 %copy-start.69 = (bf16[2048,896]{0,1:T(8,128)(2,1)}, bf16[2048,896]{0,1:T(8,128)(2,1)S(1)}, u32[]{:S(2)}) copy-start(bf16[2048,896]{0,1:T(8,128)(2,1)S(1)} %get-tuple-element.75) | copy-start | bytes 11010052
  282.6 28.5 %copy-start.42 = (f32[256]{0:T(256)S(1)}, f32[256]{0:T(256)}, u32[]{:S(2)}) copy-start(f32[256]{0:T(256)} %copy-done.41) | copy-start | bytes 3076
  282.6 28.5 %copy-start.5 = (f32[256,1152]{1,0:T(8,128)S(1)}, f32[256,1152]{1,0:T(8,128)}, u32[]{:S(2)}) copy-start(f32[256,1152]{1,0:T(8,128)} %copy-done.4) | copy-start | bytes 3538948
  308.9 2.3 copy-start.6
  311.2 1.7 copy-start.26
  311.2 1.7 copy-start.28
  311.2 1.7 copy-start.30
  311.2 1.7 copy-start.32
  312.5 2.6 copy-start.64
  315.2 1.9 copy-start.3
  320.6 15.0 %copy-start.44 = (f32[256]{0:T(256)S(1)}, f32[256]{0:T(256)}, u32[]{:S(2)}) copy-start(f32[256]{0:T(256)} %copy-done.43) | copy-start | bytes 3076
  320.6 15.0 %copy-start.58 = (f32[128]{0:T(128)S(1)}, f32[128]{0:T(128)}, u32[]{:S(2)}) copy-start(f32[128]{0:T(128)} %copy-done.57) | copy-start | bytes 1540
  320.6 15.6 %copy-start.37 = (f32[256]{0:T(256)S(1)}, f32[256]{0:T(256)}, u32[]{:S(2)}) copy-start(f32[256]{0:T(256)} %copy-done.36) | copy-start | bytes 3076
  320.6 17.4 %copy-start.49 = (f32[256]{0:T(256)S(1)}, f32[256]{0:T(256)}, u32[]{:S(2)}) copy-start(f32[256]{0:T(256)} %copy-done.48) | copy-start | bytes 3076
  334.4 4.1 copy-start.18
  336.2 4.7 %copy-start.8 = (f32[256,256]{1,0:T(8,128)S(1)}, f32[256,256]{1,0:T(8,128)}, u32[]{:S(2)}) copy-start(f32[256,256]{1,0:T(8,128)} %copy-done.7) | copy-start | bytes 786436
  336.2 4.7 %copy-start.10 = (f32[256,256]{1,0:T(8,128)S(1)}, f32[256,256]{1,0:T(8,128)}, u32[]{:S(2)}) copy-start(f32[256,256]{1,0:T(8,128)} %copy-done.9) | copy-start | bytes 786436
  341.0 2.3 copy-start.39
  341.4 4.9 %slice-start = ((s8[4718592]{0:T(1024)(128)(4,1)}), s8[4194304]{0:T(1024)(128)(4,1)S(1)}, s32[]{:S(2)}) async-start(s8[4718592]{0:T(1024)(128)(4,1)} %bitcast.182), calls=%async_computation | async-start | bytes 8388608
  343.2 3.1 slice-start.1
  343.2 3.1 copy-start.67
  346.3 6.5 %copy-start.62 = (bf16[4,4,72,1536]{3,2,1,0:T(8,128)(2,1)S(1)}, bf16[4,4,72,1536]{3,2,1,0:T(8,128)(2,1)}, u32[]{:S(2)}) copy-start(bf16[4,4,72,1536]{3,2,1,0:T(8,128)(2,1)} %get-tuple-element.39) | copy-start | bytes 10616836
  352.9 4.0 copy-start.54
  352.9 4.2 copy-start.34
  352.9 4.3 copy-start.33
  458.3 12.0 %copy-start.47 = (f32[256]{0:T(256)S(1)}, f32[256]{0:T(256)}, u32[]{:S(2)}) copy-start(f32[256]{0:T(256)} %copy-done.46) | copy-start | bytes 3076
  458.3 12.6 %copy-start.40 = (f32[256]{0:T(256)S(1)}, f32[256]{0:T(256)}, u32[]{:S(2)}) copy-start(f32[256]{0:T(256)} %copy-done.38) | copy-start | bytes 3076
  (8 other events, 7.4 us)

commit v2 on v1

--- a/solution.py
+++ b/solution.py
@@ -541,6 +541,315 @@
     return call(kernel, name, number, outs, ins, scratch, copies, out_specs=[VMEM] * n, local=n)
 
 
+def dot(a, b, contract_a, contract_b):
+    return lax.dot_general(a, b, (((contract_a,), (contract_b,)), ((), ())), preferred_element_type=jnp.float32)
+
+
+SUBS = 2
+BACK = (0, 1, 3, 2)
+
+
+def gelu_terms(gate):
+    a, b = math.sqrt(2.0 / math.pi), 0.044715
+    square = gate * gate
+    bend = jnp.tanh(a * gate * (1.0 + b * square))
+    half = 0.5 * (1.0 + bend)
+    slope = half + 0.5 * gate * (1.0 - bend * bend) * a * (1.0 + 3.0 * b * square)
+    return gate * half, slope
+
+
+def feed_forward(name, number, feed, full_both, full_down, hidden, cotangent, gain):
+    tokens, width = feed.shape
+    rows = tokens // SUBS
+    half = rows // 2
+
+    def kernel(
+        feed_in, both_in, down_in, hidden_in, cotangent_in, gain_in,
+        block_out, feed_out, gain_out, square_out, both_out, down_out,
+        feeds, downs, both, active, part, inbox, near, right, left, w_both, w_down, send, recv, here,
+    ):
+        x, y, z, c = place()
+        sems = Sems(send, recv)
+        other = device(x, y, z, 1 - c)
+        to = lambda d: device(x, y + d, z, c)
+        greet([to(1), to(3), other])
+        loads = [
+            pltpu.make_async_copy(both_in, w_both, here.at[0]),
+            pltpu.make_async_copy(down_in, w_down, here.at[1]),
+        ]
+
+        def gather(source, blocks, s):
+            slot = lambda k: blocks.at[s, k * 2 + c]
+            ring = RingGather(
+                source, slot, lambda k, h: blocks.at[s, k * 2 + c, pl.ds(h * half, half)],
+                y, lambda k: device(x, k, z, c), sems,
+            )
+            cross = []
+            for d in range(4):
+                k = (y + d) % 4
+                cross.append(
+                    Push(source if d == 0 else slot(k), slot(k), sems, other, blocks.at[s, k * 2 + 1 - c])
+                )
+
+            def first():
+                ring.first()
+                cross[0].start()
+
+            def relay():
+                ring.relay()
+                cross[1].start()
+                cross[3].start()
+
+            def last():
+                ring.last()
+                cross[2].start()
+
+            def close():
+                ring.close()
+                for push in cross:
+                    push.sent()
+
+            return first, relay, last, [push.arrived for push in cross], close
+
+        class Total:
+            def __init__(self, s):
+                self.s = s
+                self.cross = {}
+                for d in range(4):
+                    k = (y + d) % 4
+                    self.cross[d] = Push(part.at[s, k * 2 + 1 - c], inbox.at[s, d], sems, other)
+                self.own = lambda d: part.at[s, (y + d) % 4 * 2 + c]
+                self.far_a = Push(self.own(2).at[pl.ds(0, half)], near.at[s, 0], sems, to(1))
+                self.far_b = Push(self.own(2).at[pl.ds(half, half)], near.at[s, 1], sems, to(3))
+                self.right = Push(self.own(1), right.at[s], sems, to(1))
+                self.left = Push(self.own(3), left.at[s], sems, to(3))
+
+            def far(self):
+                self.cross[2].arrived()
+                add_into(self.own(2), inbox.at[self.s, 2])
+                self.far_a.start()
+                self.far_b.start()
+
+            def sides(self):
+                for d in (1, 3):
+                    self.cross[d].arrived()
+                    add_into(self.own(d), inbox.at[self.s, d])
+
+            def go(self):
+                self.far_a.arrived()
+                add_into(self.own(1).at[pl.ds(0, half)], near.at[self.s, 0])
+                self.right.start()
+                self.far_b.arrived()
+                add_into(self.own(3).at[pl.ds(half, half)], near.at[self.s, 1])
+                self.left.start()
+
+            def final(self):
+                self.cross[0].arrived()
+                self.right.arrived()
+                self.left.arrived()
+                s = self.s
+                pieces = (self.own(0), inbox.at[s, 0], right.at[s], left.at[s])
+                return functools.reduce(jnp.add, [p[...].astype(jnp.float32) for p in pieces])
+
+            def close(self):
+                for push in list(self.cross.values()) + [self.far_a, self.far_b, self.right, self.left]:
+                    push.sent()
+
+        def steps(body, before, totals):
+            @pl.loop(0, 4 * SUBS)
+            def _(t):
+                for at, hook in before.items():
+                    pl.when(t == at)(hook)
+                s, i = t // 4, t % 4
+                d = i + i // 2 - i // 3 * 2
+                body(s, pl.ds((y + d) % 4 * 2, 2))
+                for at in range(4 * SUBS):
+                    push = totals[at // 4].cross[BACK[at % 4]]
+                    pl.when(t == at)(push.start)
+
+        def flat(value):
+            return value.reshape(2 * rows, value.shape[-1])
+
+        def pair(value):
+            return value.reshape(2, rows, value.shape[-1])
+
+        def forward(s, chip):
+            sums = dot(flat(feeds[s, chip]), w_both[...], 1, 0)
+            both[s, chip] = pair(sums.astype(jnp.bfloat16))
+            bent, _ = gelu_terms(sums[:, :WIDE])
+            low = (bent * sums[:, WIDE:]).astype(jnp.bfloat16)
+            active[s, chip] = pair(low)
+            part[s, chip] = pair(dot(low, w_down[...], 1, 0).astype(jnp.bfloat16))
+
+        def backward(s, chip):
+            grad = dot(flat(downs[s, chip]), w_down[...], 1, 1)
+            sums = flat(both[s, chip]).astype(jnp.float32)
+            bent, slope = gelu_terms(sums[:, :WIDE])
+            gate_grad = (grad * sums[:, WIDE:] * slope).astype(jnp.bfloat16)
+            up_grad = (grad * bent).astype(jnp.bfloat16)
+            both[s, chip, :, :WIDE] = pair(gate_grad)
+            both[s, chip, :, WIDE:] = pair(up_grad)
+            part[s, chip] = pair(dot(flat(both[s, chip]), w_both[...], 1, 1).astype(jnp.bfloat16))
+
+        span = lambda s: pl.ds(s * rows, rows)
+        gain_out[...] = jnp.zeros_like(gain_out)
+        square_out[...] = jnp.zeros_like(square_out)
+
+        def norm_back(total, s):
+            down = total.final()
+            gain_row = gain_in[...]
+            upstream = cotangent_in[span(s), :].astype(jnp.float32)
+            scale = lax.rsqrt(jnp.mean(down * down, axis=-1, keepdims=True) + EPSILON)
+            unit = down * scale
+            result = hidden_in[span(s), :] + unit * gain_row
+            block_out[span(s), :] = result.astype(jnp.bfloat16)
+            square_out[...] += jnp.sum(result * result, axis=0, keepdims=True)
+            gain_out[...] += jnp.sum(upstream * unit, axis=0, keepdims=True)
+            scaled = gain_row * upstream
+            grad = scale * (scaled - unit * jnp.mean(unit * scaled, axis=-1, keepdims=True))
+            downs[s, y * 2 + c] = grad.astype(jnp.bfloat16)
+
+        a, b = 0, 1
+        first_a, relay_a, last_a, met_a, close_a = gather(feed_in.at[span(a)], feeds, a)
+        first_b, relay_b, last_b, met_b, close_b = gather(feed_in.at[span(b)], feeds, b)
+        sum_a, sum_b = Total(a), Total(b)
+        first_a()
+        for load in loads:
+            load.start()
+        own = [pltpu.make_async_copy(feed_in.at[span(s)], feeds.at[s, y * 2 + c], here.at[2 + s]) for s in (a, b)]
+        for copy in own:
+            copy.start()
+        for copy in own + loads:
+            copy.wait()
+
+        def at_1():
+            relay_a()
+            first_b()
+            met_a[1]()
+
+        def at_2():
+            last_a()
+            met_a[3]()
+
+        def at_3():
+            relay_b()
+            met_a[2]()
+
+        def at_4():
+            sum_a.far()
+            met_b[0]()
+
+        def at_5():
+            last_b()
+            sum_a.sides()
+            met_b[1]()
+
+        def at_6():
+            sum_a.go()
+            met_b[3]()
+
+        steps(
+            forward,
+            {0: met_a[0], 1: at_1, 2: at_2, 3: at_3, 4: at_4, 5: at_5, 6: at_6, 7: met_b[2]},
+            (sum_a, sum_b),
+        )
+        sum_b.far()
+        norm_back(sum_a, a)
+        sum_a.close()
+        close_a()
+        first_a, relay_a, last_a, met_a, close_a = gather(downs.at[a, y * 2 + c], downs, a)
+        first_a()
+        sum_b.sides()
+        sum_b.go()
+        old_a, old_b, old_close_b = sum_a, sum_b, close_b
+        first_b, relay_b, last_b, met_b, close_b = gather(downs.at[b, y * 2 + c], downs, b)
+        sum_a, sum_b = Total(a), Total(b)
+
+        def back_1():
+            relay_a()
+            met_a[1]()
+
+        def back_2():
+            last_a()
+            norm_back(old_b, b)
+            old_b.close()
+            old_close_b()
+            first_b()
+            met_a[3]()
+
+        def back_4():
+            sum_a.far()
+            met_b[0]()
+
+        def back_5():
+            relay_b()
+            sum_a.sides()
+            met_b[1]()
+
+        def back_6():
+            last_b()
+            sum_a.go()
+            met_b[3]()
+
+        steps(
+            backward,
+            {0: met_a[0], 1: back_1, 2: back_2, 3: met_a[2], 4: back_4, 5: back_5, 6: back_6, 7: met_b[2]},
+            (sum_a, sum_b),
+        )
+        sum_b.far()
+        sum_b.sides()
+        every = 8 * tokens
+
+        @pl.loop(0, WIDE // 128)
+        def _(i):
+            units = pl.ds(pl.multiple_of(i * 128, 128), 128)
+            lhs = active[:, :, :, units].reshape(every, 128)
+            down_out[units, :] = dot(lhs, downs[...].reshape(every, width), 0, 0).astype(jnp.bfloat16)
+
+        sum_b.go()
+        feed_out[span(a), :] = sum_a.final()
+
+        @pl.loop(0, width // 128)
+        def _(i):
+            lanes = pl.ds(pl.multiple_of(i * 128, 128), 128)
+            lhs = feeds[:, :, :, lanes].reshape(every, 128)
+            both_out[lanes, :] = dot(lhs, both[...].reshape(every, 2 * WIDE), 0, 0).astype(jnp.bfloat16)
+
+        feed_out[span(b), :] = sum_b.final()
+        sum_a.close()
+        sum_b.close()
+        close_a()
+        close_b()
+
+    low, wide = jnp.bfloat16, jnp.float32
+    blocks = (SUBS, 8, rows)
+    scratch = [
+        pltpu.VMEM(blocks + (width,), low),
+        pltpu.VMEM(blocks + (width,), low),
+        pltpu.VMEM(blocks + (2 * WIDE,), low),
+        pltpu.VMEM(blocks + (WIDE,), low),
+        pltpu.VMEM(blocks + (width,), low),
+        pltpu.VMEM((SUBS, 4, rows, width), low),
+        pltpu.VMEM((SUBS, 2, half, width), low),
+        pltpu.VMEM((SUBS, rows, width), low),
+        pltpu.VMEM((SUBS, rows, width), low),
+        pltpu.VMEM((width, 2 * WIDE), low),
+        pltpu.VMEM((WIDE, width), low),
+    ]
+    outs = [
+        ((tokens, width), low),
+        ((tokens, width), wide),
+        ((1, width), wide),
+        ((1, width), wide),
+        ((width, 2 * WIDE), low),
+        ((WIDE, width), low),
+    ]
+    return call(
+        kernel, name, number, outs, [feed, full_both, full_down, hidden, cotangent, gain], scratch, 32 * SUBS,
+        in_specs=[ANY, ANY, ANY, VMEM, VMEM, VMEM], out_specs=[VMEM] * 6, local=2 + SUBS,
+    )
+
+
 def norm_rows(values, weight):
     return values * lax.rsqrt(jnp.mean(values * values, axis=-1, keepdims=True) + EPSILON) * weight
 
@@ -558,10 +867,6 @@
 
 def head_prep(values, weight, angles):
     return rotate(norm_rows(values, weight), angles)
-
-
-def geglu(gate_part, up_part):
-    return jax.nn.gelu(gate_part, approximate=True) * up_part
 
 
 def frequencies(width):
@@ -629,7 +934,6 @@
         [qkv8.reshape(72, 1536), out8.reshape(64, D)],
     )
     full_both = both16.reshape(D, 2 * WIDE)
-    full_gate, full_up = full_both[:, :WIDE], full_both[:, WIDE:]
     full_down = jnp.pad(down16.reshape(16, PIECE, D), ((0, 0), (0, SLOT - PIECE), (0, 0))).reshape(WIDE, D)
     full_qkv = qkv16.reshape(D, 1536)
     full_output = out16.reshape(HEADS * HEAD_DIM, D)
@@ -666,22 +970,9 @@
     hidden = inputs + norm_rows(branch, gain_post)
     feed = norm_rows(hidden, gain_mlp).astype(jnp.bfloat16)
 
-    feed_all = gather_tokens("gather_feed", 3, feed).reshape(8 * tokens, D)
-    gate_out = matmul(feed_all, full_gate)
-    up_out = matmul(feed_all, full_up)
-    active = geglu(gate_out, up_out).astype(jnp.bfloat16)
-    down_part = matmul(active, full_down).astype(jnp.bfloat16)
-    down_out = sum_tokens("sum_down", 4, down_part.reshape(8, tokens, D))
-    result = hidden + norm_rows(down_out, gain_mlp_post)
-    down_grad, gain_mlp_post_grad = jax.vjp(norm_rows, down_out, gain_mlp_post)[1](upstream)
-    down_all = gather_tokens("gather_down", 5, down_grad.astype(jnp.bfloat16)).reshape(8 * tokens, D)
-    active_grad = matmul_nt(down_all, full_down)
-    down_term = matmul_tn(active, down_all).astype(jnp.bfloat16)
-    gate_grad, up_grad = jax.vjp(geglu, gate_out, up_out)[1](active_grad)
-    both_low = jnp.concatenate([gate_grad.astype(jnp.bfloat16), up_grad.astype(jnp.bfloat16)], axis=1)
-    both_term = matmul_tn(feed_all, both_low).astype(jnp.bfloat16)
-    feed_part = matmul_nt(both_low, full_both).astype(jnp.bfloat16)
-    feed_grad = sum_tokens("sum_feed", 6, feed_part.reshape(8, tokens, D))
+    block_output, feed_grad, gain_mlp_post_grad, result_squares, both_term, down_term = feed_forward(
+        "feed_forward", 3, feed, full_both, full_down, hidden, cotangent[0], gain_mlp_post[None]
+    )
 
     hidden_extra, gain_mlp_grad = jax.vjp(norm_rows, hidden, gain_mlp)[1](feed_grad)
     hidden_grad = upstream + hidden_extra
@@ -697,7 +988,7 @@
     value_grads = matmul_tn(probability_low, mixed_grad)
     kv_grads = jnp.concatenate([key_grads, value_grads], axis=1)
     returned = halo(
-        "halo_back", 7, (-2, -1), kv_grads[:WINDOW].astype(jnp.bfloat16).reshape(2, tokens, 2 * HEAD_DIM)
+        "halo_back", 4, (-2, -1), kv_grads[:WINDOW].astype(jnp.bfloat16).reshape(2, tokens, 2 * HEAD_DIM)
     )
     kv_own = kv_grads[WINDOW:] + returned[0].astype(jnp.float32) + returned[1].astype(jnp.float32)
     query_grad, gain_query_grad = jax.vjp(lambda v, w: head_prep(v, w, angles_q), query_proj, gain_query)[1](
@@ -712,18 +1003,18 @@
     input_extra, gain_input_grad = jax.vjp(norm_rows, inputs, gain_input)[1](normed_grad)
     stream_grad = (hidden_grad + input_extra).astype(jnp.bfloat16)
 
-    squares = jnp.stack([jnp.sum(inputs * inputs), jnp.sum(hidden * hidden), jnp.sum(result * result)])
+    squares = jnp.stack([jnp.sum(inputs * inputs), jnp.sum(hidden * hidden), jnp.sum(result_squares)])
     small = [g.reshape(16, 72) for g in (gain_input_grad, gain_post_grad, gain_mlp_grad, gain_mlp_post_grad)]
     small += [jnp.pad(g.reshape(16, 16), ((0, 0), (0, 56))) for g in (gain_query_grad, gain_key_grad)]
     small.append(jnp.pad(jnp.broadcast_to(squares[None], (16, 3)), ((0, 0), (0, 69))))
     small = jnp.pad(jnp.stack(small, axis=1), ((0, 0), (0, 1), (0, 56))).reshape(4, 4, 8, 128)
     down_blocks = down_term.reshape(16, SLOT, D)[:, :PIECE].reshape(4, 4, PIECE, D)
     both_sum, small_sum, down_sum, qkv_sum, output_sum = sum_seq(
-        "sum_weights", 8, [both_term.reshape(4, 4, 72, 2 * WIDE), small], [down_blocks],
+        "sum_weights", 5, [both_term.reshape(4, 4, 72, 2 * WIDE), small], [down_blocks],
         [(qkv_term.reshape(4, 4, 72, 1536), 768, 768), (output_term.reshape(4, 4, 64, D), 512, 640)],
     )
     small_all, both_rows, qkv_rows, output_rows = exchange_shard(
-        "exchange_grads", 9, [small_sum],
+        "exchange_grads", 6, [small_sum],
         [both_sum.reshape(8, 9, 2 * WIDE), qkv_sum.reshape(8, 9, 768), output_sum.reshape(8, 8, 640)],
     )
 
@@ -741,7 +1032,7 @@
     head_grads = lax.dynamic_slice_in_dim(small_sum, shard * 2, 2, 1)
     stream_rms = jnp.sqrt(small_sum[6, :3] / (32768 * D))
     return (
-        result.astype(jnp.bfloat16)[None],
+        block_output[None],
         stream_grad[None],
         gain_grads[0],
         qkv_grad[:, :1024],

time: 478 us -> 398 us (0.83)
  matrix products: 87.3 us -> 16.4 us
  other arithmetic: 43 us -> 35.5 us
  Pallas kernels: 305 us -> 300 us
    dot_general x6 -> x4, matrix products: 29.3 us -> 4.22 us  [matmul_nt(): lax.dot_general(a, b, (((1,), (1,)), ((), ())), preferred_element_type=jn...]
    dot_general x7 -> x4, matrix products: 29.9 us -> 5.61 us  [matmul(): return jnp.dot(a, b, preferred_element_type=jnp.float32)]
    dot_general x6 -> x4, matrix products: 28.1 us -> 6.52 us  [matmul_tn(): lax.dot_general(a, b, (((0,), (0,)), ((), ())), preferred_element_type=jn...]
    pallas_call x10 -> x7, Pallas kernels: 305 us -> 300 us  [call(): pl.pallas_call(kernel, name=name, out_shape=outs, in_specs=in_specs or [A...]
where the time goes in v2:
time: 398 us; the launch traced here: 392 us
  Pallas kernels  300 us (75%)
  local copies, waits for them, and re-layouts  37.2 us (9%)
  other arithmetic  35.5 us (9%)
  matrix products  16.4 us (4%)
    pallas_call x7, Pallas kernels, call(): pl.pallas_call(kernel, name=name, out_shape=outs, in_specs=in_specs or [A...  300 us
    unnamed x121, local copies, waits for them, and re-layouts  8.02 us

profile of v2, /device:TPU:1, one launch (start us, length us, event | category | flops | bytes accessed | tf_op | source)
XLA Modules:
  0.0 391.8 jit_solution(11515404802141471940)
XLA Ops:
  0.7 0.7 pad_bitcast_fusion
  1.4 0.7 stack.51
  2.7 1.7 reshape.287
  4.9 0.8 reshape.289
  6.2 0.8 pad_maximum_fusion.6.refs_3_
  7.0 0.6 pad_maximum_fusion.15.refs_0_
  7.6 18.2 %exchange_weights.1 = (bf16[8,9,1536]{2,1,0:T(8,128)(2,1)}, bf16[8,8,1152]{2,1,0:T(8,128)(2,1)}, bf16[8,16,128]{2,1,0:T(8,128)(2,1)}, bf16[8,9,1792]{2,1,0:T(8,128)(2,1)}) custom-call(bf16[9,1536]{1,0:T(8,128)(2,1)} %pad_maximum_fusion.15.refs_0_, bf16[8,1152]{1,0:T(8,128)(2,1)} %refs_1_.1, bf16[16,128]{1,0:T(8,128)(2,1)} %pad.55.refs_2_, ...), custom_call_target="tpu_custom_call" | custom-call | tf_op jit(solution)/shard_map/exchange_weights/pallas_call | solution.py:161
  25.9 1.8 reshape.291.refs_0_
  27.7 1.8 reshape.293.refs_3_
  29.5 0.7 slice_bitcast_fusion.4
  30.9 69.4 %gather_weights.1 = (bf16[4,4,72,1792]{3,2,1,0:T(8,128)(2,1)}, bf16[4,4,16,128]{3,2,1,0:T(8,128)(2,1)}, bf16[4,4,54,1152]{3,2,1,0:T(8,128)(2,1)}, bf16[4,4,72,15...) custom-call(bf16[72,1792]{1,0:T(8,128)(2,1)} %reshape.291.refs_0_, bf16[16,128]{1,0:T(8,128)(2,1)} %pad.58.refs_1_, ...), custom_call_target="tpu_custom_call" | custom-call | tf_op jit(solution)/shard_map/gather_weights/pallas_call | solution.py:161
  100.3 0.9 bitcast_convert_fusion
  101.5 3.2 fusion.27
  104.8 1.2 copy-done.10
  106.3 1.4 fusion.66
  109.2 2.5 subtract_convert_fusion
  111.8 1.2 slice.352
  112.9 0.7 pad_maximum_fusion.9.src
  113.7 17.4 %halo.1 = bf16[2,256,512]{2,1,0:T(8,128)(2,1)} custom-call(bf16[256,512]{1,0:T(8,128)(2,1)} %pad_maximum_fusion.9.src), custom_call_target="tpu_custom_call" | custom-call | tf_op jit(solution)/shard_map/halo/pallas_call | solution.py:161
  131.1 1.1 maximum_maximum_fusion
  132.5 0.6 fusion.72
  133.6 1.2 copy-done.3
  134.9 0.8 convolution_convert_fusion.3
  135.8 0.8 copy-done.56
  136.5 1.0 multiply_reduce_fusion.5
  138.7 1.1 multiply_convert_fusion.1.feed_in
  139.8 0.7 broadcast_in_dim_reshape_squeeze.2.gain_in
  140.5 3.1 pad.59
  143.6 105.0 %feed_forward.1 = (bf16[256,1152]{1,0:T(8,128)(2,1)}, f32[256,1152]{1,0:T(8,128)}, f32[1,1152]{1,0:T(1,128)}, f32[1,1152]{1,0:T(1,128)}, bf16[1152,1792]{1,0:T(8,128)(2,1)}, /*index=5*/bf16[896,1152]{1,0:T(8,128)(2,1)}) custom-call(bf16[256,1152]{1,0:T(8,128)(2,1)} %multiply_convert_fusion.1.feed_in, bf16[1152,1792]{1,0:T(8,128)(2,1)} %bitcast.163, ...), custom_call_target="tpu_custom_call" | custom-call | tf_op jit(solution)/shard_map/feed_forward/pallas_call | solution.py:161
  248.7 2.4 multiply_reduce_fusion.1
  251.1 1.3 multiply_reduce_fusion.2
  253.6 2.3 convolution_convert_fusion.1
  255.9 0.9 convolution_convert_fusion.2
  256.8 1.0 copy-done.4
  257.7 0.6 fusion.22
  258.9 0.8 multiply_reduce_fusion
  259.7 0.9 multiply_convert_fusion
  261.9 0.8 fusion.21
  262.7 13.1 %halo_back.1 = bf16[2,256,512]{2,1,0:T(8,128)(2,1)} custom-call(bf16[2,256,512]{2,1,0:T(8,128)(2,1)} %bitcast.167), custom_call_target="tpu_custom_call" | custom-call | tf_op jit(solution)/shard_map/halo_back/pallas_call | solution.py:161
  275.9 1.2 fusion.36
  277.7 1.1 multiply_reduce_fusion.11
  279.8 2.6 multiply_add_fusion.1
  283.3 1.1 fusion.48
  284.5 3.0 convolution_convert_fusion
  287.5 2.0 fusion.11
  290.1 2.0 select_maximum_fusion
  292.8 0.6 pad.67
  293.4 62.5 %sum_weights.1 = (bf16[72,1792]{1,0:T(8,128)(2,1)}, f32[8,128]{1,0:T(8,128)}, bf16[54,1152]{1,0:T(8,128)(2,1)}, bf16[72,768]{1,0:T(8,128)(2,1)}, bf16[64,640]{1,0:T(8,128)(2,1)}) custom-call(bf16[4,4,72,1792]{3,2,1,0:T(8,128)(2,1)} %bitcast.162, f32[4,4,8,128]{3,2,1,0:T(8,128)} %bitcast.173, bf16[4,4,54,1152]{3,2,1,0:T(8,128)(2,1)} %bitcast.169, ...), custom_call_target="tpu_custom_call" | custom-call | tf_op jit(solution)/shard_map/sum_weights/pallas_call | solution.py:161
  355.9 1.8 reshape.310.refs_1_
  357.7 1.6 reshape.311.refs_2_
  359.4 14.8 %exchange_grads.1 = (f32[8,8,128]{2,1,0:T(8,128)}, bf16[8,9,1792]{2,1,0:T(8,128)(2,1)}, bf16[8,9,768]{2,1,0:T(8,128)(2,1)}, bf16[8,8,640]{2,1,0:T(8,128)(2,1)}) custom-call(f32[8,128]{1,0:T(8,128)} %get-tuple-element.55.refs_0_, bf16[8,9,1792]{2,1,0:T(8,128)(2,1)} %reshape.310.refs_1_, bf16[8,9,768]{2,1,0:T(8,128)(2,1)} %reshape.311.refs_2_, ...), custom_call_target="tpu_custom_call" | custom-call | tf_op jit(solution)/shard_map/exchange_grads/pallas_call | solution.py:161
  374.2 1.8 fusion.69
  376.7 1.2 reshape.321
  377.9 1.0 copy.90
  379.6 1.2 reshape.322
  380.7 0.9 convert_reduce_fusion.1
  381.7 0.6 pad_maximum_fusion.16
  382.3 1.0 convert_reduce_fusion
  383.3 0.6 pad_maximum_fusion.14
  384.5 0.8 reduce_sum.237
  387.0 1.6 convert_element_type.162
  388.6 0.7 multiply_multiply_fusion.3
  389.3 1.2 fusion.25
  390.5 0.8 copy.110
  (195 shorter events, 16.6 us)
Async XLA Ops:
  0.6 4.2 %copy-start.23 = (bf16[9,6912]{1,0:T(8,128)(2,1)S(1)}, bf16[9,6912]{1,0:T(8,128)(2,1)}, u32[]{:S(2)}) copy-start(bf16[9,6912]{1,0:T(8,128)(2,1)} %param.29) | copy-start | bytes 373252
  4.8 2.1 copy-start.32
  4.8 2.1 copy-start.46
  4.9 2.1 copy-start.47
  7.0 94.3 %copy-start.2 = (bf16[1,256,1152]{2,1,0:T(8,128)(2,1)S(1)}, bf16[1,256,1152]{2,1,0:T(8,128)(2,1)}, u32[]{:S(2)}) copy-start(bf16[1,256,1152]{2,1,0:T(8,128)(2,1)} %param.16) | copy-start | bytes 1769476
  101.5 3.3 copy-start.42
  101.5 3.3 copy-start.38
  104.8 1.2 copy-start.10
  106.1 1.9 copy-start.44
  106.1 1.7 copy-start.35
  106.3 1.4 copy-start.33
  107.7 0.7 copy-start.5
  107.7 0.8 copy-start.7
  107.8 0.8 copy-start.54
  108.6 22.4 %copy-start.40 = (f32[256]{0:T(256)}, f32[256]{0:T(256)S(1)}, u32[]{:S(2)}) copy-start(f32[256]{0:T(256)S(1)} %get-tuple-element.133) | copy-start | bytes 3076
  108.6 22.4 %copy-start.52 = (f32[128]{0:T(128)}, f32[128]{0:T(128)S(1)}, u32[]{:S(2)}) copy-start(f32[128]{0:T(128)S(1)} %multiply_exponential_fusion) | copy-start | bytes 1540
  109.2 21.9 %copy-start.14 = (f32[256,128]{1,0:T(8,128)}, f32[256,128]{1,0:T(8,128)S(1)}, u32[]{:S(2)}) copy-start(f32[256,128]{1,0:T(8,128)S(1)} %get-tuple-element.123) | copy-start | bytes 393220
  111.8 20.8 %copy-start.19 = (bf16[1024,128]{1,0:T(8,128)(2,1)}, bf16[1024,128]{1,0:T(8,128)(2,1)S(1)}, u32[]{:S(2)}) copy-start(bf16[1024,128]{1,0:T(8,128)(2,1)S(1)} %get-tuple-element.89) | copy-start | bytes 786436
  111.8 20.8 %copy-start.21 = (bf16[1024,128]{1,0:T(8,128)(2,1)}, bf16[1024,128]{1,0:T(8,128)(2,1)S(1)}, u32[]{:S(2)}) copy-start(bf16[1024,128]{1,0:T(8,128)(2,1)S(1)} %get-tuple-element.90) | copy-start | bytes 786436
  132.2 1.4 copy-start.16
  133.2 1.7 copy-start.3
  134.9 1.7 copy-start.56
  135.7 1.8 copy-start.24
  135.7 1.8 copy-start.26
  135.8 1.8 copy-start.28
  135.8 1.8 copy-start.30
  137.5 0.6 copy-start.50
  138.6 5.0 %copy-start = (f32[256,1152]{1,0:T(8,128)}, f32[256,1152]{1,0:T(8,128)S(1)}, u32[]{:S(2)}) copy-start(f32[256,1152]{1,0:T(8,128)S(1)} %get-tuple-element.81.hidden_in) | copy-start | bytes 3538948
  138.6 110.0 %copy-start.37 = (f32[256]{0:T(256)}, f32[256]{0:T(256)S(1)}, u32[]{:S(2)}) copy-start(f32[256]{0:T(256)S(1)} %fusion.55) | copy-start | bytes 3076
  143.6 105.1 %copy-start.1 = (f32[256,1152]{1,0:T(8,128)S(1)}, f32[256,1152]{1,0:T(8,128)}, u32[]{:S(2)}) copy-start(f32[256,1152]{1,0:T(8,128)} %copy-done) | copy-start | bytes 3538948
  248.6 2.5 copy-start.9
  248.6 2.5 copy-start.11
  251.1 1.4 copy-start.51
  252.5 0.9 copy-start.25
  252.5 1.0 copy-start.27
  252.5 1.0 copy-start.29
  252.5 1.1 copy-start.31
  253.6 2.3 copy-start.57
  255.9 1.9 copy-start.4
  257.7 1.1 copy-start.17
  259.7 1.0 copy-start.20
  259.7 1.0 copy-start.22
  260.7 1.2 copy-start.12
  275.8 1.3 copy-start.41
  275.8 1.3 copy-start.53
  275.8 1.9 copy-start.34
  275.9 1.9 copy-start.36
  275.9 3.0 copy-start.45
  275.9 3.0 copy-start.13
  278.9 0.9 copy-start.15
  279.8 2.6 copy-start.6
  279.8 2.6 copy-start.8
  283.2 1.2 copy-start.39
  284.4 3.0 copy-start.55
  287.5 2.0 copy-start.49
  287.5 5.1 %copy-start.48 = (f32[1,1152]{1,0:T(1,128)S(1)}, f32[1,1152]{1,0:T(1,128)}, u32[]{:S(2)}) copy-start(f32[1,1152]{1,0:T(1,128)} %get-tuple-element.52) | copy-start | bytes 13828
  379.6 9.1 %copy-start.43 = (f32[256]{0:T(256)S(1)}, f32[256]{0:T(256)}, u32[]{:S(2)}) copy-start(f32[256]{0:T(256)} %copy-done.42) | copy-start | bytes 3076
  389.3 1.2 copy-start.18

commit v3 on v2

--- a/solution.py
+++ b/solution.py
@@ -153,7 +153,7 @@
 VMEM = pl.BlockSpec(memory_space=pltpu.VMEM)
 
 
-def call(kernel, name, number, outs, ins, scratch, copies, in_specs=None, out_specs=None, local=0):
+def call(kernel, name, number, outs, ins, scratch, copies, in_specs=None, out_specs=None, local=0, aliases=None):
     outs = [jax.ShapeDtypeStruct(shape, dtype) for shape, dtype in outs]
     scratch = list(scratch) + [pltpu.SemaphoreType.DMA((copies,)), pltpu.SemaphoreType.DMA((copies,))]
     if local:
@@ -165,6 +165,7 @@
         in_specs=in_specs or [ANY] * len(ins),
         out_specs=out_specs or [ANY] * len(outs),
         scratch_shapes=scratch,
+        input_output_aliases=aliases or {},
         compiler_params=pltpu.CompilerParams(
             collective_id=number, has_side_effects=True, vmem_limit_bytes=56 * MIB
         ),
@@ -850,27 +851,377 @@
     )
 
 
+class Either:
+    def __init__(self, core, sems, make):
+        self.core, start = core, sems.used
+        self.variants = []
+        for order in (0, 1):
+            sems.used = start
+            self.variants.append(make(order))
+
+    def run(self, name):
+        for order in (0, 1):
+            pl.when(self.core == order)(getattr(self.variants[order], name))
+
+    def first(self):
+        self.run("first")
+
+    def relay(self):
+        self.run("relay")
+
+    def last(self):
+        self.run("last")
+
+    def close(self):
+        self.run("close")
+
+
+def split_lanes(ref, h):
+    halves = lane_halves(ref.shape[-1])
+    return None if halves[h] is None else ref.at[:, pl.ds(*halves[h])]
+
+
+def whole_ref(ref):
+    return ref
+
+
+def ring_row(own, out, cut, sems):
+    x, y, z, c = place()
+
+    def make(order):
+        slot = (lambda k: cut(out.at[x, k])) if order == 0 else (lambda k: cut(out.at[k, z]))
+        peer = (lambda k: device(x, y, k, c)) if order == 0 else (lambda k: device(k, y, z, c))
+        return RingGather(own, slot, lambda k, h: split_lanes(slot(k), h), (z, x)[order], peer, sems)
+
+    return Either(c, sems, make)
+
+
+def ring_rest(out, cut, sems):
+    x, y, z, c = place()
+
+    def make(order):
+        if order == 0:
+            slot, half, me = lambda k: cut(out.at[k]), lambda k, h: cut(out.at[k, pl.ds(2 * h, 2)]), x
+        else:
+            slot, half, me = lambda k: cut(out.at[:, k]), lambda k, h: cut(out.at[pl.ds(2 * h, 2), k]), z
+        peer = (lambda k: device(k, y, z, c)) if order == 0 else (lambda k: device(x, y, k, c))
+        return RingGather(slot(me), slot, half, me, peer, sems)
+
+    return Either(c, sems, make)
+
+
+class Crossing:
+    def __init__(self, out, cut, other_cut, sems):
+        x, y, z, c = place()
+        self.pushes = []
+        for d in range(4):
+
+            def make(order, d=d):
+                quarters = out.at[(x + d) % 4], out.at[:, (z + d) % 4]
+                piece, lands = cut(quarters[order]), other_cut(quarters[1 - order])
+                return Push(piece, piece, sems, device(x, y, z, 1 - c), lands)
+
+            self.pushes.append(Either(c, sems, make))
+
+    def start(self, d):
+        self.pushes[d].run("start")
+
+    def close(self):
+        for push in self.pushes:
+            push.run("arrived")
+            push.run("sent")
+
+
+def turn(values, cosine, sine):
+    middle = values.shape[-1] // 2
+    leading, trailing = values[:, :middle], values[:, middle:]
+    return jnp.concatenate([leading * cosine - trailing * sine, trailing * cosine + leading * sine], axis=1)
+
+
+def unit_rows(values):
+    scale = lax.rsqrt(jnp.mean(values * values, axis=-1, keepdims=True) + EPSILON)
+    return values * scale, scale
+
+
+def allowed_keys(offset, beginning, rows, span):
+    query = offset + lax.broadcasted_iota(jnp.int32, (rows, span), 0)
+    key = offset + rows - span + lax.broadcasted_iota(jnp.int32, (rows, span), 1)
+    return (key <= query) & (key > query - WINDOW) & (key >= beginning)
+
+
+def gain_row(table, first, each, width):
+    lane = lax.broadcasted_iota(jnp.int32, (128, width), 1)
+    row = lax.broadcasted_iota(jnp.int32, (128, width), 0)
+    owner = (lane * 7282) >> 16 if each == 9 else lane >> 1
+    pick = (row == first + lane - owner * each).astype(jnp.float32).astype(jnp.bfloat16)
+    spread = dot(table, pick, 1, 0)
+    return jnp.sum(jnp.where(row == owner, spread, 0.0), axis=0, keepdims=True)
+
+
+def lanes_of(start, size):
+    return lambda ref: ref.at[(slice(None),) * (len(ref.shape) - 1) + (pl.ds(start, size),)]
+
+
+def attend(number, stream, doc_starts, own_qkv, own_gains, own_output, own_both, own_down):
+    tokens = stream.shape[0]
+    span = tokens + WINDOW
+
+    def kernel(
+        stream_in, starts_in, qkv_in, gains_in, output_in, both_in, down_in,
+        normed_out, query_out, key_out, turned_out, kv_out, probs_out, mixed_out, branch_out, hidden_out, feed_out,
+        gains_out, cosine_out, sine_out, qkv_out, output_out, both_out, down_out,
+        qkv_box, gains_box, both_box, flat, merge, qkv_own, gains_own, both_own, qkv_all, gains_all, output_all, kv,
+        send, recv, here,
+    ):
+        x, y, z, c = place()
+        q, s = lax.axis_index("seq"), lax.axis_index("shard")
+        sems = Sems(send, recv)
+        after, before = {"seq": (q + 1) % 16, "shard": s}, {"seq": (q + 15) % 16, "shard": s}
+        greet(
+            [device(x, y + dy, z, (c + dc) % 2) for dy, dc in SHARD_STEPS]
+            + [device(x, y, z + 1, c), device(x, y, z + 3, c), device(x + 1, y, z, c), device(x + 3, y, z, c)]
+            + [after, before]
+        )
+        sent = []
+
+        def spread(source, box, pieces=False):
+            pushes = []
+            for dy, dc in SHARD_STEPS:
+                to, back = (y + dy) % 4 * 2 + (c + dc) % 2, (y + 4 - dy) % 4 * 2 + (c + 2 - dc) % 2
+                src = source.at[to] if pieces else source
+                push = Push(src, box.at[s], sems, device(x, y + dy, z, (c + dc) % 2), box.at[back])
+                push.start()
+                pushes.append(push)
+            box[s] = source[s] if pieces else source[...]
+            sent.extend(pushes)
+            return pushes
+
+        def collect(pushes, box, own):
+            for push in pushes:
+                push.arrived()
+            tiles = own.shape[-1] // 128
+            for d in range(8):
+                flat[: 9 * tiles, :] = box[d].astype(jnp.float32)
+                for j in range(tiles):
+                    merge[9 * d : 9 * d + 9, 128 * j : 128 * (j + 1)] = flat[pl.ds(j, 9, tiles), :]
+            own[...] = merge[:, : own.shape[-1]].astype(own.dtype)
+
+        my_lanes = lanes_of(pl.multiple_of(c * 768, 128), 768)
+        their_lanes = lanes_of(pl.multiple_of((1 - c) * 768, 128), 768)
+        mine = lambda ref: ref.at[(slice(None),) * (len(ref.shape) - 3) + (s,)]
+
+        got_qkv = spread(qkv_in, qkv_box)
+        got_gains = spread(gains_in, gains_box)
+        down_ring = ring_row(down_in, down_out, whole_ref, sems)
+        output_ring = ring_row(output_in, output_all, mine, sems)
+        down_ring.first()
+        output_ring.first()
+        inputs = stream_in[...].astype(jnp.float32)
+        unit = unit_rows(inputs)[0]
+        starts = starts_in[...]
+        positions = q * tokens + lax.broadcasted_iota(jnp.int32, (tokens, 1), 0)
+        beginning = jnp.zeros((tokens, 1), jnp.int32)
+        for j in range(8):
+            start = starts[0:1, j : j + 1]
+            beginning = jnp.maximum(beginning, jnp.where(start <= positions, start, 0))
+        steps = lax.broadcasted_iota(jnp.int32, (1, HEAD_DIM // 2), 1).astype(jnp.float32)
+        angles = (positions - beginning).astype(jnp.float32) * jnp.exp(steps * (-2.0 * math.log(10000.0) / HEAD_DIM))
+        cosine_out[...] = jnp.cos(angles)
+        sine_out[...] = jnp.sin(angles)
+
+        own = lambda src, dst, at: pltpu.make_async_copy(src, dst, here.at[at])
+        collect(got_qkv, qkv_box, qkv_own)
+        qkv_ring = ring_row(my_lanes(qkv_own), qkv_all, my_lanes, sems)
+        qkv_ring.first()
+        got_both = spread(both_in, both_box, True)
+        for push in got_gains:
+            push.arrived()
+        for d in range(8):
+            gains_own[d : d + 1, :] = gains_box[d, 0:1, :]
+        gains_ring = ring_row(gains_own, gains_all, whole_ref, sems)
+        gains_ring.first()
+        copies = [
+            own(my_lanes(qkv_own), my_lanes(qkv_all.at[x, z]), 0),
+            own(gains_own, gains_all.at[x, z], 1),
+            own(down_in, down_out.at[x, z], 2),
+            own(output_in, output_all.at[x, z, s], 3),
+        ]
+        for copy in copies:
+            copy.start()
+        down_ring.relay()
+        output_ring.relay()
+        qkv_ring.relay()
+        gains_ring.relay()
+        for copy in copies:
+            copy.wait()
+        qkv_ring.last()
+        gains_ring.last()
+        qkv_rest = ring_rest(qkv_all, my_lanes, sems)
+        gains_rest = ring_rest(gains_all, whole_ref, sems)
+        qkv_cross = Crossing(qkv_all, my_lanes, their_lanes, sems)
+        qkv_rest.first()
+        gains_rest.first()
+        qkv_cross.start(0)
+        down_ring.last()
+        output_ring.last()
+        down_rest = ring_rest(down_out, whole_ref, sems)
+        output_rest = ring_rest(output_all, mine, sems)
+        output_rest.first()
+        down_rest.first()
+        collect(got_both, both_box, both_own)
+        both_ring = ring_row(both_own, both_out, whole_ref, sems)
+        both_ring.first()
+        both_copy = own(both_own, both_out.at[x, z], 4)
+        both_copy.start()
+        qkv_rest.relay()
+        gains_rest.relay()
+        qkv_cross.start(3)
+        qkv_cross.start(1)
+        output_rest.relay()
+        both_ring.relay()
+        down_rest.relay()
+        qkv_rest.last()
+        gains_rest.last()
+        qkv_cross.start(2)
+        output_rest.last()
+        other = device(x, y, z, 1 - c)
+        column = lambda k: output_all.at[:, :, k * 2 + c]
+        output_y = RingGather(
+            column(y), column, lambda k, h: output_all.at[pl.ds(2 * h, 2), :, k * 2 + c],
+            y, lambda k: device(x, k, z, c), sems,
+        )
+        output_cross = [
+            Push(column((y + d) % 4), column((y + d) % 4), sems, other, output_all.at[:, :, (y + d) % 4 * 2 + 1 - c])
+            for d in range(4)
+        ]
+        output_y.first()
+        output_cross[0].start()
+        both_ring.last()
+        both_copy.wait()
+        both_rest = ring_rest(both_out, whole_ref, sems)
+        table = gains_all[...].reshape(128, 128).astype(jnp.bfloat16)
+        for g in range(4):
+            gains_out[g : g + 1, :] = gain_row(table, 16 * g, 9, D)
+        for g in range(2):
+            gains_out[4 + g : 5 + g, :HEAD_DIM] = gain_row(table, 64 + 16 * g, 2, HEAD_DIM)
+        qkv_cross.close()
+
+        @pl.loop(0, 8)
+        def _(i):
+            pair = [qkv_all[i // 2, i % 2 * 2 + k].astype(jnp.float32) for k in range(2)]
+            qkv_out[pl.ds(pl.multiple_of(144 * i, 144), 144), :] = jnp.concatenate(pair, axis=0).astype(jnp.bfloat16)
+
+        near = Push(kv.at[2], kv.at[1], sems, after)
+        far = Push(kv.at[1], kv.at[0], sems, after)
+        normed = (unit * gains_out[0:1, :]).astype(jnp.bfloat16)
+        normed_out[...] = normed
+        key_value = dot(normed, qkv_out[:, 1024:], 1, 0)
+        key = key_value[:, :HEAD_DIM]
+        key_out[...] = key
+        key_turned = turn(unit_rows(key)[0] * gains_out[5:6, :HEAD_DIM], cosine_out[...], sine_out[...])
+        kv[2, :, :HEAD_DIM] = key_turned.astype(jnp.bfloat16)
+        kv[2, :, HEAD_DIM:] = key_value[:, HEAD_DIM:].astype(jnp.bfloat16)
+        near.start()
+        both_rest.first()
+        output_y.relay()
+        output_cross[1].start()
+        output_cross[3].start()
+        for h in range(HEADS):
+            lanes = slice(h * HEAD_DIM, (h + 1) * HEAD_DIM)
+            span_h = slice(h * tokens, (h + 1) * tokens)
+            query = dot(normed, qkv_out[:, lanes], 1, 0)
+            query_out[span_h, :] = query
+            turned = turn(unit_rows(query)[0] * gains_out[4:5, :HEAD_DIM], cosine_out[...], sine_out[...])
+            turned_out[span_h, :] = turned.astype(jnp.bfloat16)
+        near.arrived()
+        far.start()
+        output_y.last()
+        output_cross[2].start()
+        down_rest.last()
+        both_rest.relay()
+        for push in output_cross:
+            push.arrived()
+
+        @pl.loop(0, 16)
+        def _(i):
+            for j in range(4):
+                pair = [output_all[i // 4, i % 4, 2 * j + k].astype(jnp.float32) for k in range(2)]
+                rows = pl.ds(pl.multiple_of(64 * i + 16 * j, 16), 16)
+                output_out[rows, :] = jnp.concatenate(pair, axis=0).astype(jnp.bfloat16)
+
+        far.arrived()
+        kv_out[...] = kv[...].reshape(span, 2 * HEAD_DIM)
+        allowed = allowed_keys(q * tokens, beginning, tokens, span)
+        keys, values = kv_out[:, :HEAD_DIM], kv_out[:, HEAD_DIM:]
+        for h in range(HEADS):
+            span_h = slice(h * tokens, (h + 1) * tokens)
+            scores = dot(turned_out[span_h, :], keys, 1, 1) * HEAD_DIM ** (-0.5)
+            scores = jnp.where(allowed, scores, NEGATIVE)
+            exponent = jnp.exp(scores - jnp.max(scores, axis=-1, keepdims=True))
+            probs = exponent / jnp.sum(exponent, axis=-1, keepdims=True)
+            probs_out[span_h, :] = probs
+            mixed_out[:, h * HEAD_DIM : (h + 1) * HEAD_DIM] = dot(probs.astype(jnp.bfloat16), values, 1, 0).astype(
+                jnp.bfloat16
+            )
+        branch = dot(mixed_out[...], output_out[...], 1, 0)
+        branch_out[...] = branch
+        hidden = inputs + unit_rows(branch)[0] * gains_out[1:2, :]
+        hidden_out[...] = hidden
+        feed_out[...] = (unit_rows(hidden)[0] * gains_out[2:3, :]).astype(jnp.bfloat16)
+        both_rest.last()
+        rings = [qkv_ring, gains_ring, down_ring, output_ring, both_ring]
+        rings += [qkv_rest, gains_rest, down_rest, output_rest, both_rest, output_y]
+        for ring in rings:
+            ring.close()
+        for push in sent + output_cross + [near, far]:
+            push.sent()
+
+    low, wide = jnp.bfloat16, jnp.float32
+    outs = [
+        ((tokens, D), low),
+        ((HEADS * tokens, HEAD_DIM), wide),
+        ((tokens, HEAD_DIM), wide),
+        ((HEADS * tokens, HEAD_DIM), low),
+        ((span, 2 * HEAD_DIM), low),
+        ((HEADS * tokens, span), wide),
+        ((tokens, HEADS * HEAD_DIM), low),
+        ((tokens, D), wide),
+        ((tokens, D), wide),
+        ((tokens, D), low),
+        ((8, D), wide),
+        ((tokens, HEAD_DIM // 2), wide),
+        ((tokens, HEAD_DIM // 2), wide),
+        ((D, 1536), low),
+        ((HEADS * HEAD_DIM, D), low),
+        ((4, 4, 72, 2 * WIDE), low),
+        ((4, 4, PIECE, D), low),
+    ]
+    scratch = [
+        pltpu.VMEM((8, 108, 128), low),
+        pltpu.VMEM((8, 8, 128), wide),
+        pltpu.VMEM((8, 126, 128), low),
+        pltpu.VMEM((128, 128), wide),
+        pltpu.VMEM((72, 2 * WIDE), wide),
+        pltpu.VMEM((72, 1536), low),
+        pltpu.VMEM((8, 128), wide),
+        pltpu.VMEM((72, 2 * WIDE), low),
+        pltpu.VMEM((4, 4, 72, 1536), low),
+        pltpu.VMEM((4, 4, 8, 128), wide),
+        pltpu.VMEM((4, 4, 8, 8, D), low),
+        pltpu.VMEM((3, tokens, 2 * HEAD_DIM), low),
+    ]
+    return call(
+        kernel, "attend", number, outs, [stream, doc_starts, own_qkv, own_gains, own_output, own_both, own_down],
+        scratch, 21 + 10 * 4 + 4 + 4 + 4 + 2, in_specs=[VMEM] * 7, out_specs=[VMEM] * 15 + [ANY] * 2, local=5,
+    )
+
+
 def norm_rows(values, weight):
     return values * lax.rsqrt(jnp.mean(values * values, axis=-1, keepdims=True) + EPSILON) * weight
 
 
-def rotate(values, angles):
-    middle = values.shape[-1] // 2
-    leading = values[..., :middle]
-    trailing = values[..., middle:]
-    cosine = jnp.cos(angles)
-    sine_part = jnp.sin(angles)
-    return jnp.concatenate(
-        [leading * cosine - trailing * sine_part, trailing * cosine + leading * sine_part], axis=-1
-    )
-
-
-def head_prep(values, weight, angles):
-    return rotate(norm_rows(values, weight), angles)
-
-
-def frequencies(width):
-    return jnp.exp(jnp.arange(width // 2, dtype=jnp.float32) * (-2.0 * math.log(10000.0) / width))
+def head_prep(values, weight, cosine, sine):
+    return turn(norm_rows(values, weight), cosine, sine)
 
 
 def matmul(a, b):
@@ -911,67 +1262,27 @@
     scale = HEAD_DIM ** (-0.5)
     inputs = stream[0].astype(jnp.float32)
     upstream = cotangent[0].astype(jnp.float32)
-    offset = lax.axis_index("seq") * tokens
-    positions = offset + jnp.arange(tokens, dtype=jnp.int32)
-    starts_row = doc_starts[0]
-    beginning = jnp.max(
-        jnp.where(starts_row[None, :] <= positions[:, None], starts_row[None, :], 0), axis=1
+    own_qkv = jnp.concatenate([query_weight, key_weight, value_weight], axis=1)
+    norms = (attention_norm, attention_post_norm, mlp_norm, mlp_post_norm, query_norm, key_norm)
+    own_gains = jnp.concatenate([jnp.pad(g, (0, 16 - g.shape[0])) for g in norms] + [jnp.zeros((32,), jnp.bfloat16)])
+    own_gains = jnp.broadcast_to(own_gains.astype(jnp.float32)[None], (8, 128))
+    own_both = jnp.concatenate([split_hidden(gate_weight), split_hidden(up_weight)], axis=2)
+    (
+        normed, query_proj, key_proj, query_rot, kv, probability, mixed, branch, hidden, feed,
+        gain_rows, cosine, sine, full_qkv, full_output, both16, down16,
+    ) = attend(
+        0, stream[0], doc_starts, own_qkv.reshape(108, 128), own_gains, output_weight, own_both.reshape(8, 126, 128),
+        down_weight,
     )
-    angles = (positions - beginning).astype(jnp.float32)[:, None] * frequencies(HEAD_DIM)[None, :]
-    angles_q = jnp.concatenate([angles] * HEADS, axis=0)
-
-    own_qkv = jnp.concatenate([query_weight, key_weight, value_weight], axis=1)
-    own_gains = jnp.stack(
-        [jnp.pad(g, (0, 9 - g.shape[0])) for g in (attention_norm, attention_post_norm, mlp_norm, mlp_post_norm, query_norm, key_norm)]
-    )
-    own_both = jnp.concatenate([split_hidden(gate_weight), split_hidden(up_weight)], axis=2)
-    qkv8, out8, gains8, both8 = exchange_shard(
-        "exchange_weights", 0, [own_qkv, output_weight, pad_rows(own_gains, 16)], [own_both]
-    )
-    gains_row = gains8[:, :6, :9].transpose(1, 0, 2).reshape(6, 72)
-    both16, gains16, down16, qkv16, out16 = gather_seq(
-        "gather_weights", 1, [both8.reshape(72, 2 * WIDE), pad_rows(gains_row, 16)], [down_weight],
-        [qkv8.reshape(72, 1536), out8.reshape(64, D)],
-    )
+    gain_input, gain_post, gain_mlp, gain_mlp_post = (gain_rows[i] for i in range(4))
+    gain_query, gain_key = gain_rows[4, :HEAD_DIM], gain_rows[5, :HEAD_DIM]
+    keys_all, values_all = kv[:, :HEAD_DIM], kv[:, HEAD_DIM:]
+    probability_low = probability.astype(jnp.bfloat16)
     full_both = both16.reshape(D, 2 * WIDE)
     full_down = jnp.pad(down16.reshape(16, PIECE, D), ((0, 0), (0, SLOT - PIECE), (0, 0))).reshape(WIDE, D)
-    full_qkv = qkv16.reshape(D, 1536)
-    full_output = out16.reshape(HEADS * HEAD_DIM, D)
-    gains = gains16.reshape(16, 16, 128).astype(jnp.float32)
-    gain_input, gain_post, gain_mlp, gain_mlp_post = (gains[:, i, :72].reshape(D) for i in range(4))
-    gain_query, gain_key = (gains[:, i, :72].reshape(16, 8, 9)[:, :, :2].reshape(HEAD_DIM) for i in (4, 5))
-
-    normed = norm_rows(inputs, gain_input).astype(jnp.bfloat16)
-    projected = matmul(normed, full_qkv)
-    query_proj = heads_first(projected[:, :1024])
-    key_proj = projected[:, 1024:1280]
-    values_low = projected[:, 1280:].astype(jnp.bfloat16)
-    query_rot = head_prep(query_proj, gain_query, angles_q).astype(jnp.bfloat16)
-    key_rot = head_prep(key_proj, gain_key, angles).astype(jnp.bfloat16)
-    own_kv = jnp.concatenate([key_rot, values_low], axis=1)
-    far_kv = halo("halo", 2, (2, 1), own_kv)
-    kv = jnp.concatenate([far_kv.reshape(2 * tokens, 2 * HEAD_DIM), own_kv], axis=0)
-    keys_all, values_all = kv[:, :HEAD_DIM], kv[:, HEAD_DIM:]
-    key_place = offset - WINDOW + jnp.arange(tokens + WINDOW, dtype=jnp.int32)
-    allowed = (
-        (key_place[None, :] <= positions[:, None])
-        & (key_place[None, :] > positions[:, None] - WINDOW)
-        & (key_place[None, :] >= beginning[:, None])
-    )
-    allowed = jnp.concatenate([allowed] * HEADS, axis=0)
-    scores = jnp.where(allowed, matmul_nt(query_rot, keys_all) * scale, NEGATIVE)
-    highest = jnp.max(scores, axis=-1, keepdims=True)
-    exponent = jnp.exp(scores - highest)
-    totals = jnp.sum(exponent, axis=-1, keepdims=True)
-    probability = exponent / totals
-    probability_low = probability.astype(jnp.bfloat16)
-    mixed = heads_last(matmul(probability_low, values_all).astype(jnp.bfloat16))
-    branch = matmul(mixed, full_output)
-    hidden = inputs + norm_rows(branch, gain_post)
-    feed = norm_rows(hidden, gain_mlp).astype(jnp.bfloat16)
 
     block_output, feed_grad, gain_mlp_post_grad, result_squares, both_term, down_term = feed_forward(
-        "feed_forward", 3, feed, full_both, full_down, hidden, cotangent[0], gain_mlp_post[None]
+        "feed_forward", 2, feed, full_both, full_down, hidden, cotangent[0], gain_mlp_post[None]
     )
 
     hidden_extra, gain_mlp_grad = jax.vjp(norm_rows, hidden, gain_mlp)[1](feed_grad)
@@ -988,13 +1299,13 @@
     value_grads = matmul_tn(probability_low, mixed_grad)
     kv_grads = jnp.concatenate([key_grads, value_grads], axis=1)
     returned = halo(
-        "halo_back", 4, (-2, -1), kv_grads[:WINDOW].astype(jnp.bfloat16).reshape(2, tokens, 2 * HEAD_DIM)
+        "halo_back", 3, (-2, -1), kv_grads[:WINDOW].astype(jnp.bfloat16).reshape(2, tokens, 2 * HEAD_DIM)
     )
     kv_own = kv_grads[WINDOW:] + returned[0].astype(jnp.float32) + returned[1].astype(jnp.float32)
-    query_grad, gain_query_grad = jax.vjp(lambda v, w: head_prep(v, w, angles_q), query_proj, gain_query)[1](
+    query_grad, gain_query_grad = jax.vjp(lambda v, w: head_prep(v, w, jnp.concatenate([cosine] * HEADS), jnp.concatenate([sine] * HEADS)), query_proj, gain_query)[1](
         query_grad_rot
     )
-    key_grad, gain_key_grad = jax.vjp(lambda v, w: head_prep(v, w, angles), key_proj, gain_key)[1](
+    key_grad, gain_key_grad = jax.vjp(lambda v, w: head_prep(v, w, cosine, sine), key_proj, gain_key)[1](
         kv_own[:, :HEAD_DIM]
     )
     qkv_low = jnp.concatenate([heads_last(query_grad), key_grad, kv_own[:, HEAD_DIM:]], axis=1).astype(jnp.bfloat16)
@@ -1010,11 +1321,11 @@
     small = jnp.pad(jnp.stack(small, axis=1), ((0, 0), (0, 1), (0, 56))).reshape(4, 4, 8, 128)
     down_blocks = down_term.reshape(16, SLOT, D)[:, :PIECE].reshape(4, 4, PIECE, D)
     both_sum, small_sum, down_sum, qkv_sum, output_sum = sum_seq(
-        "sum_weights", 5, [both_term.reshape(4, 4, 72, 2 * WIDE), small], [down_blocks],
+        "sum_weights", 4, [both_term.reshape(4, 4, 72, 2 * WIDE), small], [down_blocks],
         [(qkv_term.reshape(4, 4, 72, 1536), 768, 768), (output_term.reshape(4, 4, 64, D), 512, 640)],
     )
     small_all, both_rows, qkv_rows, output_rows = exchange_shard(
-        "exchange_grads", 6, [small_sum],
+        "exchange_grads", 5, [small_sum],
         [both_sum.reshape(8, 9, 2 * WIDE), qkv_sum.reshape(8, 9, 768), output_sum.reshape(8, 8, 640)],
     )
 

time: 398 us -> 342 us (0.86); the launches traced: 392 us -> 341 us
  Pallas kernels: 300 us -> 278 us
  other arithmetic: 35.5 us -> 17.9 us
  local copies, waits for them, and re-layouts: 37.2 us -> 31.6 us
    pallas_call x7 -> x5, Pallas kernels: 300 us -> 278 us  [call(): pl.pallas_call(kernel, name=name, out_shape=outs, in_specs=in_specs or [A...]
    dot_general x4 -> x1, matrix products: 5.61 us -> 0.58 us  [matmul(): return jnp.dot(a, b, preferred_element_type=jnp.float32)]
    unnamed x121 -> x70, local copies, waits for them, and re-layouts: 8.02 us -> 7.62 us
where the time goes in v3:
time: 342 us; the launch traced here: 341 us
  Pallas kernels  278 us (81%)
  local copies, waits for them, and re-layouts  31.6 us (9%)
  other arithmetic  17.9 us (5%)
  matrix products  12.7 us (4%)
    pallas_call x5, Pallas kernels, call(): pl.pallas_call(kernel, name=name, out_shape=outs, in_specs=in_specs or [A...  278 us
    unnamed x70, local copies, waits for them, and re-layouts  7.62 us

profile of v3, /device:TPU:1, one launch (start us, length us, event | category | flops | bytes accessed | tf_op | source)
XLA Modules:
  0.0 341.5 jit_solution(16867553945318671671)
XLA Ops:
  0.7 1.7 reshape.270
  2.5 0.3 reshape.271
  2.8 0.8 reshape.272
  3.9 0.3 reshape.273
  4.2 0.7 copy.57.both_in
  5.0 0.7 reshape.269.qkv_in
  5.9 0.6 broadcast_in_dim.19.gains_in
  6.5 81.6 %attend.1 = (bf16[256,1152]{1,0:T(8,128)(2,1)}, f32[1024,256]{1,0:T(8,128)}, f32[256,256]{1,0:T(8,128)}, bf16[1024,256]{1,0:T(8,128)(2,1)}, bf16[768,512]{1,0:T(...) custom-call(bf16[256,1152]{1,0:T(8,128)(2,1)} %bitcast.105, ...), custom_call_target="tpu_custom_call" | custom-call | tf_op jit(solution)/shard_map/attend/pallas_call | solution.py:161
  88.0 1.5 slice_reduce_fusion
  89.6 3.1 pad.66
  92.7 105.2 %feed_forward.1 = (bf16[256,1152]{1,0:T(8,128)(2,1)}, f32[256,1152]{1,0:T(8,128)}, f32[1,1152]{1,0:T(1,128)}, f32[1,1152]{1,0:T(1,128)}, bf16[1152,1792]{1,0:T(8,128)(2,1)}, /*index=5*/bf16[896,1152]{1,0:T(8,128)(2,1)}) custom-call(bf16[256,1152]{1,0:T(8,128)(2,1)} %get-tuple-element.48.feed_in, bf16[1152,1792]{1,0:T(8,128)(2,1)} %bitcast.107, ...), custom_call_target="tpu_custom_call" | custom-call | tf_op jit(solution)/shard_map/feed_forward/pallas_call | solution.py:161
  198.1 1.1 copy-done.2
  199.1 2.6 multiply_reduce_fusion.1
  201.8 0.8 multiply_reduce_fusion.2
  202.6 0.3 fusion.5
  202.9 0.8 copy-done.14
  203.6 2.3 convolution_convert_fusion.1
  205.9 0.9 convolution_convert_fusion.2
  206.9 1.0 copy-done
  207.8 0.6 fusion
  208.4 0.5 copy-done.12
  208.9 0.7 multiply_reduce_fusion
  209.7 0.4 multiply_convert_fusion
  210.1 0.6 copy-done.24
  210.7 0.6 fusion.36
  211.3 0.8 fusion.12
  212.2 14.4 %halo_back.1 = bf16[2,256,512]{2,1,0:T(8,128)(2,1)} custom-call(bf16[2,256,512]{2,1,0:T(8,128)(2,1)} %bitcast.109), custom_call_target="tpu_custom_call" | custom-call | tf_op jit(solution)/shard_map/halo_back/pallas_call | solution.py:161
  226.6 1.2 fusion.16
  227.9 0.8 copy-done.6
  228.9 0.8 fusion.35
  229.8 0.6 fusion.17
  230.6 1.1 copy-done.3
  231.7 0.2 multiply_reduce_fusion.10
  231.9 0.4 multiply_reduce_fusion.8
  232.4 0.3 fusion.11
  233.0 0.8 copy-done.10
  233.8 2.9 convolution_convert_fusion
  236.7 0.6 reduce_sum.256
  237.3 0.9 fusion.2
  238.2 2.0 select_maximum_fusion
  240.2 4.2 %fusion.10 = (f32[1152]{0:T(1024)S(1)}, f32[256]{0:T(256)}, f32[256,1152]{1,0:T(8,128)S(1)}) fusion(f32[256]{0:T(256)S(1)} %fusion.28, bf16[1,256,1152]{2,1,0:T(8,128)(2,1)S(1)} %copy-done.4, f32[1152]{0:T(1024)S(1)} %get-tuple-element.93, bf16[256,1536]{1,0:T(8,128)(2,1)} %copy-done.11, bf16[1152,1536]{1,0:T(8,128)(2,1)} %get-tuple-element.64), kind=kOutput, calls=%fused_computation.25 | convolution fusion | flops 908032640 | bytes 6106112 | tf_op jit(solution)/shard_map/dot_general | solution.py:1236
  245.1 0.6 pad.74
  245.7 62.1 %sum_weights.1 = (bf16[72,1792]{1,0:T(8,128)(2,1)}, f32[8,128]{1,0:T(8,128)}, bf16[54,1152]{1,0:T(8,128)(2,1)}, bf16[72,768]{1,0:T(8,128)(2,1)}, bf16[64,640]{1,0:T(8,128)(2,1)}) custom-call(bf16[4,4,72,1792]{3,2,1,0:T(8,128)(2,1)} %bitcast.106, f32[4,4,8,128]{3,2,1,0:T(8,128)} %bitcast.116, bf16[4,4,54,1152]{3,2,1,0:T(8,128)(2,1)} %bitcast.111, ...), custom_call_target="tpu_custom_call" | custom-call | tf_op jit(solution)/shard_map/sum_weights/pallas_call | solution.py:161
  307.8 1.8 reshape.287.refs_1_
  309.7 1.6 reshape.288.refs_2_
  311.3 14.6 %exchange_grads.1 = (f32[8,8,128]{2,1,0:T(8,128)}, bf16[8,9,1792]{2,1,0:T(8,128)(2,1)}, bf16[8,9,768]{2,1,0:T(8,128)(2,1)}, bf16[8,8,640]{2,1,0:T(8,128)(2,1)}) custom-call(f32[8,128]{1,0:T(8,128)} %get-tuple-element.71.refs_0_, bf16[8,9,1792]{2,1,0:T(8,128)(2,1)} %reshape.287.refs_1_, bf16[8,9,768]{2,1,0:T(8,128)(2,1)} %reshape.288.refs_2_, ...), custom_call_target="tpu_custom_call" | custom-call | tf_op jit(solution)/shard_map/exchange_grads/pallas_call | solution.py:161
  325.9 1.8 fusion.33
  327.7 0.5 reshape.290
  328.4 1.2 reshape.296
  329.6 1.0 copy.67
  330.5 0.5 reshape.291
  331.3 1.2 reshape.297
  332.4 0.9 convert_reduce_fusion.1
  333.4 0.6 pad_maximum_fusion.7
  334.0 1.0 convert_reduce_fusion
  335.0 0.6 pad_maximum_fusion.5
  335.7 0.6 fusion.34
  336.3 0.8 reduce_sum.257
  337.1 0.5 slice_bitcast_fusion.7
  337.7 0.5 slice_bitcast_fusion.4
  338.2 0.5 sqrt_bitcast_fusion
  338.8 0.7 convert_element_type.125
  339.5 1.2 fusion.13
  340.7 0.8 copy.89
  (116 shorter events, 2.8 us)
Async XLA Ops:
  0.6 2.1 copy-start.15
  3.6 1.3 copy-start.17
  3.6 1.3 copy-start.18
  3.7 1.3 copy-start.19
  3.7 1.9 copy-start.25
  3.7 1.9 copy-start.26
  3.7 1.9 copy-start.27
  3.8 1.9 copy-start.28
  3.8 1.9 copy-start.29
  3.8 2.0 copy-start.30
  92.7 105.2 %copy-start.1 = (f32[256,1152]{1,0:T(8,128)S(1)}, f32[256,1152]{1,0:T(8,128)}, u32[]{:S(2)}) copy-start(f32[256,1152]{1,0:T(8,128)} %get-tuple-element.51.hidden_in) | copy-start | bytes 3538948
  197.9 1.3 copy-start.2
  199.1 2.6 copy-start.5
  199.1 2.6 copy-start.7
  202.6 1.0 copy-start.14
  203.6 2.3 copy-start.23
  205.9 1.9 copy-start
  207.8 1.1 copy-start.12
  209.7 1.0 copy-start.24
  226.6 1.2 copy-start.9
  226.6 1.2 copy-start.8
  227.8 1.0 copy-start.6
  230.5 1.2 copy-start.3
  232.7 1.1 copy-start.10
  233.0 3.7 %copy-start.11 = (bf16[256,1536]{1,0:T(8,128)(2,1)}, bf16[256,1536]{1,0:T(8,128)(2,1)S(1)}, u32[]{:S(2)}) copy-start(bf16[256,1536]{1,0:T(8,128)(2,1)S(1)} %fusion.22) | copy-start | bytes 2359300
  233.8 2.9 copy-start.21
  233.8 3.5 %copy-start.4 = (bf16[1,256,1152]{2,1,0:T(8,128)(2,1)S(1)}, bf16[1,256,1152]{2,1,0:T(8,128)(2,1)}, u32[]{:S(2)}) copy-start(bf16[1,256,1152]{2,1,0:T(8,128)(2,1)} %param.16) | copy-start | bytes 1769476
  240.2 4.6 %copy-start.20 = (f32[1,1152]{1,0:T(1,128)S(1)}, f32[1,1152]{1,0:T(1,128)}, u32[]{:S(2)}) copy-start(f32[1,1152]{1,0:T(1,128)} %get-tuple-element.66) | copy-start | bytes 13828
  332.4 6.3 %copy-start.16 = (bf16[54,1152]{1,0:T(8,128)(2,1)S(1)}, bf16[54,1152]{1,0:T(8,128)(2,1)}, u32[]{:S(2)}) copy-start(bf16[54,1152]{1,0:T(8,128)(2,1)} %get-tuple-element.79) | copy-start | bytes 373252
  332.4 7.0 %copy-start.22 = (f32[256]{0:T(256)S(1)}, f32[256]{0:T(256)}, u32[]{:S(2)}) copy-start(f32[256]{0:T(256)} %get-tuple-element.87) | copy-start | bytes 3076
  339.5 1.2 copy-start.13

commit v4 on v3

--- a/solution.py
+++ b/solution.py
@@ -1,5 +1,6 @@
 import functools
 import math
+from types import SimpleNamespace
 
 import jax
 import jax.numpy as jnp
@@ -167,379 +168,17 @@
         scratch_shapes=scratch,
         input_output_aliases=aliases or {},
         compiler_params=pltpu.CompilerParams(
-            collective_id=number, has_side_effects=True, vmem_limit_bytes=56 * MIB
+            collective_id=number, has_side_effects=True, vmem_limit_bytes=60 * MIB
         ),
     )(*ins)
 
 
 SHARD_STEPS = [(dy, dc) for dy in range(4) for dc in range(2) if dy or dc]
-
-
-def exchange_shard(name, number, shared, spread):
-    n_shared, n = len(shared), len(shared) + len(spread)
-
-    def kernel(*refs):
-        ins, outs, (send, recv, here) = refs[:n], refs[n : 2 * n], refs[2 * n :]
-        x, y, z, c = place()
-        mine = y * 2 + c
-        sems = Sems(send, recv)
-        greet([device(x, y + dy, z, (c + dc) % 2) for dy, dc in SHARD_STEPS])
-        pushes = []
-        for dy, dc in SHARD_STEPS:
-            to_y, to_c = (y + dy) % 4, (c + dc) % 2
-            from_y, from_c = (y + 4 - dy) % 4, (c + 2 - dc) % 2
-            for at in range(n):
-                src = ins[at] if at < n_shared else ins[at].at[to_y * 2 + to_c]
-                push = Push(
-                    src, outs[at].at[mine], sems, device(x, to_y, z, to_c), outs[at].at[from_y * 2 + from_c]
-                )
-                push.start()
-                pushes.append(push)
-        own = []
-        for at in range(n):
-            src = ins[at] if at < n_shared else ins[at].at[mine]
-            own.append(pltpu.make_async_copy(src, outs[at].at[mine], here.at[at]))
-            own[-1].start()
-        for copy in own:
-            copy.wait()
-        for push in pushes:
-            push.arrived()
-            push.sent()
-
-    outs = [((8,) + a.shape, a.dtype) for a in shared] + [(a.shape, a.dtype) for a in spread]
-    return call(kernel, name, number, outs, list(shared) + list(spread), [], 7 * n, local=n)
 
 
 def lane_halves(width):
     low = width // 256 * 128 if width % 256 == 0 else (width // 128 + 1) // 2 * 128
     return ((0, low), (low, width - low)) if width > 128 else ((0, width), None)
-
-
-def gather_seq(name, number, z_first, x_first, shared):
-    ins = list(z_first) + list(x_first) + list(shared)
-    n = len(ins)
-    copies = 8 * n + 4 * len(shared)
-
-    def kernel(*refs):
-        sources, outs, (send, recv, here) = refs[:n], refs[n : 2 * n], refs[2 * n :]
-        x, y, z, c = place()
-        sems = Sems(send, recv)
-        greet(
-            [device(x, y, z + 1, c), device(x, y, z + 3, c), device(x + 1, y, z, c), device(x + 3, y, z, c)]
-            + ([device(x, y, z, 1 - c)] if shared else [])
-        )
-
-        def z_peer(k):
-            return device(x, y, k, c)
-
-        def x_peer(k):
-            return device(k, y, z, c)
-
-        jobs, own = [], []
-        for at in range(n):
-            source, out = sources[at], outs[at]
-            rows, width = source.shape
-            is_shared, by_rows = at >= len(z_first) + len(x_first), rows % 32 == 0
-            part = lambda ref: ref
-            if is_shared and by_rows:
-                share = pl.ds(pl.multiple_of(c * (rows // 2), 16), rows // 2)
-                part = lambda ref, share=share: ref.at[(slice(None),) * (len(ref.shape) - 2) + (share,)]
-            elif is_shared:
-                width //= 2
-                share = pl.ds(pl.multiple_of(c * width, 128), width)
-                part = lambda ref, share=share: ref.at[(slice(None),) * (len(ref.shape) - 1) + (share,)]
-            halves = lane_halves(width)
-
-            def lanes(ref, h, halves=halves, part=part):
-                return None if halves[h] is None else part(ref).at[:, pl.ds(*halves[h])]
-
-            mine = part(source)
-            own.append(pltpu.make_async_copy(mine, part(out.at[x, z]), here.at[at]))
-            own[-1].start()
-            if at < len(z_first):
-                one = RingGather(
-                    mine,
-                    lambda k, out=out, part=part: part(out.at[x, k]),
-                    lambda k, h, out=out, lanes=lanes: lanes(out.at[x, k], h),
-                    z, z_peer, sems,
-                )
-                two = RingGather(
-                    part(out.at[x]),
-                    lambda k, out=out, part=part: part(out.at[k]),
-                    lambda k, h, out=out, part=part: part(out.at[k, pl.ds(2 * h, 2)]),
-                    x, x_peer, sems,
-                )
-                piece = lambda k, out=out, part=part: part(out.at[k])
-                me = x
-            else:
-                one = RingGather(
-                    mine,
-                    lambda k, out=out, part=part: part(out.at[k, z]),
-                    lambda k, h, out=out, lanes=lanes: lanes(out.at[k, z], h),
-                    x, x_peer, sems,
-                )
-                two = RingGather(
-                    part(out.at[:, z]),
-                    lambda k, out=out, part=part: part(out.at[:, k]),
-                    lambda k, h, out=out, part=part: part(out.at[pl.ds(2 * h, 2), k]),
-                    z, z_peer, sems,
-                )
-                piece = lambda k, out=out, part=part: part(out.at[:, k])
-                me = z
-            crossings = []
-            if is_shared:
-                half = rows // 2 if by_rows else width
-                theirs = pl.ds(pl.multiple_of((1 - c) * half, 16 if by_rows else 128), half)
-                for k in (me, (me + 3) % 4, (me + 1) % 4, (me + 2) % 4):
-                    lands = out.at[:, k, theirs] if by_rows else out.at[:, k, :, theirs]
-                    crossings.append(Push(piece(k), piece(k), sems, device(x, y, z, 1 - c), lands))
-            jobs.append((one, two, crossings))
-        for one, _, _ in jobs:
-            one.first()
-        for one, _, _ in jobs:
-            one.relay()
-        for copy in own:
-            copy.wait()
-        for one, two, crossings in jobs:
-            one.last()
-            two.first()
-            if crossings:
-                crossings[0].start()
-        for _, two, crossings in jobs:
-            two.relay()
-            if crossings:
-                crossings[1].start()
-                crossings[2].start()
-        for one, two, crossings in jobs:
-            two.last()
-            if crossings:
-                crossings[3].start()
-        for one, two, crossings in jobs:
-            for push in crossings:
-                push.arrived()
-                push.sent()
-            one.close()
-            two.close()
-
-    outs = [((4, 4) + a.shape, a.dtype) for a in ins]
-    return call(kernel, name, number, outs, ins, [], copies, local=n)
-
-
-def halo(name, number, steps, value):
-    def kernel(src, out, send, recv):
-        q, s = lax.axis_index("seq"), lax.axis_index("shard")
-        sems = Sems(send, recv)
-        there = [{"seq": (q + 16 + d) % 16, "shard": s} for d in steps]
-        back = [{"seq": (q + 16 - d) % 16, "shard": s} for d in steps]
-        greet(there + back)
-        pushes = []
-        for at in range(len(steps)):
-            piece = src if len(src.shape) == 2 else src.at[at]
-            pushes.append(Push(piece, out.at[at], sems, there[at]))
-            pushes[-1].start()
-        for push in pushes:
-            push.arrived()
-            push.sent()
-
-    shape = (len(steps),) + value.shape[-2:]
-    return call(kernel, name, number, [(shape, value.dtype)], [value], [], len(steps))[0]
-
-
-def gather_tokens(name, number, value):
-    rows, width = value.shape
-
-    def kernel(src, out, send, recv, here):
-        x, y, z, c = place()
-        sems = Sems(send, recv)
-        other = device(x, y, z, 1 - c)
-        greet([device(x, y + 1, z, c), device(x, y + 3, z, c), other])
-        slot = lambda k: out.at[k * 2 + c]
-        ring = RingGather(
-            src, slot, lambda k, h: out.at[k * 2 + c, pl.ds(h * (rows // 2), rows // 2)],
-            y, lambda k: device(x, k, z, c), sems,
-        )
-        there = lambda k: out.at[k * 2 + 1 - c]
-        cross = [
-            Push(src if i == 0 else slot((y + i) % 4), slot((y + i) % 4), sems, other, there((y + i) % 4))
-            for i in range(4)
-        ]
-        ring.first()
-        cross[0].start()
-        own = pltpu.make_async_copy(src, slot(y), here.at[0])
-        own.start()
-        ring.relay()
-        cross[3].start()
-        cross[1].start()
-        ring.last()
-        cross[2].start()
-        own.wait()
-        for push in cross:
-            push.arrived()
-            push.sent()
-        ring.close()
-
-    return call(kernel, name, number, [((8, rows, width), value.dtype)], [value], [], 8, local=1)[0]
-
-
-def sum_tokens(name, number, value):
-    _, rows, width = value.shape
-    half = rows // 2
-
-    def kernel(src, out, chunks, inbox, near_a, near_b, right, left, send, recv, here):
-        x, y, z, c = place()
-        sems = Sems(send, recv)
-        other = device(x, y, z, 1 - c)
-        greet([device(x, y + 1, z, c), device(x, y + 3, z, c), other])
-        order = [(y + 2) % 4, (y + 1) % 4, (y + 3) % 4, y]
-        cross = [Push(src.at[k * 2 + 1 - c], inbox.at[i], sems, other) for i, k in enumerate(order)]
-        for push in cross:
-            push.start()
-        loads = [pltpu.make_async_copy(src.at[k * 2 + c], chunks.at[i], here.at[i]) for i, k in enumerate(order)]
-        for load in loads:
-            load.start()
-        at = {2: 0, 1: 1, 3: 2, 0: 3}
-        to = lambda d: device(x, y + d, z, c)
-        far_a = Push(chunks.at[0, pl.ds(0, half)], near_a, sems, to(1))
-        far_b = Push(chunks.at[0, pl.ds(half, half)], near_b, sems, to(3))
-        go_right = Push(chunks.at[1], right, sems, to(1))
-        go_left = Push(chunks.at[2], left, sems, to(3))
-        for i in range(4):
-            loads[i].wait()
-            cross[i].arrived()
-            if i < 3:
-                add_into(chunks.at[i], inbox.at[i])
-            if i == 0:
-                far_a.start()
-                far_b.start()
-        far_a.arrived()
-        add_into(chunks.at[1, pl.ds(0, half)], near_a)
-        go_right.start()
-        far_b.arrived()
-        add_into(chunks.at[2, pl.ds(half, half)], near_b)
-        go_left.start()
-        out[...] = chunks[3].astype(jnp.float32) + inbox[3].astype(jnp.float32)
-        go_right.arrived()
-        out[...] += right[...].astype(jnp.float32)
-        go_left.arrived()
-        out[...] += left[...].astype(jnp.float32)
-        for push in cross + [far_a, far_b, go_right, go_left]:
-            push.sent()
-
-    kind = value.dtype
-    scratch = [
-        pltpu.VMEM((4, rows, width), kind),
-        pltpu.VMEM((4, rows, width), kind),
-        pltpu.VMEM((half, width), kind),
-        pltpu.VMEM((half, width), kind),
-        pltpu.VMEM((rows, width), kind),
-        pltpu.VMEM((rows, width), kind),
-    ]
-    return call(
-        kernel, name, number, [((rows, width), jnp.float32)], [value], scratch, 8, out_specs=[VMEM], local=4
-    )[0]
-
-
-def sum_seq(name, number, z_first, x_first, shared):
-    ins = list(z_first) + list(x_first) + [a for a, _, _ in shared]
-    n, plain = len(ins), len(z_first) + len(x_first)
-    shapes = [a.shape for a in z_first + x_first] + [a.shape[:3] + (size,) for a, _, size in shared]
-    kinds = [a.dtype for a in ins]
-    copies = 8 * n + len(shared)
-
-    def boxes(shape, kind, first_axis):
-        rows, width = shape[2:]
-        lanes = lane_halves(width)
-        out = [pltpu.VMEM((2, rows, width), kind)] * 2 + [pltpu.VMEM((4, rows, width), kind)] * 2
-        out += [pltpu.VMEM((rows, lanes[0][1]), kind)]
-        out += [pltpu.VMEM((rows, (lanes[1] or lanes[0])[1]), kind)]
-        out += [pltpu.VMEM((rows, width), kind)] * 2
-        return out
-
-    scratch = []
-    for at in range(n):
-        scratch.append(pltpu.VMEM(shapes[at], kinds[at]))
-        scratch += boxes(shapes[at], kinds[at], 0)
-    for at in range(plain, n):
-        scratch.append(pltpu.VMEM(shapes[at], kinds[at]))
-
-    def kernel(*refs):
-        sources, outs = refs[:n], refs[n : 2 * n]
-        room = refs[2 * n : 2 * n + 9 * n]
-        extra = refs[11 * n : 11 * n + len(shared)]
-        send, recv, here = refs[11 * n + len(shared) :]
-        x, y, z, c = place()
-        sems = Sems(send, recv)
-        greet(
-            [device(x, y, z + 1, c), device(x, y, z + 3, c), device(x + 1, y, z, c), device(x + 3, y, z, c)]
-            + ([device(x, y, z, 1 - c)] if shared else [])
-        )
-        z_peer = lambda k: device(x, y, k, c)
-        x_peer = lambda k: device(k, y, z, c)
-        loads, cross, jobs = [], [], []
-        for at in range(n):
-            total = room[9 * at]
-            source = sources[at]
-            if at >= plain:
-                _, step, size = shared[at - plain]
-                theirs = source.at[:, :, :, pl.ds(pl.multiple_of((1 - c) * step, 128), size)]
-                cross.append(Push(theirs, extra[at - plain], sems, device(x, y, z, 1 - c)))
-                cross[-1].start()
-                source = source.at[:, :, :, pl.ds(pl.multiple_of(c * step, 128), size)]
-            loads.append(pltpu.make_async_copy(source, total, here.at[at]))
-            loads[-1].start()
-            halves = lane_halves(shapes[at][3])
-
-            def lanes(ref, h, halves=halves):
-                return None if halves[h] is None else ref.at[:, pl.ds(*halves[h])]
-
-            inbox1, inbox2 = room[9 * at + 1 : 9 * at + 5], room[9 * at + 5 : 9 * at + 9]
-            if at < len(z_first):
-                one = RingSum(
-                    lambda k, t=total: t.at[:, k],
-                    lambda k, h, t=total: t.at[pl.ds(2 * h, 2), k],
-                    inbox1, z, z_peer, sems, add_into,
-                )
-                two = RingSum(
-                    lambda k, t=total: t.at[k, z],
-                    lambda k, h, t=total, lanes=lanes: lanes(t.at[k, z], h),
-                    inbox2, x, x_peer, sems, add_into,
-                )
-            else:
-                one = RingSum(
-                    lambda k, t=total: t.at[k],
-                    lambda k, h, t=total: t.at[k, pl.ds(2 * h, 2)],
-                    inbox1, x, x_peer, sems, add_into,
-                )
-                two = RingSum(
-                    lambda k, t=total: t.at[x, k],
-                    lambda k, h, t=total, lanes=lanes: lanes(t.at[x, k], h),
-                    inbox2, z, z_peer, sems, add_into,
-                )
-            jobs.append((one, two))
-        for at in range(n):
-            loads[at].wait()
-            if at >= plain:
-                cross[at - plain].arrived()
-                add_into(room[9 * at], extra[at - plain])
-            jobs[at][0].first()
-        for one, _ in jobs:
-            one.second()
-        for one, two in jobs:
-            one.third()
-            two.first()
-        for _, two in jobs:
-            two.second()
-        for at, (one, two) in enumerate(jobs):
-            two.third()
-            outs[at][...] = room[9 * at][x, z].astype(outs[at].dtype)
-        for one, two in jobs:
-            one.close()
-            two.close()
-        for push in cross:
-            push.sent()
-
-    outs = [(shape[2:], kind) for shape, kind in zip(shapes, kinds)]
-    return call(kernel, name, number, outs, ins, scratch, copies, out_specs=[VMEM] * n, local=n)
 
 
 def dot(a, b, contract_a, contract_b):
@@ -859,21 +498,12 @@
             sems.used = start
             self.variants.append(make(order))
 
-    def run(self, name):
-        for order in (0, 1):
-            pl.when(self.core == order)(getattr(self.variants[order], name))
-
-    def first(self):
-        self.run("first")
-
-    def relay(self):
-        self.run("relay")
-
-    def last(self):
-        self.run("last")
-
-    def close(self):
-        self.run("close")
+    def __getattr__(self, name):
+        def run():
+            for order in (0, 1):
+                pl.when(self.core == order)(getattr(self.variants[order], name))
+
+        return run
 
 
 def split_lanes(ref, h):
@@ -924,12 +554,12 @@
             self.pushes.append(Either(c, sems, make))
 
     def start(self, d):
-        self.pushes[d].run("start")
+        self.pushes[d].start()
 
     def close(self):
         for push in self.pushes:
-            push.run("arrived")
-            push.run("sent")
+            push.arrived()
+            push.sent()
 
 
 def turn(values, cosine, sine):
@@ -1216,37 +846,364 @@
     )
 
 
-def norm_rows(values, weight):
-    return values * lax.rsqrt(jnp.mean(values * values, axis=-1, keepdims=True) + EPSILON) * weight
-
-
-def head_prep(values, weight, cosine, sine):
-    return turn(norm_rows(values, weight), cosine, sine)
-
-
-def matmul(a, b):
-    return jnp.dot(a, b, preferred_element_type=jnp.float32)
-
-
-def matmul_tn(a, b):
-    return lax.dot_general(a, b, (((0,), (0,)), ((), ())), preferred_element_type=jnp.float32)
-
-
-def matmul_nt(a, b):
-    return lax.dot_general(a, b, (((1,), (1,)), ((), ())), preferred_element_type=jnp.float32)
-
-
-def heads_first(values):
-    return jnp.concatenate([values[:, h * HEAD_DIM : (h + 1) * HEAD_DIM] for h in range(HEADS)], axis=0)
-
-
-def heads_last(values):
-    rows = values.shape[0] // HEADS
-    return jnp.concatenate([values[h * rows : (h + 1) * rows] for h in range(HEADS)], axis=1)
-
-
-def pad_rows(values, rows):
-    return jnp.pad(values, ((0, rows - values.shape[0]), (0, 128 - values.shape[1])))
+def norm_grad(values, gain, grad):
+    unit, scale = unit_rows(values)
+    scaled = gain * grad
+    return (
+        scale * (scaled - unit * jnp.mean(unit * scaled, axis=-1, keepdims=True)),
+        jnp.sum(grad * unit, axis=0, keepdims=True),
+    )
+
+
+def scatter_rings(total, boxes, sems):
+    x, y, z, c = place()
+    z_peer, x_peer = (lambda k: device(x, y, k, c)), (lambda k: device(k, y, z, c))
+
+    def one(order):
+        if order == 0:
+            chunk, half = lambda k: total.at[:, k], lambda k, h: total.at[pl.ds(2 * h, 2), k]
+        else:
+            chunk, half = lambda k: total.at[k], lambda k, h: total.at[k, pl.ds(2 * h, 2)]
+        return RingSum(chunk, half, boxes[:4], (z, x)[order], (z_peer, x_peer)[order], sems, add_into)
+
+    def two(order):
+        chunk = (lambda k: total.at[k, z]) if order == 0 else (lambda k: total.at[x, k])
+        half = lambda k, h: split_lanes(chunk(k), h)
+        return RingSum(chunk, half, boxes[4:], (x, z)[order], (x_peer, z_peer)[order], sems, add_into)
+
+    return Either(c, sems, one), Either(c, sems, two)
+
+
+def scatter_boxes(rows, width, kind):
+    lanes = lane_halves(width)
+    return (
+        [pltpu.VMEM((4, 4, rows, width), kind)]
+        + [pltpu.VMEM((2, rows, width), kind)] * 2
+        + [pltpu.VMEM((4, rows, width), kind)] * 2
+        + [pltpu.VMEM((rows, size), kind) for _, size in lanes]
+        + [pltpu.VMEM((rows, width), kind)] * 2
+    )
+
+
+BOTH, DOWN, OUTPUT, QUERY, KV = range(5)
+SHARED = (OUTPUT, QUERY, KV)
+GIVE, TAKE = 9, 10
+
+
+def attend_back(number, arrays):
+    tokens = arrays["hidden"].shape[0]
+    span = tokens + WINDOW
+    names = list(arrays)
+    low, wide = jnp.bfloat16, jnp.float32
+    results = dict(
+        stream_grad=((tokens, D), low),
+        both_rows=((8, 126, 128), low),
+        query_grad=((9, 1024), wide),
+        key_grad=((9, 256), wide),
+        value_grad=((9, 256), wide),
+        output_grad=((8, D), wide),
+        down_grad=((PIECE, D), wide),
+        sums=((8, D), wide),
+    )
+    sizes = {BOTH: (72, 2 * WIDE), DOWN: (PIECE, D), OUTPUT: (64, 640), QUERY: (72, 512), KV: (72, 256)}
+    stores = []
+    for name, (rows, width) in sizes.items():
+        stores.append(scatter_boxes(rows, width, low))
+        if name in SHARED:
+            stores[-1] += [pltpu.VMEM((4, 4, rows, width), low)] * 2
+    room = SimpleNamespace(
+        hidden_grad=pltpu.VMEM((tokens, D), wide),
+        branch_low=pltpu.VMEM((tokens, D), low),
+        mixed_grad=pltpu.VMEM((HEADS * tokens, HEAD_DIM), low),
+        score_low=pltpu.VMEM((HEADS * tokens, span), low),
+        probs_low=pltpu.VMEM((HEADS * tokens, span), low),
+        kv_grad=pltpu.VMEM((span, 2 * HEAD_DIM), wide),
+        halo_out=pltpu.VMEM((2, tokens, 2 * HEAD_DIM), low),
+        halo_in=pltpu.VMEM((2, tokens, 2 * HEAD_DIM), low),
+        qkv_low=pltpu.VMEM((tokens, 1536), low),
+        term=pltpu.VMEM((D, 1024), wide),
+        merge=pltpu.VMEM((72, 2 * WIDE), wide),
+        flat=pltpu.VMEM((128, 128), wide),
+        both_give=pltpu.VMEM((8, 126, 128), low),
+        query_give=pltpu.VMEM((8, 36, 128), low),
+        query_take=pltpu.VMEM((8, 36, 128), low),
+        kv_give=pltpu.VMEM((8, 18, 128), low),
+        kv_take=pltpu.VMEM((8, 18, 128), low),
+        output_give=pltpu.VMEM((8, 8, 640), low),
+        output_take=pltpu.VMEM((8, 8, 640), low),
+        own_sums=pltpu.VMEM((3, 8, D), wide),
+        shard_sums=pltpu.VMEM((8, 8, D), wide),
+        z_sums=pltpu.VMEM((4, 8, D), wide),
+        x_sums=pltpu.VMEM((4, 8, D), wide),
+    )
+    room = vars(room)
+
+    def kernel(*refs):
+        refs = list(refs)
+
+        def take(count):
+            taken, refs[:] = refs[:count], refs[count:]
+            return taken
+
+        a = SimpleNamespace(**dict(zip(names, take(len(names)))))
+        o = SimpleNamespace(**dict(zip(results, take(len(results)))))
+        b = SimpleNamespace(**dict(zip(room, take(len(room)))))
+        held = {n: take(len(store)) for n, store in zip(sizes, stores)}
+        send, recv, here = refs
+        x, y, z, c = place()
+        q, s = lax.axis_index("seq"), lax.axis_index("shard")
+        sems = Sems(send, recv)
+        other = device(x, y, z, 1 - c)
+        after, before = {"seq": (q + 1) % 16, "shard": s}, {"seq": (q + 15) % 16, "shard": s}
+        greet(
+            [device(x, y + dy, z, (c + dc) % 2) for dy, dc in SHARD_STEPS]
+            + [device(x, y, z + d, c) for d in (1, 2, 3)]
+            + [device(x + d, y, z, c) for d in (1, 2, 3)]
+            + [after, before]
+        )
+        rings = {n: scatter_rings(held[n][0], held[n][1:9], sems) for n in sizes}
+        cross = {n: Push(held[n][GIVE], held[n][TAKE], sems, other) for n in SHARED}
+        loads = [
+            pltpu.make_async_copy(a.both_term, held[BOTH][0], here.at[0]),
+            pltpu.make_async_copy(a.down_term, held[DOWN][0], here.at[1]),
+        ]
+        for load in loads:
+            load.start()
+        gains = a.gains
+        cosine, sine = a.cosine, a.sine
+        own = b.own_sums.at[0]
+        own[...] = jnp.zeros(own.shape, wide)
+        pending = []
+
+        upstream = a.cotangent[...].astype(wide)
+        extra, own[2:3, :] = norm_grad(a.hidden[...], gains[2:3, :], a.feed_grad[...])
+        hidden_grad = upstream + extra
+        b.hidden_grad[...] = hidden_grad
+        branch_grad, own[1:2, :] = norm_grad(a.branch[...], gains[1:2, :], hidden_grad)
+        b.branch_low[...] = branch_grad.astype(low)
+        own[3:4, :] = a.post_grad[...]
+        for at, squares in enumerate((
+            jnp.sum(jnp.square(a.stream[...].astype(wide)), axis=0, keepdims=True),
+            jnp.sum(jnp.square(a.hidden[...]), axis=0, keepdims=True),
+            a.result_squares[...],
+        )):
+            folded = functools.reduce(jnp.add, [squares[:, 128 * j : 128 * (j + 1)] for j in range(D // 128)])
+            own[4:5, 512 + 128 * at : 640 + 128 * at] = folded
+        for n, load in zip((BOTH, DOWN), loads):
+            load.wait()
+            rings[n][0].first()
+        for h in range(HEADS):
+            rows, lanes = slice(h * tokens, (h + 1) * tokens), slice(h * HEAD_DIM, (h + 1) * HEAD_DIM)
+            b.mixed_grad[rows, :] = dot(b.branch_low[...], a.output_weight[lanes, :], 1, 1).astype(low)
+        keys, values = a.kv[:, :HEAD_DIM], a.kv[:, HEAD_DIM:]
+        for h in range(HEADS):
+            rows = slice(h * tokens, (h + 1) * tokens)
+            probs = a.probs[rows, :]
+            prob_grad = dot(b.mixed_grad[rows, :], values, 1, 1)
+            inner = jnp.sum(probs * prob_grad, axis=-1, keepdims=True)
+            b.score_low[rows, :] = (probs * (prob_grad - inner) * HEAD_DIM ** (-0.5)).astype(low)
+            b.probs_low[rows, :] = probs.astype(low)
+        b.kv_grad[:, :HEAD_DIM] = dot(b.score_low[...], a.turned[...], 0, 0)
+        b.kv_grad[:, HEAD_DIM:] = dot(b.probs_low[...], b.mixed_grad[...], 0, 0)
+
+        halo_far = Push(b.halo_out.at[0], b.halo_in.at[0], sems, before)
+        halo_near = Push(b.halo_out.at[1], b.halo_in.at[1], sems, before)
+        b.halo_out[0] = b.kv_grad[:tokens, :].astype(low)
+        halo_far.start()
+
+        gain_grad = jnp.zeros((1, HEAD_DIM), wide)
+        for h in range(HEADS):
+            rows, lanes = slice(h * tokens, (h + 1) * tokens), slice(h * HEAD_DIM, (h + 1) * HEAD_DIM)
+            turned_grad = dot(b.score_low[rows, :], keys, 1, 0)
+            back = turn(turned_grad, cosine[...], -sine[...])
+            grad, extra = norm_grad(a.query[rows, :], gains[4:5, :HEAD_DIM], back)
+            gain_grad += extra
+            b.qkv_low[:, lanes] = grad.astype(low)
+        own[4:5, :HEAD_DIM] = gain_grad
+
+        def term(start, width, give, take):
+            out = b.term
+
+            @pl.loop(0, D // 128)
+            def _(i):
+                lanes = pl.ds(pl.multiple_of(i * 128, 128), 128)
+                out[lanes, : 2 * width] = dot(a.normed[:, lanes], b.qkv_low[:, start : start + 2 * width], 0, 0)
+
+            @pl.loop(0, 16)
+            def _(i):
+                rows = pl.ds(pl.multiple_of(72 * i, 8), 72)
+                for ref, core in ((take, c), (give, 1 - c)):
+                    lanes = pl.ds(pl.multiple_of(core * width, 128), width)
+                    ref[i // 4, i % 4] = out[rows, lanes].astype(low)
+
+        term(0, 512, held[QUERY][GIVE], held[QUERY][0])
+        cross[QUERY].start()
+
+        @pl.loop(0, 8)
+        def _(i):
+            lanes = pl.ds(pl.multiple_of(i * 128, 128), 128)
+            part = dot(a.mixed[:, lanes], b.branch_low[...], 0, 0).astype(low)
+            for k in range(2):
+                block = (2 * i + k) // 4, (2 * i + k) % 4
+                for core in range(2):
+                    lanes_out = slice(512 * core, 512 * core + 640)
+                    value = part[64 * k : 64 * (k + 1), lanes_out]
+
+                    @pl.when(c == core)
+                    def _():
+                        held[OUTPUT][0][block] = value
+
+                    @pl.when(c != core)
+                    def _():
+                        held[OUTPUT][GIVE][block] = value
+
+        cross[OUTPUT].start()
+        halo_far.arrived()
+        b.halo_out[1] = (b.kv_grad[tokens : 2 * tokens, :] + b.halo_in[0].astype(wide)).astype(low)
+        halo_near.start()
+        for n in (BOTH, DOWN):
+            rings[n][0].second()
+        for n in (QUERY, OUTPUT):
+            cross[n].arrived()
+            add_into(held[n][0], held[n][TAKE])
+            rings[n][0].first()
+        for n in (BOTH, DOWN):
+            rings[n][0].third()
+            rings[n][1].first()
+        halo_near.arrived()
+        kv_grad = b.kv_grad[2 * tokens :, :] + b.halo_in[1].astype(wide)
+        back = turn(kv_grad[:, :HEAD_DIM], cosine[...], -sine[...])
+        grad, own[4:5, HEAD_DIM : 2 * HEAD_DIM] = norm_grad(a.key[...], gains[5:6, :HEAD_DIM], back)
+        b.qkv_low[:, 1024:1280] = grad.astype(low)
+        b.qkv_low[:, 1280:] = kv_grad[:, HEAD_DIM:].astype(low)
+        term(1024, 256, held[KV][GIVE], held[KV][0])
+        cross[KV].start()
+        for n in (QUERY, OUTPUT):
+            rings[n][0].second()
+        cross[KV].arrived()
+        add_into(held[KV][0], held[KV][TAKE])
+        rings[KV][0].first()
+        normed_grad = dot(b.qkv_low[...], a.qkv_weight[...], 1, 1)
+        extra, own[0:1, :] = norm_grad(a.stream[...].astype(wide), gains[0:1, :], normed_grad)
+        o.stream_grad[...] = (b.hidden_grad[...] + extra).astype(low)
+
+        def all_sum(stage, box, me, steps, target):
+            source = b.own_sums.at[stage]
+            pushes = []
+            for to, back in steps:
+                push = Push(source, box.at[me], sems, target(to), box.at[back])
+                push.start()
+                pushes.append(push)
+            pending.extend(pushes)
+            box[me] = source[...]
+
+            def finish():
+                for push in pushes:
+                    push.arrived()
+                return functools.reduce(jnp.add, [box[k] for k in range(box.shape[0])])
+
+            return finish
+
+        steps = []
+        for dy, dc in SHARD_STEPS:
+            there = (y + dy) % 4, (c + dc) % 2
+            steps.append((there, (y + 4 - dy) % 4 * 2 + (c + 2 - dc) % 2))
+        finish = all_sum(0, b.shard_sums, s, steps, lambda t: device(x, t[0], z, t[1]))
+        for n in (BOTH, DOWN):
+            rings[n][1].second()
+        for n in (QUERY, OUTPUT):
+            rings[n][0].third()
+            rings[n][1].first()
+        b.own_sums[1] = finish()
+        turns = lambda at: [((at + d) % 4, (at + 4 - d) % 4) for d in (1, 2, 3)]
+        finish = all_sum(1, b.z_sums, z, turns(z), lambda t: device(x, y, t, c))
+        rings[KV][0].second()
+
+        def spread(source, box):
+            pushes = []
+            for dy, dc in SHARD_STEPS:
+                to, back = (y + dy) % 4 * 2 + (c + dc) % 2, (y + 4 - dy) % 4 * 2 + (c + 2 - dc) % 2
+                push = Push(source.at[to], box.at[s], sems, device(x, y + dy, z, (c + dc) % 2), box.at[back])
+                push.start()
+                pushes.append(push)
+            box[s] = source[s]
+            pending.extend(pushes)
+            return pushes
+
+        def flatten(block, give):
+            width = block.shape[-1]
+            tiles = width // 128
+            merge, flat = b.merge, b.flat
+            merge[:, :width] = block[...].astype(wide)
+            for d in range(8):
+                for j in range(tiles):
+                    flat[pl.ds(j, 9, tiles), :] = merge[9 * d : 9 * d + 9, 128 * j : 128 * (j + 1)]
+                give[d] = flat[: 9 * tiles, :].astype(low)
+
+        def unflatten(value, tiles, write):
+            b.flat[: 9 * tiles, :] = value
+            for j in range(tiles):
+                write(j, b.flat[pl.ds(j, 9, tiles), :])
+
+        for n in (BOTH, DOWN):
+            rings[n][1].third()
+        flatten(held[BOTH][0].at[x, z], b.both_give)
+        got_both = spread(b.both_give, o.both_rows)
+        o.down_grad[...] = held[DOWN][0][x, z].astype(wide)
+        b.own_sums[2] = finish()
+        finish = all_sum(2, b.x_sums, x, turns(x), lambda t: device(t, y, z, c))
+        rings[KV][0].third()
+        rings[KV][1].first()
+        for n in (QUERY, OUTPUT):
+            rings[n][1].second()
+        rings[KV][1].second()
+        for n in (QUERY, OUTPUT):
+            rings[n][1].third()
+        flatten(held[QUERY][0].at[x, z], b.query_give)
+        got_query = spread(b.query_give, b.query_take)
+        for d in range(8):
+            b.output_give[d] = held[OUTPUT][0][x, z, 8 * d : 8 * d + 8, :]
+        got_output = spread(b.output_give, b.output_take)
+        rings[KV][1].third()
+        flatten(held[KV][0].at[x, z], b.kv_give)
+        got_kv = spread(b.kv_give, b.kv_take)
+        o.sums[...] = finish()
+
+        def over_y(box, core):
+            return functools.reduce(jnp.add, [box[2 * k + core].astype(wide) for k in range(4)])
+
+        for push in got_query:
+            push.arrived()
+        for core in range(2):
+            def write(j, value, core=core):
+                o.query_grad[:, 512 * core + 128 * j : 512 * core + 128 * (j + 1)] = value
+
+            unflatten(over_y(b.query_take, core), 4, write)
+        for push in got_output:
+            push.arrived()
+        o.output_grad[:, :512] = over_y(b.output_take, 0)[:, :512]
+        o.output_grad[:, 512:] = over_y(b.output_take, 1)
+        for push in got_kv:
+            push.arrived()
+        for core, out in enumerate((o.key_grad, o.value_grad)):
+            def write(j, value, out=out):
+                out[:, 128 * j : 128 * (j + 1)] = value
+
+            unflatten(over_y(b.kv_take, core), 2, write)
+        for push in got_both:
+            push.arrived()
+        for pair in rings.values():
+            for ring in pair:
+                ring.close()
+        for push in list(cross.values()) + pending + [halo_far, halo_near]:
+            push.sent()
+
+    ins = list(arrays.values())
+    out = call(
+        kernel, "attend_back", number, list(results.values()), ins, list(room.values()) + sum(stores, []), 5 * 8 + 3 + 2 + 13 + 28,
+        in_specs=[VMEM] * (len(ins) - 2) + [ANY] * 2, out_specs=[VMEM] * len(results), local=2,
+    )
+    return dict(zip(results, out))
 
 
 def split_hidden(weight):
@@ -1258,10 +1215,6 @@
     stream, doc_starts, cotangent, attention_norm, query_weight, key_weight, value_weight, query_norm, key_norm,
     output_weight, attention_post_norm, mlp_norm, gate_weight, up_weight, down_weight, mlp_post_norm,
 ):
-    tokens = stream.shape[1]
-    scale = HEAD_DIM ** (-0.5)
-    inputs = stream[0].astype(jnp.float32)
-    upstream = cotangent[0].astype(jnp.float32)
     own_qkv = jnp.concatenate([query_weight, key_weight, value_weight], axis=1)
     norms = (attention_norm, attention_post_norm, mlp_norm, mlp_post_norm, query_norm, key_norm)
     own_gains = jnp.concatenate([jnp.pad(g, (0, 16 - g.shape[0])) for g in norms] + [jnp.zeros((32,), jnp.bfloat16)])
@@ -1274,89 +1227,51 @@
         0, stream[0], doc_starts, own_qkv.reshape(108, 128), own_gains, output_weight, own_both.reshape(8, 126, 128),
         down_weight,
     )
-    gain_input, gain_post, gain_mlp, gain_mlp_post = (gain_rows[i] for i in range(4))
-    gain_query, gain_key = gain_rows[4, :HEAD_DIM], gain_rows[5, :HEAD_DIM]
-    keys_all, values_all = kv[:, :HEAD_DIM], kv[:, HEAD_DIM:]
-    probability_low = probability.astype(jnp.bfloat16)
     full_both = both16.reshape(D, 2 * WIDE)
     full_down = jnp.pad(down16.reshape(16, PIECE, D), ((0, 0), (0, SLOT - PIECE), (0, 0))).reshape(WIDE, D)
 
     block_output, feed_grad, gain_mlp_post_grad, result_squares, both_term, down_term = feed_forward(
-        "feed_forward", 2, feed, full_both, full_down, hidden, cotangent[0], gain_mlp_post[None]
+        "feed_forward", 1, feed, full_both, full_down, hidden, cotangent[0], gain_rows[3:4]
     )
 
-    hidden_extra, gain_mlp_grad = jax.vjp(norm_rows, hidden, gain_mlp)[1](feed_grad)
-    hidden_grad = upstream + hidden_extra
-    branch_grad, gain_post_grad = jax.vjp(norm_rows, branch, gain_post)[1](hidden_grad)
-    branch_low = branch_grad.astype(jnp.bfloat16)
-    output_term = matmul_tn(mixed, branch_low).astype(jnp.bfloat16)
-    mixed_grad = heads_first(matmul_nt(branch_low, full_output).astype(jnp.bfloat16))
-    prob_grad = matmul_nt(mixed_grad, values_all)
-    inner_sum = jnp.sum(probability * prob_grad, axis=-1, keepdims=True)
-    score_low = (probability * (prob_grad - inner_sum) * scale).astype(jnp.bfloat16)
-    query_grad_rot = matmul(score_low, keys_all)
-    key_grads = matmul_tn(score_low, query_rot)
-    value_grads = matmul_tn(probability_low, mixed_grad)
-    kv_grads = jnp.concatenate([key_grads, value_grads], axis=1)
-    returned = halo(
-        "halo_back", 3, (-2, -1), kv_grads[:WINDOW].astype(jnp.bfloat16).reshape(2, tokens, 2 * HEAD_DIM)
-    )
-    kv_own = kv_grads[WINDOW:] + returned[0].astype(jnp.float32) + returned[1].astype(jnp.float32)
-    query_grad, gain_query_grad = jax.vjp(lambda v, w: head_prep(v, w, jnp.concatenate([cosine] * HEADS), jnp.concatenate([sine] * HEADS)), query_proj, gain_query)[1](
-        query_grad_rot
-    )
-    key_grad, gain_key_grad = jax.vjp(lambda v, w: head_prep(v, w, cosine, sine), key_proj, gain_key)[1](
-        kv_own[:, :HEAD_DIM]
-    )
-    qkv_low = jnp.concatenate([heads_last(query_grad), key_grad, kv_own[:, HEAD_DIM:]], axis=1).astype(jnp.bfloat16)
-    qkv_term = matmul_tn(normed, qkv_low).astype(jnp.bfloat16)
-    normed_grad = matmul_nt(qkv_low, full_qkv)
-    input_extra, gain_input_grad = jax.vjp(norm_rows, inputs, gain_input)[1](normed_grad)
-    stream_grad = (hidden_grad + input_extra).astype(jnp.bfloat16)
-
-    squares = jnp.stack([jnp.sum(inputs * inputs), jnp.sum(hidden * hidden), jnp.sum(result_squares)])
-    small = [g.reshape(16, 72) for g in (gain_input_grad, gain_post_grad, gain_mlp_grad, gain_mlp_post_grad)]
-    small += [jnp.pad(g.reshape(16, 16), ((0, 0), (0, 56))) for g in (gain_query_grad, gain_key_grad)]
-    small.append(jnp.pad(jnp.broadcast_to(squares[None], (16, 3)), ((0, 0), (0, 69))))
-    small = jnp.pad(jnp.stack(small, axis=1), ((0, 0), (0, 1), (0, 56))).reshape(4, 4, 8, 128)
-    down_blocks = down_term.reshape(16, SLOT, D)[:, :PIECE].reshape(4, 4, PIECE, D)
-    both_sum, small_sum, down_sum, qkv_sum, output_sum = sum_seq(
-        "sum_weights", 4, [both_term.reshape(4, 4, 72, 2 * WIDE), small], [down_blocks],
-        [(qkv_term.reshape(4, 4, 72, 1536), 768, 768), (output_term.reshape(4, 4, 64, D), 512, 640)],
-    )
-    small_all, both_rows, qkv_rows, output_rows = exchange_shard(
-        "exchange_grads", 5, [small_sum],
-        [both_sum.reshape(8, 9, 2 * WIDE), qkv_sum.reshape(8, 9, 768), output_sum.reshape(8, 8, 640)],
-    )
+    back = SimpleNamespace(**attend_back(
+        2,
+        dict(
+            feed_grad=feed_grad, hidden=hidden, branch=branch, cotangent=cotangent[0], stream=stream[0],
+            normed=normed, query=query_proj, key=key_proj, turned=query_rot, kv=kv, probs=probability, mixed=mixed,
+            gains=gain_rows, cosine=cosine, sine=sine, qkv_weight=full_qkv, output_weight=full_output,
+            post_grad=gain_mlp_post_grad, result_squares=result_squares,
+            both_term=both_term.reshape(4, 4, 72, 2 * WIDE),
+            down_term=down_term.reshape(16, SLOT, D)[:, :PIECE].reshape(4, 4, PIECE, D),
+        ),
+    ))
 
     def whole(rows):
         parts = rows.reshape(8, 9, 16, SLOT)[..., :PIECE]
         return parts.transpose(1, 2, 0, 3).reshape(9, FF).astype(jnp.float32)
 
-    qkv_grad = jnp.sum(qkv_rows.reshape(4, 2, 9, 768).astype(jnp.float32), axis=0)
-    qkv_grad = jnp.concatenate([qkv_grad[0], qkv_grad[1]], axis=1)
-    output_grad = jnp.sum(output_rows.reshape(4, 2, 8, 640).astype(jnp.float32), axis=0)
-    output_grad = jnp.concatenate([output_grad[0][:, :512], output_grad[1]], axis=1)
-    small_sum = jnp.sum(small_all, axis=0)
-    shard = lax.axis_index("shard")
-    gain_grads = lax.dynamic_slice_in_dim(small_sum, shard * 9, 9, 1)
-    head_grads = lax.dynamic_slice_in_dim(small_sum, shard * 2, 2, 1)
-    stream_rms = jnp.sqrt(small_sum[6, :3] / (32768 * D))
+    both_rows = back.both_rows.reshape(8, 9, 2 * WIDE)
+    sums = back.sums
+    own = lax.axis_index("seq") * 8 + lax.axis_index("shard")
+    gain_grads = lax.dynamic_slice_in_dim(sums[:4], own * 9, 9, 1)
+    query_gain_grad = lax.dynamic_slice_in_dim(sums[4, :HEAD_DIM], own * 2, 2, 0)
+    key_gain_grad = lax.dynamic_slice_in_dim(sums[4, HEAD_DIM : 2 * HEAD_DIM], own * 2, 2, 0)
+    stream_rms = jnp.sqrt(jnp.sum(sums[4, 512:896].reshape(3, 128), axis=1) / (32768 * D))
     return (
         block_output[None],
-        stream_grad[None],
+        back.stream_grad[None],
         gain_grads[0],
-        qkv_grad[:, :1024],
-        qkv_grad[:, 1024:1280],
-        qkv_grad[:, 1280:],
-        head_grads[4],
-        head_grads[5],
-        output_grad,
+        back.query_grad,
+        back.key_grad,
+        back.value_grad,
+        query_gain_grad,
+        key_gain_grad,
+        back.output_grad,
         gain_grads[1],
         gain_grads[2],
         whole(both_rows[:, :, :WIDE]),
         whole(both_rows[:, :, WIDE:]),
-        down_sum.astype(jnp.float32),
+        back.down_grad,
         gain_grads[3],
         stream_rms,
     )

time: 342 us -> 298 us (0.87)
  other arithmetic: 17.9 us -> 0.76 us
  matrix products: 12.7 us -> 0 us
  local copies, waits for them, and re-layouts: 31.6 us -> 20.8 us
    dot_general x8 -> x0, matrix products: 12.7 us -> none  [the longest x4 6.41 us: matmul_tn(): lax.dot_general(a, b, (((0,), (0,)), ((), ())), preferred_element_type=jn...]
    reduce_sum x12 -> x1, other arithmetic: 8.64 us -> 0.12 us  [local(): jnp.sum(sums[4, 512:896].reshape(3, 128), axis=1) / (32768 * D)]
    reshape x4 -> x0, local copies, waits for them, and re-layouts: 3.61 us -> none  [the longest x1 1.83 us: local(): both_sum.reshape(8, 9, 2 * WIDE)]
    unnamed x70 -> x43, local copies, waits for them, and re-layouts: 7.62 us -> 4.88 us
    pallas_call x5 -> x3, Pallas kernels: 278 us -> 275 us  [call(): pl.pallas_call(kernel, name=name, out_shape=outs, in_specs=in_specs or [A...]
where the time goes in v4:
time: 298 us
  Pallas kernels  275 us (92%)
  local copies, waits for them, and re-layouts  20.8 us (7%)
    pallas_call x3, Pallas kernels, call(): pl.pallas_call(kernel, name=name, out_shape=outs, in_specs=in_specs or [A...  275 us

profile of v4, /device:TPU:1, one launch (start us, length us, event | category | flops | bytes accessed | tf_op | source)
XLA Modules:
  0.0 297.8 jit_solution(11196797716085825945)
XLA Ops:
  0.6 0.0 copy-start.3
  0.7 1.7 reshape.133
  2.4 0.0 copy-start.6
  2.4 0.0 copy-start.10
  2.4 0.0 copy-start.11
  2.4 0.0 copy-start.12
  2.5 0.0 copy-start.13
  2.5 0.0 copy-start.14
  2.5 0.0 copy-start.15
  2.5 0.0 copy-start.16
  2.5 0.0 copy-start.17
  2.5 0.1 pad.37
  2.6 0.3 reshape.134
  2.9 0.0 copy-done.3
  2.9 0.8 reshape.135
  3.8 0.1 pad.38
  3.9 0.3 reshape.136
  4.2 0.7 copy.42.both_in
  4.9 0.0 copy-done.6
  4.9 0.0 copy-done.10
  4.9 0.0 copy-done.11
  5.0 0.7 reshape.132.qkv_in
  5.6 0.0 copy-done.12
  5.6 0.0 copy-done.13
  5.7 0.0 copy-done.14
  5.7 0.0 copy-done.15
  5.7 0.0 copy-done.16
  5.7 0.0 copy-done.17
  5.8 0.1 concatenate.14
  5.9 0.6 broadcast_in_dim.16.gains_in
  6.5 81.6 %attend.1 = (bf16[256,1152]{1,0:T(8,128)(2,1)}, f32[1024,256]{1,0:T(8,128)}, f32[256,256]{1,0:T(8,128)}, bf16[1024,256]{1,0:T(8,128)(2,1)}, bf16[768,512]{1,0:T(...) custom-call(bf16[256,1152]{1,0:T(8,128)(2,1)} %bitcast.56, ...), custom_call_target="tpu_custom_call" | custom-call | tf_op jit(solution)/shard_map/attend/pallas_call | solution.py:162
  88.1 1.4 slice.42.gain_in
  89.5 3.1 %pad.39 = bf16[16,56,1152]{2,1,0:T(8,128)(2,1)} pad(bf16[16,54,1152]{2,1,0:T(8,128)(2,1)} %bitcast.61, bf16[]{:T(256)} %constant.7.clone.1), padding=0_0x0_2x0_0 | pad | bytes 4055042 | tf_op jit(solution)/shard_map/jit(_pad)/pad | solution.py:1231
  92.5 105.1 %feed_forward.1 = (bf16[256,1152]{1,0:T(8,128)(2,1)}, f32[256,1152]{1,0:T(8,128)}, f32[1,1152]{1,0:T(1,128)}, f32[1,1152]{1,0:T(1,128)}, bf16[1152,1792]{1,0:T(8,128)(2,1)}, /*index=5*/bf16[896,1152]{1,0:T(8,128)(2,1)}) custom-call(bf16[256,1152]{1,0:T(8,128)(2,1)} %get-tuple-element.47.feed_in, bf16[1152,1792]{1,0:T(8,128)(2,1)} %bitcast.55, ...), custom_call_target="tpu_custom_call" | custom-call | tf_op jit(solution)/shard_map/feed_forward/pallas_call | solution.py:162
  197.6 88.5 %attend_back.1 = (bf16[256,1152]{1,0:T(8,128)(2,1)}, bf16[8,126,128]{2,1,0:T(8,128)(2,1)}, f32[9,1024]{1,0:T(8,128)}, f32[9,256]{1,0:T(8,128)}, f32[9,256]{1,0:T...) custom-call(f32[256,1152]{1,0:T(8,128)} %get-tuple-element.53.refs_0_, ...), custom_call_target="tpu_custom_call" | custom-call | tf_op jit(solution)/shard_map/attend_back/pallas_call | solution.py:162
  286.1 1.1 copy.43
  287.2 0.5 reshape.145
  287.8 0.2 copy.44
  288.0 0.0 copy-start.9
  288.0 1.2 reshape.147
  289.2 0.5 reshape.146
  289.6 0.0 copy-start.1
  289.7 0.0 copy-start.4
  289.7 0.2 copy.45
  289.9 0.0 copy-start.8
  289.9 0.0 copy-start.7
  289.9 0.0 copy-start.5
  289.9 0.0 copy-start.2
  290.0 1.2 reshape.148
  291.1 0.6 fusion
  291.7 0.1 constant_dynamic-slice_fusion.2
  291.8 0.5 slice_bitcast_fusion
  292.3 0.1 bitcast_reduce_fusion
  292.5 0.5 multiply_sqrt_fusion
  293.0 0.0 copy-done
  293.0 0.8 copy.57
  293.8 0.8 copy.58
  294.6 0.6 copy.59
  295.3 0.0 copy-done.8
  295.3 0.6 copy.60
  295.9 0.0 copy-done.7
  295.9 0.6 copy.61
  296.5 0.6 copy.62
  297.1 0.7 copy.63
  (23 shorter events, 0.3 us)
Async XLA Ops:
  0.6 2.2 copy-start.3
  2.4 2.5 copy-start.6
  2.4 2.5 copy-start.10
  2.4 2.5 copy-start.11
  2.4 3.2 %copy-start.12 = (bf16[9]{0:T(256)(128)(2,1)S(1)}, bf16[9]{0:T(256)(128)(2,1)}, u32[]{:S(2)}) copy-start(bf16[9]{0:T(256)(128)(2,1)} %param.19) | copy-start | bytes 58
  2.5 3.2 %copy-start.13 = (bf16[9]{0:T(256)(128)(2,1)S(1)}, bf16[9]{0:T(256)(128)(2,1)}, u32[]{:S(2)}) copy-start(bf16[9]{0:T(256)(128)(2,1)} %param.26) | copy-start | bytes 58
  2.5 3.2 %copy-start.14 = (bf16[9]{0:T(256)(128)(2,1)S(1)}, bf16[9]{0:T(256)(128)(2,1)}, u32[]{:S(2)}) copy-start(bf16[9]{0:T(256)(128)(2,1)} %param.27) | copy-start | bytes 58
  2.5 3.2 %copy-start.15 = (bf16[9]{0:T(256)(128)(2,1)S(1)}, bf16[9]{0:T(256)(128)(2,1)}, u32[]{:S(2)}) copy-start(bf16[9]{0:T(256)(128)(2,1)} %param.31) | copy-start | bytes 58
  2.5 3.2 %copy-start.16 = (bf16[2]{0:T(256)(128)(2,1)S(1)}, bf16[2]{0:T(256)(128)(2,1)}, u32[]{:S(2)}) copy-start(bf16[2]{0:T(256)(128)(2,1)} %param.23) | copy-start | bytes 16
  2.5 3.2 %copy-start.17 = (bf16[2]{0:T(256)(128)(2,1)S(1)}, bf16[2]{0:T(256)(128)(2,1)}, u32[]{:S(2)}) copy-start(bf16[2]{0:T(256)(128)(2,1)} %param.24) | copy-start | bytes 16
  288.0 3.2 %copy-start.9 = (f32[8,1152]{1,0:T(8,128)S(1)}, f32[8,1152]{1,0:T(8,128)}, u32[]{:S(2)}) copy-start(f32[8,1152]{1,0:T(8,128)} %get-tuple-element.71) | copy-start | bytes 110596
  289.2 3.8 %copy-start = (bf16[256,1152]{1,0:T(8,128)(2,1)S(1)}, bf16[256,1152]{1,0:T(8,128)(2,1)}, u32[]{:S(2)}) copy-start(bf16[256,1152]{1,0:T(8,128)(2,1)} %get-tuple-element.52) | copy-start | bytes 1769476
  289.6 4.2 %copy-start.1 = (bf16[256,1152]{1,0:T(8,128)(2,1)S(1)}, bf16[256,1152]{1,0:T(8,128)(2,1)}, u32[]{:S(2)}) copy-start(bf16[256,1152]{1,0:T(8,128)(2,1)} %get-tuple-element.70) | copy-start | bytes 1769476
  289.7 4.9 %copy-start.4 = (f32[9,1024]{1,0:T(8,128)S(1)}, f32[9,1024]{1,0:T(8,128)}, u32[]{:S(2)}) copy-start(f32[9,1024]{1,0:T(8,128)} %get-tuple-element.107) | copy-start | bytes 110596
  289.9 5.3 %copy-start.8 = (f32[9,256]{1,0:T(8,128)S(1)}, f32[9,256]{1,0:T(8,128)}, u32[]{:S(2)}) copy-start(f32[9,256]{1,0:T(8,128)} %get-tuple-element.108) | copy-start | bytes 27652
  289.9 5.9 %copy-start.7 = (f32[9,256]{1,0:T(8,128)S(1)}, f32[9,256]{1,0:T(8,128)}, u32[]{:S(2)}) copy-start(f32[9,256]{1,0:T(8,128)} %get-tuple-element.109) | copy-start | bytes 27652
  289.9 6.5 %copy-start.5 = (f32[8,1152]{1,0:T(8,128)S(1)}, f32[8,1152]{1,0:T(8,128)}, u32[]{:S(2)}) copy-start(f32[8,1152]{1,0:T(8,128)} %get-tuple-element.112) | copy-start | bytes 110596
  289.9 7.2 %copy-start.2 = (f32[54,1152]{1,0:T(8,128)S(1)}, f32[54,1152]{1,0:T(8,128)}, u32[]{:S(2)}) copy-start(f32[54,1152]{1,0:T(8,128)} %get-tuple-element.117) | copy-start | bytes 746500

commit v5 on v4

--- a/solution.py
+++ b/solution.py
@@ -75,7 +75,8 @@
         up, down, far = (me + 1) % 4, (me + 3) % 4, (me + 2) % 4
         self.right = Push(own, slot(me), sems, peer(up), slot(down))
         self.left = Push(own, slot(me), sems, peer(down), slot(up))
-        self.right2 = Push(half(down, 0), half(down, 0), sems, peer(up), half(far, 0))
+        split = half(down, 0)
+        self.right2 = None if split is None else Push(split, split, sems, peer(up), half(far, 0))
         split = half(up, 1)
         self.left2 = None if split is None else Push(split, split, sems, peer(down), half(far, 1))
 
@@ -85,13 +86,15 @@
 
     def relay(self):
         self.right.arrived()
-        self.right2.start()
+        if self.right2 is not None:
+            self.right2.start()
         self.left.arrived()
         if self.left2 is not None:
             self.left2.start()
 
     def last(self):
-        self.right2.arrived()
+        if self.right2 is not None:
+            self.right2.arrived()
         if self.left2 is not None:
             self.left2.arrived()
 
@@ -198,25 +201,32 @@
     return gate * half, slope
 
 
-def feed_forward(name, number, feed, full_both, full_down, hidden, cotangent, gain):
+def feed_forward(number, feed, feeds_a, full_both, down16, hidden, cotangent, gains):
     tokens, width = feed.shape
     rows = tokens // SUBS
     half = rows // 2
 
     def kernel(
-        feed_in, both_in, down_in, hidden_in, cotangent_in, gain_in,
+        feed_in, feeds_in, both_in, down_in, hidden_in, cotangent_in, gains_in,
         block_out, feed_out, gain_out, square_out, both_out, down_out,
-        feeds, downs, both, active, part, inbox, near, right, left, w_both, w_down, send, recv, here,
+        feeds, downs, both, active, part, inbox, near, right, left, w_both, w_down, raw, pad, both_term, down_term,
+        send, recv, here,
     ):
         x, y, z, c = place()
         sems = Sems(send, recv)
         other = device(x, y, z, 1 - c)
         to = lambda d: device(x, y + d, z, c)
+        span = lambda s: pl.ds(s * rows, rows)
+        a, b = 0, 1
+        loads = [
+            pltpu.make_async_copy(feeds_in, feeds.at[a], here.at[0]),
+            pltpu.make_async_copy(both_in, w_both, here.at[1]),
+            pltpu.make_async_copy(down_in, raw, here.at[2]),
+            pltpu.make_async_copy(feed_in.at[span(b)], feeds.at[b, y * 2 + c], here.at[3]),
+        ]
+        for load in loads:
+            load.start()
         greet([to(1), to(3), other])
-        loads = [
-            pltpu.make_async_copy(both_in, w_both, here.at[0]),
-            pltpu.make_async_copy(down_in, w_down, here.at[1]),
-        ]
 
         def gather(source, blocks, s):
             slot = lambda k: blocks.at[s, k * 2 + c]
@@ -331,13 +341,12 @@
             both[s, chip, :, WIDE:] = pair(up_grad)
             part[s, chip] = pair(dot(flat(both[s, chip]), w_both[...], 1, 1).astype(jnp.bfloat16))
 
-        span = lambda s: pl.ds(s * rows, rows)
         gain_out[...] = jnp.zeros_like(gain_out)
         square_out[...] = jnp.zeros_like(square_out)
 
         def norm_back(total, s):
             down = total.final()
-            gain_row = gain_in[...]
+            gain_row = gains_in[3:4, :]
             upstream = cotangent_in[span(s), :].astype(jnp.float32)
             scale = lax.rsqrt(jnp.mean(down * down, axis=-1, keepdims=True) + EPSILON)
             unit = down * scale
@@ -349,31 +358,18 @@
             grad = scale * (scaled - unit * jnp.mean(unit * scaled, axis=-1, keepdims=True))
             downs[s, y * 2 + c] = grad.astype(jnp.bfloat16)
 
-        a, b = 0, 1
-        first_a, relay_a, last_a, met_a, close_a = gather(feed_in.at[span(a)], feeds, a)
         first_b, relay_b, last_b, met_b, close_b = gather(feed_in.at[span(b)], feeds, b)
         sum_a, sum_b = Total(a), Total(b)
-        first_a()
+        first_b()
+        pad[...] = jnp.zeros_like(pad)
         for load in loads:
-            load.start()
-        own = [pltpu.make_async_copy(feed_in.at[span(s)], feeds.at[s, y * 2 + c], here.at[2 + s]) for s in (a, b)]
-        for copy in own:
-            copy.start()
-        for copy in own + loads:
-            copy.wait()
-
-        def at_1():
-            relay_a()
-            first_b()
-            met_a[1]()
-
-        def at_2():
-            last_a()
-            met_a[3]()
-
-        def at_3():
-            relay_b()
-            met_a[2]()
+            load.wait()
+
+        @pl.loop(0, 8)
+        def _(i):
+            for k in range(2):
+                pad[SLOT * k : SLOT * k + PIECE, :] = raw[i // 2, i % 2 * 2 + k].astype(jnp.float32)
+            w_down[pl.ds(pl.multiple_of(2 * SLOT * i, 16), 2 * SLOT), :] = pad[...].astype(jnp.bfloat16)
 
         def at_4():
             sum_a.far()
@@ -388,22 +384,39 @@
             sum_a.go()
             met_b[3]()
 
-        steps(
-            forward,
-            {0: met_a[0], 1: at_1, 2: at_2, 3: at_3, 4: at_4, 5: at_5, 6: at_6, 7: met_b[2]},
-            (sum_a, sum_b),
-        )
+        steps(forward, {3: relay_b, 4: at_4, 5: at_5, 6: at_6, 7: met_b[2]}, (sum_a, sum_b))
         sum_b.far()
         norm_back(sum_a, a)
         sum_a.close()
-        close_a()
         first_a, relay_a, last_a, met_a, close_a = gather(downs.at[a, y * 2 + c], downs, a)
         first_a()
         sum_b.sides()
         sum_b.go()
-        old_a, old_b, old_close_b = sum_a, sum_b, close_b
+        old_b, old_close_b = sum_b, close_b
         first_b, relay_b, last_b, met_b, close_b = gather(downs.at[b, y * 2 + c], downs, b)
         sum_a, sum_b = Total(a), Total(b)
+
+        def down_terms(s):
+            every = 8 * rows
+
+            @pl.loop(0, WIDE // 128)
+            def _(i):
+                units = pl.ds(pl.multiple_of(i * 128, 128), 128)
+                value = dot(active[s, :, :, units].reshape(every, 128), downs[s].reshape(every, width), 0, 0)
+                if s == b:
+                    value += down_term[units, :].astype(jnp.float32)
+                down_term[units, :] = value.astype(jnp.bfloat16)
+
+        def both_terms(s):
+            every = 8 * rows
+
+            @pl.loop(0, width // 128)
+            def _(i):
+                lanes = pl.ds(pl.multiple_of(i * 128, 128), 128)
+                value = dot(feeds[s, :, :, lanes].reshape(every, 128), both[s].reshape(every, 2 * WIDE), 0, 0)
+                if s == b:
+                    value += both_term[lanes, :].astype(jnp.float32)
+                both_term[lanes, :] = value.astype(jnp.bfloat16)
 
         def back_1():
             relay_a()
@@ -411,55 +424,49 @@
 
         def back_2():
             last_a()
+            met_a[3]()
+
+        def back_4():
             norm_back(old_b, b)
             old_b.close()
             old_close_b()
             first_b()
-            met_a[3]()
-
-        def back_4():
             sum_a.far()
             met_b[0]()
 
         def back_5():
+            down_terms(a)
+            sum_a.sides()
             relay_b()
-            sum_a.sides()
+            both_terms(a)
+            sum_a.go()
+            last_b()
             met_b[1]()
-
-        def back_6():
-            last_b()
-            sum_a.go()
-            met_b[3]()
 
         steps(
             backward,
-            {0: met_a[0], 1: back_1, 2: back_2, 3: met_a[2], 4: back_4, 5: back_5, 6: back_6, 7: met_b[2]},
+            {0: met_a[0], 1: back_1, 2: back_2, 3: met_a[2], 4: back_4, 5: back_5, 6: met_b[3], 7: met_b[2]},
             (sum_a, sum_b),
         )
         sum_b.far()
         sum_b.sides()
-        every = 8 * tokens
-
-        @pl.loop(0, WIDE // 128)
-        def _(i):
-            units = pl.ds(pl.multiple_of(i * 128, 128), 128)
-            lhs = active[:, :, :, units].reshape(every, 128)
-            down_out[units, :] = dot(lhs, downs[...].reshape(every, width), 0, 0).astype(jnp.bfloat16)
-
+        down_terms(b)
+        saves = [
+            pltpu.make_async_copy(down_term, down_out, here.at[0]),
+            pltpu.make_async_copy(both_term, both_out, here.at[1]),
+        ]
+        saves[0].start()
         sum_b.go()
         feed_out[span(a), :] = sum_a.final()
-
-        @pl.loop(0, width // 128)
-        def _(i):
-            lanes = pl.ds(pl.multiple_of(i * 128, 128), 128)
-            lhs = feeds[:, :, :, lanes].reshape(every, 128)
-            both_out[lanes, :] = dot(lhs, both[...].reshape(every, 2 * WIDE), 0, 0).astype(jnp.bfloat16)
-
+        both_terms(b)
+        saves[1].start()
         feed_out[span(b), :] = sum_b.final()
         sum_a.close()
         sum_b.close()
         close_a()
         close_b()
+        for save in saves:
+            save.wait()
 
     low, wide = jnp.bfloat16, jnp.float32
     blocks = (SUBS, 8, rows)
@@ -475,6 +482,10 @@
         pltpu.VMEM((SUBS, rows, width), low),
         pltpu.VMEM((width, 2 * WIDE), low),
         pltpu.VMEM((WIDE, width), low),
+        pltpu.VMEM((4, 4, PIECE, width), low),
+        pltpu.VMEM((2 * SLOT, width), wide),
+        pltpu.VMEM((width, 2 * WIDE), low),
+        pltpu.VMEM((WIDE, width), low),
     ]
     outs = [
         ((tokens, width), low),
@@ -485,18 +496,20 @@
         ((WIDE, width), low),
     ]
     return call(
-        kernel, name, number, outs, [feed, full_both, full_down, hidden, cotangent, gain], scratch, 32 * SUBS,
-        in_specs=[ANY, ANY, ANY, VMEM, VMEM, VMEM], out_specs=[VMEM] * 6, local=2 + SUBS,
+        kernel, "feed_forward", number, outs, [feed, feeds_a, full_both, down16, hidden, cotangent, gains], scratch,
+        32 * SUBS - 8, in_specs=[ANY] * 4 + [VMEM] * 3, out_specs=[VMEM] * 4 + [ANY] * 2, local=4,
     )
 
 
 class Either:
     def __init__(self, core, sems, make):
-        self.core, start = core, sems.used
+        self.core, start, most = core, sems.used, 0
         self.variants = []
         for order in (0, 1):
             sems.used = start
             self.variants.append(make(order))
+            most = max(most, sems.used)
+        sems.used = most
 
     def __getattr__(self, name):
         def run():
@@ -526,7 +539,7 @@
     return Either(c, sems, make)
 
 
-def ring_rest(out, cut, sems):
+def ring_rest(out, cut, sems, lean=False):
     x, y, z, c = place()
 
     def make(order):
@@ -534,6 +547,8 @@
             slot, half, me = lambda k: cut(out.at[k]), lambda k, h: cut(out.at[k, pl.ds(2 * h, 2)]), x
         else:
             slot, half, me = lambda k: cut(out.at[:, k]), lambda k, h: cut(out.at[pl.ds(2 * h, 2), k]), z
+            if lean:
+                half = lambda k, h: slot(k) if h else None
         peer = (lambda k: device(k, y, z, c)) if order == 0 else (lambda k: device(x, y, k, c))
         return RingGather(slot(me), slot, half, me, peer, sems)
 
@@ -579,30 +594,71 @@
     return (key <= query) & (key > query - WINDOW) & (key >= beginning)
 
 
-def gain_row(table, first, each, width):
+def gain_picks(each, width):
+    lane = lax.broadcasted_iota(jnp.int32, (16, width), 1)
+    owner = (lane * 7282) >> 16 if each == 9 else lane >> 1
+    pick = lax.broadcasted_iota(jnp.int32, (16, width), 0) == lane - owner * each
     lane = lax.broadcasted_iota(jnp.int32, (128, width), 1)
-    row = lax.broadcasted_iota(jnp.int32, (128, width), 0)
     owner = (lane * 7282) >> 16 if each == 9 else lane >> 1
-    pick = (row == first + lane - owner * each).astype(jnp.float32).astype(jnp.bfloat16)
-    spread = dot(table, pick, 1, 0)
-    return jnp.sum(jnp.where(row == owner, spread, 0.0), axis=0, keepdims=True)
+    owns = lax.broadcasted_iota(jnp.int32, (128, width), 0) == owner
+    return pick.astype(jnp.float32).astype(jnp.bfloat16), owns.astype(jnp.float32)
+
+
+def gain_row(table, first, pick, owns):
+    spread = dot(table[:, first : first + 16], pick, 1, 0)
+    return jnp.sum(spread * owns, axis=0, keepdims=True)
 
 
 def lanes_of(start, size):
     return lambda ref: ref.at[(slice(None),) * (len(ref.shape) - 1) + (pl.ds(start, size),)]
 
 
-def attend(number, stream, doc_starts, own_qkv, own_gains, own_output, own_both, own_down):
+def attend(number, stream, doc_starts, own_query, own_kv, own_output, own_both, own_down):
     tokens = stream.shape[0]
     span = tokens + WINDOW
 
+    low, wide = jnp.bfloat16, jnp.float32
+    keep = dict(
+        normed=((tokens, D), low),
+        query=((HEADS * tokens, HEAD_DIM), wide),
+        key=((tokens, HEAD_DIM), wide),
+        turned=((HEADS * tokens, HEAD_DIM), low),
+        kv=((span, 2 * HEAD_DIM), low),
+        probs=((HEADS * tokens, span), wide),
+        mixed=((tokens, HEADS * HEAD_DIM), low),
+        branch=((tokens, D), wide),
+        hidden=((tokens, D), wide),
+        feed=((tokens, D), low),
+        gains=((8, D), wide),
+        cosine=((tokens, HEAD_DIM // 2), wide),
+        sine=((tokens, HEAD_DIM // 2), wide),
+        qkv_weight=((D, 1536), low),
+        output_weight=((HEADS * HEAD_DIM, D), low),
+    )
+
     def kernel(
-        stream_in, starts_in, qkv_in, gains_in, output_in, both_in, down_in,
-        normed_out, query_out, key_out, turned_out, kv_out, probs_out, mixed_out, branch_out, hidden_out, feed_out,
-        gains_out, cosine_out, sine_out, qkv_out, output_out, both_out, down_out,
-        qkv_box, gains_box, both_box, flat, merge, qkv_own, gains_own, both_own, qkv_all, gains_all, output_all, kv,
-        send, recv, here,
+        stream_in, starts_in, query_in, kv_in, output_in, both_in, down_in, *refs
     ):
+        refs = list(refs)
+
+        def take(count):
+            taken, refs[:] = refs[:count], refs[count:]
+            return taken
+
+        saved = SimpleNamespace(**dict(zip(keep, take(len(keep)))))
+        both_out, down_out, feeds_out = take(3)
+        v = SimpleNamespace(**dict(zip(keep, take(len(keep)))))
+        (
+            query_box, kv_box, both_box, flat, merge, query_own, kv_own, both_own, query_all, kv_all, output_all, kv,
+            owns9, owns2,
+            send, recv, here,
+        ) = refs
+        saves = []
+
+        def save(src, dst):
+            saves.append(pltpu.make_async_copy(src, dst, here.at[5 + len(saves)]))
+            saves[-1].start()
+
         x, y, z, c = place()
         q, s = lax.axis_index("seq"), lax.axis_index("shard")
         sems = Sems(send, recv)
@@ -631,17 +687,23 @@
                 push.arrived()
             tiles = own.shape[-1] // 128
             for d in range(8):
-                flat[: 9 * tiles, :] = box[d].astype(jnp.float32)
+                flat[: box.shape[1], :] = box[d].astype(jnp.float32)
                 for j in range(tiles):
                     merge[9 * d : 9 * d + 9, 128 * j : 128 * (j + 1)] = flat[pl.ds(j, 9, tiles), :]
-            own[...] = merge[:, : own.shape[-1]].astype(own.dtype)
-
-        my_lanes = lanes_of(pl.multiple_of(c * 768, 128), 768)
-        their_lanes = lanes_of(pl.multiple_of((1 - c) * 768, 128), 768)
+                if box.shape[1] > 9 * tiles:
+                    for start in (0, 256):
+                        merge[72 + d : 73 + d, start : start + 128] = flat[9 * tiles : 9 * tiles + 1, :]
+            own[...] = merge[: own.shape[0], : own.shape[-1]].astype(own.dtype)
+
+        def halves(size):
+            return [lanes_of(pl.multiple_of(core * size, 128), size) for core in (c, 1 - c)]
+
+        my_query, their_query = halves(512)
+        my_kv, their_kv = halves(256)
         mine = lambda ref: ref.at[(slice(None),) * (len(ref.shape) - 3) + (s,)]
 
-        got_qkv = spread(qkv_in, qkv_box)
-        got_gains = spread(gains_in, gains_box)
+        got_kv = spread(kv_in, kv_box)
+        got_query = spread(query_in, query_box)
         down_ring = ring_row(down_in, down_out, whole_ref, sems)
         output_ring = ring_row(output_in, output_all, mine, sems)
         down_ring.first()
@@ -656,63 +718,95 @@
             beginning = jnp.maximum(beginning, jnp.where(start <= positions, start, 0))
         steps = lax.broadcasted_iota(jnp.int32, (1, HEAD_DIM // 2), 1).astype(jnp.float32)
         angles = (positions - beginning).astype(jnp.float32) * jnp.exp(steps * (-2.0 * math.log(10000.0) / HEAD_DIM))
-        cosine_out[...] = jnp.cos(angles)
-        sine_out[...] = jnp.sin(angles)
+        v.cosine[...] = jnp.cos(angles)
+        v.sine[...] = jnp.sin(angles)
+        pick9, owns9[...] = gain_picks(9, D)
+        pick2, owns2[...] = gain_picks(2, HEAD_DIM)
+        v.gains[...] = jnp.zeros_like(v.gains)
+        merge[72:80, :] = jnp.zeros((8, merge.shape[1]), jnp.float32)
 
         own = lambda src, dst, at: pltpu.make_async_copy(src, dst, here.at[at])
-        collect(got_qkv, qkv_box, qkv_own)
-        qkv_ring = ring_row(my_lanes(qkv_own), qkv_all, my_lanes, sems)
-        qkv_ring.first()
+        collect(got_kv, kv_box, kv_own)
+        kv_ring = ring_row(my_kv(kv_own), kv_all, my_kv, sems)
+        kv_ring.first()
+        collect(got_query, query_box, query_own)
+        query_ring = ring_row(my_query(query_own), query_all, my_query, sems)
+        query_ring.first()
         got_both = spread(both_in, both_box, True)
-        for push in got_gains:
-            push.arrived()
-        for d in range(8):
-            gains_own[d : d + 1, :] = gains_box[d, 0:1, :]
-        gains_ring = ring_row(gains_own, gains_all, whole_ref, sems)
-        gains_ring.first()
         copies = [
-            own(my_lanes(qkv_own), my_lanes(qkv_all.at[x, z]), 0),
-            own(gains_own, gains_all.at[x, z], 1),
-            own(down_in, down_out.at[x, z], 2),
-            own(output_in, output_all.at[x, z, s], 3),
+            own(my_kv(kv_own), my_kv(kv_all.at[x, z]), 0),
+            own(down_in, down_out.at[x, z], 1),
+            own(output_in, output_all.at[x, z, s], 2),
+            own(my_query(query_own), my_query(query_all.at[x, z]), 3),
         ]
         for copy in copies:
             copy.start()
         down_ring.relay()
         output_ring.relay()
-        qkv_ring.relay()
-        gains_ring.relay()
+        kv_ring.relay()
+        query_ring.relay()
         for copy in copies:
             copy.wait()
-        qkv_ring.last()
-        gains_ring.last()
-        qkv_rest = ring_rest(qkv_all, my_lanes, sems)
-        gains_rest = ring_rest(gains_all, whole_ref, sems)
-        qkv_cross = Crossing(qkv_all, my_lanes, their_lanes, sems)
-        qkv_rest.first()
-        gains_rest.first()
-        qkv_cross.start(0)
+        kv_ring.last()
+        kv_rest = ring_rest(kv_all, my_kv, sems)
+        kv_cross = Crossing(kv_all, my_kv, their_kv, sems)
+        kv_rest.first()
+        kv_cross.start(0)
+        query_ring.last()
+        query_rest = ring_rest(query_all, my_query, sems)
+        query_cross = Crossing(query_all, my_query, their_query, sems)
+        query_rest.first()
+        query_cross.start(0)
         down_ring.last()
         output_ring.last()
-        down_rest = ring_rest(down_out, whole_ref, sems)
+        down_rest = ring_rest(down_out, whole_ref, sems, True)
         output_rest = ring_rest(output_all, mine, sems)
+        kv_rest.relay()
+        kv_cross.start(3)
+        kv_cross.start(1)
         output_rest.first()
-        down_rest.first()
         collect(got_both, both_box, both_own)
         both_ring = ring_row(both_own, both_out, whole_ref, sems)
         both_ring.first()
         both_copy = own(both_own, both_out.at[x, z], 4)
         both_copy.start()
-        qkv_rest.relay()
-        gains_rest.relay()
-        qkv_cross.start(3)
-        qkv_cross.start(1)
+        kv_rest.last()
+        kv_cross.start(2)
+        query_rest.relay()
+        query_cross.start(3)
+        query_cross.start(1)
         output_rest.relay()
+        down_rest.first()
+        table = kv_all[:, :, 72:80, pl.ds(pl.multiple_of(c * 256, 128), 128)].reshape(128, 128)
+        for g in range(4):
+            v.gains[g : g + 1, :] = gain_row(table, 16 * g, pick9, owns9[...])
+        for g in range(2):
+            v.gains[4 + g : 5 + g, :HEAD_DIM] = gain_row(table, 64 + 16 * g, pick2, owns2[...])
+        normed = (unit * v.gains[0:1, :]).astype(jnp.bfloat16)
+        v.normed[...] = normed
+
+        def assemble(blocks, lanes):
+            @pl.loop(0, 8)
+            def _(i):
+                pair = [blocks[i // 2, i % 2 * 2 + k, :72].astype(jnp.float32) for k in range(2)]
+                rows = pl.ds(pl.multiple_of(144 * i, 144), 144)
+                v.qkv_weight[rows, lanes] = jnp.concatenate(pair, axis=0).astype(jnp.bfloat16)
+
+        kv_cross.close()
+        assemble(kv_all, slice(1024, 1536))
+
+        near = Push(kv.at[2], kv.at[1], sems, after)
+        far = Push(kv.at[1], kv.at[0], sems, after)
+        key_value = dot(normed, v.qkv_weight[:, 1024:], 1, 0)
+        key = key_value[:, :HEAD_DIM]
+        v.key[...] = key
+        key_turned = turn(unit_rows(key)[0] * v.gains[5:6, :HEAD_DIM], v.cosine[...], v.sine[...])
+        kv[2, :, :HEAD_DIM] = key_turned.astype(jnp.bfloat16)
+        kv[2, :, HEAD_DIM:] = key_value[:, HEAD_DIM:].astype(jnp.bfloat16)
+        near.start()
+        query_rest.last()
+        query_cross.start(2)
         both_ring.relay()
-        down_rest.relay()
-        qkv_rest.last()
-        gains_rest.last()
-        qkv_cross.start(2)
         output_rest.last()
         other = device(x, y, z, 1 - c)
         column = lambda k: output_all.at[:, :, k * 2 + c]
@@ -726,49 +820,36 @@
         ]
         output_y.first()
         output_cross[0].start()
+        for src, dst in ((v.gains, saved.gains), (v.cosine, saved.cosine), (v.sine, saved.sine)):
+            save(src, dst)
+        query_cross.close()
+        assemble(query_all, slice(0, 1024))
+        save(v.qkv_weight, saved.qkv_weight)
         both_ring.last()
         both_copy.wait()
-        both_rest = ring_rest(both_out, whole_ref, sems)
-        table = gains_all[...].reshape(128, 128).astype(jnp.bfloat16)
-        for g in range(4):
-            gains_out[g : g + 1, :] = gain_row(table, 16 * g, 9, D)
-        for g in range(2):
-            gains_out[4 + g : 5 + g, :HEAD_DIM] = gain_row(table, 64 + 16 * g, 2, HEAD_DIM)
-        qkv_cross.close()
-
-        @pl.loop(0, 8)
-        def _(i):
-            pair = [qkv_all[i // 2, i % 2 * 2 + k].astype(jnp.float32) for k in range(2)]
-            qkv_out[pl.ds(pl.multiple_of(144 * i, 144), 144), :] = jnp.concatenate(pair, axis=0).astype(jnp.bfloat16)
-
-        near = Push(kv.at[2], kv.at[1], sems, after)
-        far = Push(kv.at[1], kv.at[0], sems, after)
-        normed = (unit * gains_out[0:1, :]).astype(jnp.bfloat16)
-        normed_out[...] = normed
-        key_value = dot(normed, qkv_out[:, 1024:], 1, 0)
-        key = key_value[:, :HEAD_DIM]
-        key_out[...] = key
-        key_turned = turn(unit_rows(key)[0] * gains_out[5:6, :HEAD_DIM], cosine_out[...], sine_out[...])
-        kv[2, :, :HEAD_DIM] = key_turned.astype(jnp.bfloat16)
-        kv[2, :, HEAD_DIM:] = key_value[:, HEAD_DIM:].astype(jnp.bfloat16)
-        near.start()
+        both_rest = ring_rest(both_out, whole_ref, sems, True)
         both_rest.first()
+        down_rest.relay()
+        for h in range(HEADS):
+            lanes = slice(h * HEAD_DIM, (h + 1) * HEAD_DIM)
+            span_h = slice(h * tokens, (h + 1) * tokens)
+            query = dot(normed, v.qkv_weight[:, lanes], 1, 0)
+            v.query[span_h, :] = query
+            turned = turn(unit_rows(query)[0] * v.gains[4:5, :HEAD_DIM], v.cosine[...], v.sine[...])
+            v.turned[span_h, :] = turned.astype(jnp.bfloat16)
+        save(v.query, saved.query)
+        save(v.turned, saved.turned)
+        save(v.normed, saved.normed)
+        save(v.key, saved.key)
+        near.arrived()
+        far.start()
         output_y.relay()
         output_cross[1].start()
         output_cross[3].start()
-        for h in range(HEADS):
-            lanes = slice(h * HEAD_DIM, (h + 1) * HEAD_DIM)
-            span_h = slice(h * tokens, (h + 1) * tokens)
-            query = dot(normed, qkv_out[:, lanes], 1, 0)
-            query_out[span_h, :] = query
-            turned = turn(unit_rows(query)[0] * gains_out[4:5, :HEAD_DIM], cosine_out[...], sine_out[...])
-            turned_out[span_h, :] = turned.astype(jnp.bfloat16)
-        near.arrived()
-        far.start()
+        both_rest.relay()
         output_y.last()
         output_cross[2].start()
         down_rest.last()
-        both_rest.relay()
         for push in output_cross:
             push.arrived()
 
@@ -777,73 +858,99 @@
             for j in range(4):
                 pair = [output_all[i // 4, i % 4, 2 * j + k].astype(jnp.float32) for k in range(2)]
                 rows = pl.ds(pl.multiple_of(64 * i + 16 * j, 16), 16)
-                output_out[rows, :] = jnp.concatenate(pair, axis=0).astype(jnp.bfloat16)
-
+                v.output_weight[rows, :] = jnp.concatenate(pair, axis=0).astype(jnp.bfloat16)
+
+        save(v.output_weight, saved.output_weight)
         far.arrived()
-        kv_out[...] = kv[...].reshape(span, 2 * HEAD_DIM)
+        v.kv[...] = kv[...].reshape(span, 2 * HEAD_DIM)
+        save(v.kv, saved.kv)
         allowed = allowed_keys(q * tokens, beginning, tokens, span)
-        keys, values = kv_out[:, :HEAD_DIM], kv_out[:, HEAD_DIM:]
-        for h in range(HEADS):
-            span_h = slice(h * tokens, (h + 1) * tokens)
-            scores = dot(turned_out[span_h, :], keys, 1, 1) * HEAD_DIM ** (-0.5)
-            scores = jnp.where(allowed, scores, NEGATIVE)
-            exponent = jnp.exp(scores - jnp.max(scores, axis=-1, keepdims=True))
-            probs = exponent / jnp.sum(exponent, axis=-1, keepdims=True)
-            probs_out[span_h, :] = probs
-            mixed_out[:, h * HEAD_DIM : (h + 1) * HEAD_DIM] = dot(probs.astype(jnp.bfloat16), values, 1, 0).astype(
-                jnp.bfloat16
+        keys, values = v.kv[:, :HEAD_DIM], v.kv[:, HEAD_DIM:]
+        rows = tokens // SUBS
+
+        def attend_part(part):
+            here_rows = slice(part * rows, (part + 1) * rows)
+            for h in range(HEADS):
+                span_h = slice(h * tokens + part * rows, h * tokens + (part + 1) * rows)
+                scores = dot(v.turned[span_h, :], keys, 1, 1) * HEAD_DIM ** (-0.5)
+                scores = jnp.where(allowed[here_rows], scores, NEGATIVE)
+                exponent = jnp.exp(scores - jnp.max(scores, axis=-1, keepdims=True))
+                probs = exponent / jnp.sum(exponent, axis=-1, keepdims=True)
+                v.probs[span_h, :] = probs
+                mixed = dot(probs.astype(jnp.bfloat16), values, 1, 0)
+                v.mixed[here_rows, h * HEAD_DIM : (h + 1) * HEAD_DIM] = mixed.astype(jnp.bfloat16)
+            branch = dot(v.mixed[here_rows, :], v.output_weight[...], 1, 0)
+            v.branch[here_rows, :] = branch
+            hidden = inputs[here_rows] + unit_rows(branch)[0] * v.gains[1:2, :]
+            v.hidden[here_rows, :] = hidden
+            v.feed[here_rows, :] = (unit_rows(hidden)[0] * v.gains[2:3, :]).astype(jnp.bfloat16)
+
+        attend_part(0)
+        first_rows = v.feed.at[pl.ds(0, rows)]
+        block = lambda k: feeds_out.at[k * 2 + c]
+        feed_y = RingGather(
+            first_rows, block, lambda k, h: feeds_out.at[k * 2 + c, pl.ds(h * (rows // 2), rows // 2)],
+            y, lambda k: device(x, k, z, c), sems,
+        )
+        feed_cross = [
+            Push(
+                first_rows if d == 0 else block((y + d) % 4), block((y + d) % 4), sems, other,
+                feeds_out.at[(y + d) % 4 * 2 + 1 - c],
             )
-        branch = dot(mixed_out[...], output_out[...], 1, 0)
-        branch_out[...] = branch
-        hidden = inputs + unit_rows(branch)[0] * gains_out[1:2, :]
-        hidden_out[...] = hidden
-        feed_out[...] = (unit_rows(hidden)[0] * gains_out[2:3, :]).astype(jnp.bfloat16)
+            for d in range(4)
+        ]
+        feed_y.first()
+        feed_cross[0].start()
+        save(first_rows, feeds_out.at[s])
+        attend_part(1)
+        for src, dst in (
+            (v.probs, saved.probs), (v.branch, saved.branch), (v.hidden, saved.hidden), (v.mixed, saved.mixed),
+            (v.feed, saved.feed),
+        ):
+            save(src, dst)
+        feed_y.relay()
+        feed_cross[1].start()
+        feed_cross[3].start()
         both_rest.last()
-        rings = [qkv_ring, gains_ring, down_ring, output_ring, both_ring]
-        rings += [qkv_rest, gains_rest, down_rest, output_rest, both_rest, output_y]
+        feed_y.last()
+        feed_cross[2].start()
+        for push in feed_cross:
+            push.arrived()
+        rings = [query_ring, kv_ring, down_ring, output_ring, both_ring]
+        rings += [query_rest, kv_rest, down_rest, output_rest, both_rest, output_y, feed_y]
         for ring in rings:
             ring.close()
-        for push in sent + output_cross + [near, far]:
+        for push in sent + output_cross + feed_cross + [near, far]:
             push.sent()
-
-    low, wide = jnp.bfloat16, jnp.float32
-    outs = [
-        ((tokens, D), low),
-        ((HEADS * tokens, HEAD_DIM), wide),
-        ((tokens, HEAD_DIM), wide),
-        ((HEADS * tokens, HEAD_DIM), low),
-        ((span, 2 * HEAD_DIM), low),
-        ((HEADS * tokens, span), wide),
-        ((tokens, HEADS * HEAD_DIM), low),
-        ((tokens, D), wide),
-        ((tokens, D), wide),
-        ((tokens, D), low),
-        ((8, D), wide),
-        ((tokens, HEAD_DIM // 2), wide),
-        ((tokens, HEAD_DIM // 2), wide),
-        ((D, 1536), low),
-        ((HEADS * HEAD_DIM, D), low),
+        for copy in saves:
+            copy.wait()
+
+    outs = list(keep.values()) + [
         ((4, 4, 72, 2 * WIDE), low),
         ((4, 4, PIECE, D), low),
+        ((8, tokens // SUBS, D), low),
     ]
-    scratch = [
-        pltpu.VMEM((8, 108, 128), low),
-        pltpu.VMEM((8, 8, 128), wide),
+    scratch = [pltpu.VMEM(shape, kind) for shape, kind in keep.values()] + [
+        pltpu.VMEM((8, 72, 128), low),
+        pltpu.VMEM((8, 40, 128), low),
         pltpu.VMEM((8, 126, 128), low),
         pltpu.VMEM((128, 128), wide),
-        pltpu.VMEM((72, 2 * WIDE), wide),
-        pltpu.VMEM((72, 1536), low),
-        pltpu.VMEM((8, 128), wide),
+        pltpu.VMEM((80, 2 * WIDE), wide),
+        pltpu.VMEM((72, 1024), low),
+        pltpu.VMEM((80, 512), low),
         pltpu.VMEM((72, 2 * WIDE), low),
-        pltpu.VMEM((4, 4, 72, 1536), low),
-        pltpu.VMEM((4, 4, 8, 128), wide),
+        pltpu.VMEM((4, 4, 72, 1024), low),
+        pltpu.VMEM((4, 4, 80, 512), low),
         pltpu.VMEM((4, 4, 8, 8, D), low),
         pltpu.VMEM((3, tokens, 2 * HEAD_DIM), low),
+        pltpu.VMEM((128, D), wide),
+        pltpu.VMEM((128, HEAD_DIM), wide),
     ]
-    return call(
-        kernel, "attend", number, outs, [stream, doc_starts, own_qkv, own_gains, own_output, own_both, own_down],
-        scratch, 21 + 10 * 4 + 4 + 4 + 4 + 2, in_specs=[VMEM] * 7, out_specs=[VMEM] * 15 + [ANY] * 2, local=5,
+    out = call(
+        kernel, "attend", number, outs, [stream, doc_starts, own_query, own_kv, own_output, own_both, own_down],
+        scratch, 3 * 7 + 11 * 4 + 2 * 4 + 4 + 2 + 4 + 4, in_specs=[VMEM] * 7, local=5 + 16,
     )
+    return SimpleNamespace(**dict(zip(keep, out))), out[len(keep) :]
 
 
 def norm_grad(values, gain, grad):
@@ -937,6 +1044,7 @@
         x_sums=pltpu.VMEM((4, 8, D), wide),
     )
     room = vars(room)
+    held_names = names[:-2]
 
     def kernel(*refs):
         refs = list(refs)
@@ -945,8 +1053,9 @@
             taken, refs[:] = refs[:count], refs[count:]
             return taken
 
-        a = SimpleNamespace(**dict(zip(names, take(len(names)))))
+        given = dict(zip(names, take(len(names))))
         o = SimpleNamespace(**dict(zip(results, take(len(results)))))
+        a = SimpleNamespace(**dict(zip(held_names, take(len(held_names)))))
         b = SimpleNamespace(**dict(zip(room, take(len(room)))))
         held = {n: take(len(store)) for n, store in zip(sizes, stores)}
         send, recv, here = refs
@@ -955,20 +1064,27 @@
         sems = Sems(send, recv)
         other = device(x, y, z, 1 - c)
         after, before = {"seq": (q + 1) % 16, "shard": s}, {"seq": (q + 15) % 16, "shard": s}
+        rings = {n: scatter_rings(held[n][0], held[n][1:9], sems) for n in sizes}
+        cross = {n: Push(held[n][GIVE], held[n][TAKE], sems, other) for n in SHARED}
+        loads = [
+            pltpu.make_async_copy(given[names[-2]], held[BOTH][0], here.at[0]),
+            pltpu.make_async_copy(given[names[-1]], held[DOWN][0], here.at[1]),
+        ]
+        for at, name in enumerate(held_names):
+            loads.append(pltpu.make_async_copy(given[name], getattr(a, name), here.at[2 + at]))
+        for load in loads:
+            load.start()
         greet(
             [device(x, y + dy, z, (c + dc) % 2) for dy, dc in SHARD_STEPS]
             + [device(x, y, z + d, c) for d in (1, 2, 3)]
             + [device(x + d, y, z, c) for d in (1, 2, 3)]
             + [after, before]
         )
-        rings = {n: scatter_rings(held[n][0], held[n][1:9], sems) for n in sizes}
-        cross = {n: Push(held[n][GIVE], held[n][TAKE], sems, other) for n in SHARED}
-        loads = [
-            pltpu.make_async_copy(a.both_term, held[BOTH][0], here.at[0]),
-            pltpu.make_async_copy(a.down_term, held[DOWN][0], here.at[1]),
-        ]
-        for load in loads:
-            load.start()
+        for n, load in zip((BOTH, DOWN), loads):
+            load.wait()
+            rings[n][0].first()
+        for load in loads[2:]:
+            load.wait()
         gains = a.gains
         cosine, sine = a.cosine, a.sine
         own = b.own_sums.at[0]
@@ -989,9 +1105,6 @@
         )):
             folded = functools.reduce(jnp.add, [squares[:, 128 * j : 128 * (j + 1)] for j in range(D // 128)])
             own[4:5, 512 + 128 * at : 640 + 128 * at] = folded
-        for n, load in zip((BOTH, DOWN), loads):
-            load.wait()
-            rings[n][0].first()
         for h in range(HEADS):
             rows, lanes = slice(h * tokens, (h + 1) * tokens), slice(h * HEAD_DIM, (h + 1) * HEAD_DIM)
             b.mixed_grad[rows, :] = dot(b.branch_low[...], a.output_weight[lanes, :], 1, 1).astype(low)
@@ -1058,18 +1171,15 @@
                         held[OUTPUT][GIVE][block] = value
 
         cross[OUTPUT].start()
+        for n in (BOTH, DOWN):
+            rings[n][0].second()
         halo_far.arrived()
         b.halo_out[1] = (b.kv_grad[tokens : 2 * tokens, :] + b.halo_in[0].astype(wide)).astype(low)
         halo_near.start()
-        for n in (BOTH, DOWN):
-            rings[n][0].second()
         for n in (QUERY, OUTPUT):
             cross[n].arrived()
             add_into(held[n][0], held[n][TAKE])
             rings[n][0].first()
-        for n in (BOTH, DOWN):
-            rings[n][0].third()
-            rings[n][1].first()
         halo_near.arrived()
         kv_grad = b.kv_grad[2 * tokens :, :] + b.halo_in[1].astype(wide)
         back = turn(kv_grad[:, :HEAD_DIM], cosine[...], -sine[...])
@@ -1083,6 +1193,9 @@
         cross[KV].arrived()
         add_into(held[KV][0], held[KV][TAKE])
         rings[KV][0].first()
+        for n in (BOTH, DOWN):
+            rings[n][0].third()
+            rings[n][1].first()
         normed_grad = dot(b.qkv_low[...], a.qkv_weight[...], 1, 1)
         extra, own[0:1, :] = norm_grad(a.stream[...].astype(wide), gains[0:1, :], normed_grad)
         o.stream_grad[...] = (b.hidden_grad[...] + extra).astype(low)
@@ -1109,15 +1222,19 @@
             there = (y + dy) % 4, (c + dc) % 2
             steps.append((there, (y + 4 - dy) % 4 * 2 + (c + 2 - dc) % 2))
         finish = all_sum(0, b.shard_sums, s, steps, lambda t: device(x, t[0], z, t[1]))
-        for n in (BOTH, DOWN):
-            rings[n][1].second()
+        rings[KV][0].second()
         for n in (QUERY, OUTPUT):
             rings[n][0].third()
             rings[n][1].first()
+        for n in (BOTH, DOWN):
+            rings[n][1].second()
         b.own_sums[1] = finish()
         turns = lambda at: [((at + d) % 4, (at + 4 - d) % 4) for d in (1, 2, 3)]
         finish = all_sum(1, b.z_sums, z, turns(z), lambda t: device(x, y, t, c))
-        rings[KV][0].second()
+        rings[KV][0].third()
+        rings[KV][1].first()
+        for n in (QUERY, OUTPUT):
+            rings[n][1].second()
 
         def spread(source, box):
             pushes = []
@@ -1145,20 +1262,15 @@
             for j in range(tiles):
                 write(j, b.flat[pl.ds(j, 9, tiles), :])
 
+        rings[KV][1].second()
         for n in (BOTH, DOWN):
             rings[n][1].third()
         flatten(held[BOTH][0].at[x, z], b.both_give)
         got_both = spread(b.both_give, o.both_rows)
-        o.down_grad[...] = held[DOWN][0][x, z].astype(wide)
+        for n in (QUERY, OUTPUT):
+            rings[n][1].third()
         b.own_sums[2] = finish()
         finish = all_sum(2, b.x_sums, x, turns(x), lambda t: device(t, y, z, c))
-        rings[KV][0].third()
-        rings[KV][1].first()
-        for n in (QUERY, OUTPUT):
-            rings[n][1].second()
-        rings[KV][1].second()
-        for n in (QUERY, OUTPUT):
-            rings[n][1].third()
         flatten(held[QUERY][0].at[x, z], b.query_give)
         got_query = spread(b.query_give, b.query_take)
         for d in range(8):
@@ -1167,6 +1279,7 @@
         rings[KV][1].third()
         flatten(held[KV][0].at[x, z], b.kv_give)
         got_kv = spread(b.kv_give, b.kv_take)
+        o.down_grad[...] = held[DOWN][0][x, z].astype(wide)
         o.sums[...] = finish()
 
         def over_y(box, core):
@@ -1200,8 +1313,8 @@
 
     ins = list(arrays.values())
     out = call(
-        kernel, "attend_back", number, list(results.values()), ins, list(room.values()) + sum(stores, []), 5 * 8 + 3 + 2 + 13 + 28,
-        in_specs=[VMEM] * (len(ins) - 2) + [ANY] * 2, out_specs=[VMEM] * len(results), local=2,
+        kernel, "attend_back", number, list(results.values()), ins, [pltpu.VMEM(arrays[n].shape, arrays[n].dtype) for n in held_names] + list(room.values()) + sum(stores, []), 5 * 8 + 3 + 2 + 13 + 28,
+        out_specs=[VMEM] * len(results), local=len(ins),
     )
     return dict(zip(results, out))
 
@@ -1215,31 +1328,26 @@
     stream, doc_starts, cotangent, attention_norm, query_weight, key_weight, value_weight, query_norm, key_norm,
     output_weight, attention_post_norm, mlp_norm, gate_weight, up_weight, down_weight, mlp_post_norm,
 ):
-    own_qkv = jnp.concatenate([query_weight, key_weight, value_weight], axis=1)
     norms = (attention_norm, attention_post_norm, mlp_norm, mlp_post_norm, query_norm, key_norm)
-    own_gains = jnp.concatenate([jnp.pad(g, (0, 16 - g.shape[0])) for g in norms] + [jnp.zeros((32,), jnp.bfloat16)])
-    own_gains = jnp.broadcast_to(own_gains.astype(jnp.float32)[None], (8, 128))
+    own_gains = jnp.concatenate([jnp.pad(g, (0, 16 - g.shape[0])) for g in norms] + [jnp.zeros((32 + 3 * 128,), jnp.bfloat16)])
+    own_kv = jnp.concatenate([key_weight, value_weight], axis=1).reshape(36, 128)
+    own_kv = jnp.concatenate([own_kv, own_gains.reshape(4, 128)], axis=0)
     own_both = jnp.concatenate([split_hidden(gate_weight), split_hidden(up_weight)], axis=2)
-    (
-        normed, query_proj, key_proj, query_rot, kv, probability, mixed, branch, hidden, feed,
-        gain_rows, cosine, sine, full_qkv, full_output, both16, down16,
-    ) = attend(
-        0, stream[0], doc_starts, own_qkv.reshape(108, 128), own_gains, output_weight, own_both.reshape(8, 126, 128),
-        down_weight,
+    ahead, (both16, down16, feeds_a) = attend(
+        0, stream[0], doc_starts, query_weight.reshape(72, 128), own_kv, output_weight,
+        own_both.reshape(8, 126, 128), down_weight,
     )
-    full_both = both16.reshape(D, 2 * WIDE)
-    full_down = jnp.pad(down16.reshape(16, PIECE, D), ((0, 0), (0, SLOT - PIECE), (0, 0))).reshape(WIDE, D)
 
     block_output, feed_grad, gain_mlp_post_grad, result_squares, both_term, down_term = feed_forward(
-        "feed_forward", 1, feed, full_both, full_down, hidden, cotangent[0], gain_rows[3:4]
+        1, ahead.feed, feeds_a, both16.reshape(D, 2 * WIDE), down16, ahead.hidden, cotangent[0], ahead.gains
     )
 
+    named = vars(ahead)
+    del named["feed"]
     back = SimpleNamespace(**attend_back(
         2,
         dict(
-            feed_grad=feed_grad, hidden=hidden, branch=branch, cotangent=cotangent[0], stream=stream[0],
-            normed=normed, query=query_proj, key=key_proj, turned=query_rot, kv=kv, probs=probability, mixed=mixed,
-            gains=gain_rows, cosine=cosine, sine=sine, qkv_weight=full_qkv, output_weight=full_output,
+            **named, feed_grad=feed_grad, cotangent=cotangent[0], stream=stream[0],
             post_grad=gain_mlp_post_grad, result_squares=result_squares,
             both_term=both_term.reshape(4, 4, 72, 2 * WIDE),
             down_term=down_term.reshape(16, SLOT, D)[:, :PIECE].reshape(4, 4, PIECE, D),

time: 298 us -> 283 us (0.950)
  Pallas kernels: 275 us -> 264 us
  local copies, waits for them, and re-layouts: 20.8 us -> 16.6 us
    pallas_call x3, Pallas kernels: 275 us -> 264 us  [call(): pl.pallas_call(kernel, name=name, out_shape=outs, in_specs=in_specs or [A...]
    pad x1 -> x0, local copies, waits for them, and re-layouts: 3.07 us -> none  [local(): jnp.pad(down16.reshape(16, PIECE, D), ((0, 0), (0, SLOT - PIECE), (0, 0)))]
where the time goes in v5:
time: 283 us
  Pallas kernels  264 us (93%)
  local copies, waits for them, and re-layouts  16.6 us (6%)
    pallas_call x3, Pallas kernels, call(): pl.pallas_call(kernel, name=name, out_shape=outs, in_specs=in_specs or [A...  264 us

profile of v5, /device:TPU:1, one launch (start us, length us, event | category | flops | bytes accessed | tf_op | source)
XLA Modules:
  0.0 282.6 jit_solution(12199973038566025377)
XLA Ops:
  0.6 1.7 reshape.88
  2.3 0.0 copy-start.9
  2.3 0.0 copy-start.10
  2.3 0.0 copy-start.11
  2.3 0.0 copy-start.12
  2.4 0.0 copy-start.13
  2.4 0.0 copy-start.14
  2.4 0.0 copy-start.15
  2.4 0.0 copy-start.16
  2.4 0.0 copy-start.5
  2.5 0.1 pad.33
  2.5 0.3 reshape.89
  2.8 1.7 reshape.90
  4.6 0.1 pad.34
  4.6 0.3 reshape.91
  5.0 0.7 copy.42.both_in
  5.7 0.0 copy-done.9
  5.7 0.0 copy-done.10
  5.7 0.0 copy-done.11
  5.8 0.0 copy-done.12
  5.8 0.0 copy-done.13
  5.8 0.0 copy-done.14
  5.8 0.0 copy-done.15
  5.9 0.0 copy-done.16
  5.9 0.1 concatenate.13
  6.0 0.6 pad_maximum_fusion.2.kv_in
  6.6 0.0 copy-done.5
  6.6 0.6 reshape.85.query_in
  7.2 87.7 %attend.1 = (bf16[256,1152]{1,0:T(8,128)(2,1)}, f32[1024,256]{1,0:T(8,128)}, f32[256,256]{1,0:T(8,128)}, bf16[1024,256]{1,0:T(8,128)(2,1)}, bf16[768,512]{1,0:T(...) custom-call(bf16[256,1152]{1,0:T(8,128)(2,1)} %bitcast.56, ...), custom_call_target="tpu_custom_call" | custom-call | tf_op jit(solution)/shard_map/attend/pallas_call | solution.py:165
  94.9 95.2 %feed_forward.1 = (bf16[256,1152]{1,0:T(8,128)(2,1)}, f32[256,1152]{1,0:T(8,128)}, f32[1,1152]{1,0:T(1,128)}, f32[1,1152]{1,0:T(1,128)}, bf16[1152,1792]{1,0:T(8,128)(2,1)}, /*index=5*/bf16[896,1152]{1,0:T(8,128)(2,1)}) custom-call(bf16[256,1152]{1,0:T(8,128)(2,1)} %get-tuple-element.48.feed_in, bf16[8,128,1152]{2,1,0:T(8,128)(2,1)} %get-tuple-element.49.feeds_in, ...), custom_call_target="tpu_custom_call" | custom-call | tf_op jit(solution)/shard_map/feed_forward/pallas_call | solution.py:165
  190.2 80.7 %attend_back.1 = (bf16[256,1152]{1,0:T(8,128)(2,1)}, bf16[8,126,128]{2,1,0:T(8,128)(2,1)}, f32[9,1024]{1,0:T(8,128)}, f32[9,256]{1,0:T(8,128)}, f32[9,256]{1,0:T...) custom-call(bf16[256,1152]{1,0:T(8,128)(2,1)} %get-tuple-element.55.refs_0_, ...), custom_call_target="tpu_custom_call" | custom-call | tf_op jit(solution)/shard_map/attend_back/pallas_call | solution.py:165
  270.9 1.1 copy.43
  272.1 0.5 reshape.98
  272.6 0.2 copy.44
  272.8 0.0 copy-start.8
  272.8 0.0 copy-start
  272.8 1.2 reshape.100
  274.0 0.5 reshape.99
  274.5 0.0 copy-start.3
  274.5 0.0 copy-start.7
  274.5 0.0 copy-start.6
  274.6 0.0 copy-start.4
  274.6 0.0 copy-start.2
  274.6 0.2 copy.45
  274.8 1.2 reshape.101
  275.9 0.0 copy-done.8
  276.0 0.6 fusion
  276.5 0.1 constant_dynamic-slice_fusion.2
  276.6 0.5 slice_bitcast_fusion
  277.2 0.1 bitcast_reduce_fusion
  277.3 0.5 multiply_sqrt_fusion
  277.8 0.0 copy-done
  277.8 0.8 copy.57
  278.6 0.0 copy-done.1
  278.6 0.8 copy.58
  279.4 0.0 copy-done.3
  279.4 0.6 copy.59
  280.1 0.0 copy-done.7
  280.1 0.6 copy.60
  280.7 0.0 copy-done.6
  280.7 0.6 copy.61
  281.3 0.0 copy-done.4
  281.3 0.6 copy.62
  281.9 0.7 copy.63
  (20 shorter events, 0.3 us)
Async XLA Ops:
  2.3 3.4 %copy-start.9 = (bf16[9,256]{1,0:T(8,128)(2,1)S(1)}, bf16[9,256]{1,0:T(8,128)(2,1)}, u32[]{:S(2)}) copy-start(bf16[9,256]{1,0:T(8,128)(2,1)} %param.22) | copy-start | bytes 13828
  2.3 3.4 %copy-start.10 = (bf16[9,256]{1,0:T(8,128)(2,1)S(1)}, bf16[9,256]{1,0:T(8,128)(2,1)}, u32[]{:S(2)}) copy-start(bf16[9,256]{1,0:T(8,128)(2,1)} %param.21) | copy-start | bytes 13828
  2.3 3.4 %copy-start.11 = (bf16[9]{0:T(256)(128)(2,1)S(1)}, bf16[9]{0:T(256)(128)(2,1)}, u32[]{:S(2)}) copy-start(bf16[9]{0:T(256)(128)(2,1)} %param.19) | copy-start | bytes 58
  2.3 3.4 %copy-start.12 = (bf16[9]{0:T(256)(128)(2,1)S(1)}, bf16[9]{0:T(256)(128)(2,1)}, u32[]{:S(2)}) copy-start(bf16[9]{0:T(256)(128)(2,1)} %param.26) | copy-start | bytes 58
  2.4 3.4 %copy-start.13 = (bf16[9]{0:T(256)(128)(2,1)S(1)}, bf16[9]{0:T(256)(128)(2,1)}, u32[]{:S(2)}) copy-start(bf16[9]{0:T(256)(128)(2,1)} %param.27) | copy-start | bytes 58
  2.4 3.5 %copy-start.14 = (bf16[9]{0:T(256)(128)(2,1)S(1)}, bf16[9]{0:T(256)(128)(2,1)}, u32[]{:S(2)}) copy-start(bf16[9]{0:T(256)(128)(2,1)} %param.31) | copy-start | bytes 58
  2.4 3.5 %copy-start.15 = (bf16[2]{0:T(256)(128)(2,1)S(1)}, bf16[2]{0:T(256)(128)(2,1)}, u32[]{:S(2)}) copy-start(bf16[2]{0:T(256)(128)(2,1)} %param.23) | copy-start | bytes 16
  2.4 3.5 %copy-start.16 = (bf16[2]{0:T(256)(128)(2,1)S(1)}, bf16[2]{0:T(256)(128)(2,1)}, u32[]{:S(2)}) copy-start(bf16[2]{0:T(256)(128)(2,1)} %param.24) | copy-start | bytes 16
  2.4 4.2 %copy-start.5 = (bf16[9,1024]{1,0:T(8,128)(2,1)S(1)}, bf16[9,1024]{1,0:T(8,128)(2,1)}, u32[]{:S(2)}) copy-start(bf16[9,1024]{1,0:T(8,128)(2,1)} %param.20) | copy-start | bytes 55300
  272.8 3.2 %copy-start.8 = (f32[8,1152]{1,0:T(8,128)S(1)}, f32[8,1152]{1,0:T(8,128)}, u32[]{:S(2)}) copy-start(f32[8,1152]{1,0:T(8,128)} %get-tuple-element.73) | copy-start | bytes 110596
  272.8 5.0 %copy-start = (bf16[256,1152]{1,0:T(8,128)(2,1)S(1)}, bf16[256,1152]{1,0:T(8,128)(2,1)}, u32[]{:S(2)}) copy-start(bf16[256,1152]{1,0:T(8,128)(2,1)} %get-tuple-element.54) | copy-start | bytes 1769476
  274.0 4.6 %copy-start.1 = (bf16[256,1152]{1,0:T(8,128)(2,1)S(1)}, bf16[256,1152]{1,0:T(8,128)(2,1)}, u32[]{:S(2)}) copy-start(bf16[256,1152]{1,0:T(8,128)(2,1)} %get-tuple-element.72) | copy-start | bytes 1769476
  274.5 4.9 %copy-start.3 = (f32[9,1024]{1,0:T(8,128)S(1)}, f32[9,1024]{1,0:T(8,128)}, u32[]{:S(2)}) copy-start(f32[9,1024]{1,0:T(8,128)} %get-tuple-element.109) | copy-start | bytes 110596
  274.5 5.5 %copy-start.7 = (f32[9,256]{1,0:T(8,128)S(1)}, f32[9,256]{1,0:T(8,128)}, u32[]{:S(2)}) copy-start(f32[9,256]{1,0:T(8,128)} %get-tuple-element.110) | copy-start | bytes 27652
  274.5 6.1 %copy-start.6 = (f32[9,256]{1,0:T(8,128)S(1)}, f32[9,256]{1,0:T(8,128)}, u32[]{:S(2)}) copy-start(f32[9,256]{1,0:T(8,128)} %get-tuple-element.111) | copy-start | bytes 27652
  274.6 6.7 %copy-start.4 = (f32[8,1152]{1,0:T(8,128)S(1)}, f32[8,1152]{1,0:T(8,128)}, u32[]{:S(2)}) copy-start(f32[8,1152]{1,0:T(8,128)} %get-tuple-element.114) | copy-start | bytes 110596
  274.6 7.3 %copy-start.2 = (f32[54,1152]{1,0:T(8,128)S(1)}, f32[54,1152]{1,0:T(8,128)}, u32[]{:S(2)}) copy-start(f32[54,1152]{1,0:T(8,128)} %get-tuple-element.119) | copy-start | bytes 746500

commit v6 on v5

--- a/solution.py
+++ b/solution.py
@@ -102,6 +102,52 @@
         for push in (self.right, self.left, self.right2, self.left2):
             if push is not None:
                 push.sent()
+
+
+class DirectGather:
+    def __init__(self, own, slot, half, me, peer, sems):
+        self.pushes = [
+            Push(own, slot(me), sems, peer((me + d) % 4), slot((me + 4 - d) % 4)) for d in (1, 3, 2)
+        ]
+
+    def first(self):
+        for push in self.pushes:
+            push.start()
+
+    def relay(self):
+        for push in self.pushes[:2]:
+            push.arrived()
+
+    def last(self):
+        self.pushes[2].arrived()
+
+    def close(self):
+        for push in self.pushes:
+            push.sent()
+
+
+class DirectSum:
+    def __init__(self, chunk, half, inbox, me, peer, sems, add):
+        self.total, self.inbox, self.add = chunk(me), inbox[:3], add
+        self.pushes = [
+            Push(chunk((me + d) % 4), box, sems, peer((me + d) % 4)) for d, box in zip((2, 1, 3), self.inbox)
+        ]
+
+    def first(self):
+        for push in self.pushes:
+            push.start()
+
+    def second(self):
+        pass
+
+    def third(self):
+        for push, box in zip(self.pushes, self.inbox):
+            push.arrived()
+            self.add(self.total, box)
+
+    def close(self):
+        for push in self.pushes:
+            push.sent()
 
 
 class RingSum:
@@ -210,7 +256,7 @@
         feed_in, feeds_in, both_in, down_in, hidden_in, cotangent_in, gains_in,
         block_out, feed_out, gain_out, square_out, both_out, down_out,
         feeds, downs, both, active, part, inbox, near, right, left, w_both, w_down, raw, pad, both_term, down_term,
-        send, recv, here,
+        far_a, far_b, right4, left4, send, recv, here,
     ):
         x, y, z, c = place()
         sems = Sems(send, recv)
@@ -226,7 +272,10 @@
         ]
         for load in loads:
             load.start()
-        greet([to(1), to(3), other])
+        greet(
+            [to(1), to(3), other, device(x, y, z + 1, c), device(x, y, z + 3, c)]
+            + [device(x + 1, y, z, c), device(x + 3, y, z, c)]
+        )
 
         def gather(source, blocks, s):
             slot = lambda k: blocks.at[s, k * 2 + c]
@@ -407,10 +456,10 @@
                     value += down_term[units, :].astype(jnp.float32)
                 down_term[units, :] = value.astype(jnp.bfloat16)
 
-        def both_terms(s):
+        def both_terms(s, low=0, high=width // 128):
             every = 8 * rows
 
-            @pl.loop(0, width // 128)
+            @pl.loop(low, high)
             def _(i):
                 lanes = pl.ds(pl.multiple_of(i * 128, 128), 128)
                 value = dot(feeds[s, :, :, lanes].reshape(every, 128), both[s].reshape(every, 2 * WIDE), 0, 0)
@@ -443,6 +492,20 @@
             last_b()
             met_b[1]()
 
+        down_ring = sum_row(raw, (far_a, far_b, right4, left4), sems)
+
+        def start_down():
+            down_terms(b)
+
+            @pl.loop(0, 8)
+            def _(i):
+                both_slots = down_term[pl.ds(pl.multiple_of(2 * SLOT * i, 16), 2 * SLOT), :].astype(jnp.float32)
+                for k in range(2):
+                    slot = both_slots[SLOT * k : SLOT * k + PIECE].astype(jnp.bfloat16)
+                    raw[i // 2, i % 2 * 2 + k] = slot
+
+            down_ring.first()
+
         steps(
             backward,
             {0: met_a[0], 1: back_1, 2: back_2, 3: met_a[2], 4: back_4, 5: back_5, 6: met_b[3], 7: met_b[2]},
@@ -450,23 +513,27 @@
         )
         sum_b.far()
         sum_b.sides()
-        down_terms(b)
-        saves = [
-            pltpu.make_async_copy(down_term, down_out, here.at[0]),
-            pltpu.make_async_copy(both_term, both_out, here.at[1]),
-        ]
-        saves[0].start()
+        start_down()
         sum_b.go()
         feed_out[span(a), :] = sum_a.final()
-        both_terms(b)
-        saves[1].start()
+        both_terms(b, 0, 4)
+        down_ring.second()
+        both_terms(b, 4)
+        save = pltpu.make_async_copy(both_term, both_out, here.at[1])
+        save.start()
         feed_out[span(b), :] = sum_b.final()
+        down_ring.third()
+        rows_out = [pltpu.make_async_copy(row, down_out, here.at[0]) for row in (raw.at[:, z], raw.at[x])]
+        for core in (0, 1):
+            pl.when(c == core)(rows_out[core].start)
+        down_ring.close()
         sum_a.close()
         sum_b.close()
         close_a()
         close_b()
-        for save in saves:
-            save.wait()
+        save.wait()
+        for core in (0, 1):
+            pl.when(c == core)(rows_out[core].wait)
 
     low, wide = jnp.bfloat16, jnp.float32
     blocks = (SUBS, 8, rows)
@@ -486,6 +553,10 @@
         pltpu.VMEM((2 * SLOT, width), wide),
         pltpu.VMEM((width, 2 * WIDE), low),
         pltpu.VMEM((WIDE, width), low),
+        pltpu.VMEM((2, PIECE, width), low),
+        pltpu.VMEM((2, PIECE, width), low),
+        pltpu.VMEM((4, PIECE, width), low),
+        pltpu.VMEM((4, PIECE, width), low),
     ]
     outs = [
         ((tokens, width), low),
@@ -493,11 +564,11 @@
         ((1, width), wide),
         ((1, width), wide),
         ((width, 2 * WIDE), low),
-        ((WIDE, width), low),
+        ((4, PIECE, width), low),
     ]
     return call(
         kernel, "feed_forward", number, outs, [feed, feeds_a, full_both, down16, hidden, cotangent, gains], scratch,
-        32 * SUBS - 8, in_specs=[ANY] * 4 + [VMEM] * 3, out_specs=[VMEM] * 4 + [ANY] * 2, local=4,
+        32 * SUBS - 8 + 4, in_specs=[ANY] * 4 + [VMEM] * 3, out_specs=[VMEM] * 4 + [ANY] * 2, local=4,
     )
 
 
@@ -528,18 +599,18 @@
     return ref
 
 
-def ring_row(own, out, cut, sems):
+def ring_row(own, out, cut, sems, kind=RingGather):
     x, y, z, c = place()
 
     def make(order):
         slot = (lambda k: cut(out.at[x, k])) if order == 0 else (lambda k: cut(out.at[k, z]))
         peer = (lambda k: device(x, y, k, c)) if order == 0 else (lambda k: device(k, y, z, c))
-        return RingGather(own, slot, lambda k, h: split_lanes(slot(k), h), (z, x)[order], peer, sems)
+        return kind(own, slot, lambda k, h: split_lanes(slot(k), h), (z, x)[order], peer, sems)
 
     return Either(c, sems, make)
 
 
-def ring_rest(out, cut, sems, lean=False):
+def ring_rest(out, cut, sems, lean=False, kind=RingGather):
     x, y, z, c = place()
 
     def make(order):
@@ -550,7 +621,7 @@
             if lean:
                 half = lambda k, h: slot(k) if h else None
         peer = (lambda k: device(k, y, z, c)) if order == 0 else (lambda k: device(x, y, k, c))
-        return RingGather(slot(me), slot, half, me, peer, sems)
+        return kind(slot(me), slot, half, me, peer, sems)
 
     return Either(c, sems, make)
 
@@ -613,7 +684,7 @@
     return lambda ref: ref.at[(slice(None),) * (len(ref.shape) - 1) + (pl.ds(start, size),)]
 
 
-def attend(number, stream, doc_starts, own_query, own_kv, own_output, own_both, own_down):
+def attend(number, stream, doc_starts, own_query, own_key, own_value, own_output, own_gate, own_up, own_down, norms):
     tokens = stream.shape[0]
     span = tokens + WINDOW
 
@@ -637,9 +708,9 @@
     )
 
     def kernel(
-        stream_in, starts_in, query_in, kv_in, output_in, both_in, down_in, *refs
+        stream_in, starts_in, query_in, key_in, value_in, output_in, gate_in, up_in, down_in, *refs
     ):
-        refs = list(refs)
+        norms_in, refs = refs[: len(norms)], list(refs[len(norms) :])
 
         def take(count):
             taken, refs[:] = refs[:count], refs[count:]
@@ -649,7 +720,7 @@
         both_out, down_out, feeds_out = take(3)
         v = SimpleNamespace(**dict(zip(keep, take(len(keep)))))
         (
-            query_box, kv_box, both_box, flat, merge, query_own, kv_own, both_own, query_all, kv_all, output_all, kv,
+            query_give, kv_give, query_box, kv_box, both_box, both_give, flat, merge, query_own, kv_own, both_own, query_all, kv_all, output_all, kv,
             owns9, owns2,
             send, recv, here,
         ) = refs
@@ -663,9 +734,20 @@
         q, s = lax.axis_index("seq"), lax.axis_index("shard")
         sems = Sems(send, recv)
         after, before = {"seq": (q + 1) % 16, "shard": s}, {"seq": (q + 15) % 16, "shard": s}
+        for j in range(8):
+            flat[pl.ds(j, 9, 8), :] = query_in[:, 128 * j : 128 * (j + 1)].astype(jnp.float32)
+        query_give[...] = flat[:72, :].astype(jnp.bfloat16)
+        for at, source in enumerate((key_in, value_in)):
+            for j in range(2):
+                flat[pl.ds(2 * at + j, 9, 4), :] = source[:, 128 * j : 128 * (j + 1)].astype(jnp.float32)
+        flat[36:40, :] = jnp.zeros((4, 128), jnp.float32)
+        for g, source in enumerate(norms_in):
+            flat[36:37, 16 * g : 16 * g + source.shape[1]] = source[...].astype(jnp.float32)
+        kv_give[...] = flat[:40, :].astype(jnp.bfloat16)
         greet(
             [device(x, y + dy, z, (c + dc) % 2) for dy, dc in SHARD_STEPS]
-            + [device(x, y, z + 1, c), device(x, y, z + 3, c), device(x + 1, y, z, c), device(x + 3, y, z, c)]
+            + [device(x, y, z + d, c) for d in (1, 2, 3)]
+            + [device(x + d, y, z, c) for d in (1, 2, 3)]
             + [after, before]
         )
         sent = []
@@ -702,10 +784,10 @@
         my_kv, their_kv = halves(256)
         mine = lambda ref: ref.at[(slice(None),) * (len(ref.shape) - 3) + (s,)]
 
-        got_kv = spread(kv_in, kv_box)
-        got_query = spread(query_in, query_box)
+        got_kv = spread(kv_give, kv_box)
+        got_query = spread(query_give, query_box)
         down_ring = ring_row(down_in, down_out, whole_ref, sems)
-        output_ring = ring_row(output_in, output_all, mine, sems)
+        output_ring = ring_row(output_in, output_all, mine, sems, DirectGather)
         down_ring.first()
         output_ring.first()
         inputs = stream_in[...].astype(jnp.float32)
@@ -723,32 +805,54 @@
         pick9, owns9[...] = gain_picks(9, D)
         pick2, owns2[...] = gain_picks(2, HEAD_DIM)
         v.gains[...] = jnp.zeros_like(v.gains)
-        merge[72:80, :] = jnp.zeros((8, merge.shape[1]), jnp.float32)
+        merge[...] = jnp.zeros_like(merge)
+        for d in range(8):
+            for half, source in enumerate((gate_in, up_in)):
+                for i in range(16):
+                    to, start = WIDE * half + SLOT * i, 8 * PIECE * i + PIECE * d
+                    merge[0:9, to : to + PIECE] = source[:, start : start + PIECE].astype(jnp.float32)
+            for j in range(14):
+                flat[pl.ds(j, 9, 14), :] = merge[0:9, 128 * j : 128 * (j + 1)]
+            both_give[d] = flat[:126, :].astype(jnp.bfloat16)
 
         own = lambda src, dst, at: pltpu.make_async_copy(src, dst, here.at[at])
         collect(got_kv, kv_box, kv_own)
-        kv_ring = ring_row(my_kv(kv_own), kv_all, my_kv, sems)
+        kv_ring = ring_row(my_kv(kv_own), kv_all, my_kv, sems, DirectGather)
         kv_ring.first()
+        other = device(x, y, z, 1 - c)
+        column = lambda k: output_all.at[:, :, k * 2 + c]
+        output_y = RingGather(
+            column(y), column, lambda k, h: output_all.at[pl.ds(2 * h, 2), :, k * 2 + c],
+            y, lambda k: device(x, k, z, c), sems,
+        )
+        output_cross = [
+            Push(column((y + d) % 4), column((y + d) % 4), sems, other, output_all.at[:, :, (y + d) % 4 * 2 + 1 - c])
+            for d in range(4)
+        ]
+        own(output_in, output_all.at[x, z, s], 2).start()
         collect(got_query, query_box, query_own)
         query_ring = ring_row(my_query(query_own), query_all, my_query, sems)
         query_ring.first()
-        got_both = spread(both_in, both_box, True)
+        output_ring.relay()
+        output_ring.last()
+        own(output_in, output_all.at[x, z, s], 2).wait()
+        output_rest = ring_rest(output_all, mine, sems, kind=DirectGather)
+        output_rest.first()
+        got_both = spread(both_give, both_box, True)
         copies = [
             own(my_kv(kv_own), my_kv(kv_all.at[x, z]), 0),
             own(down_in, down_out.at[x, z], 1),
-            own(output_in, output_all.at[x, z, s], 2),
             own(my_query(query_own), my_query(query_all.at[x, z]), 3),
         ]
         for copy in copies:
             copy.start()
         down_ring.relay()
-        output_ring.relay()
         kv_ring.relay()
         query_ring.relay()
         for copy in copies:
             copy.wait()
         kv_ring.last()
-        kv_rest = ring_rest(kv_all, my_kv, sems)
+        kv_rest = ring_rest(kv_all, my_kv, sems, kind=DirectGather)
         kv_cross = Crossing(kv_all, my_kv, their_kv, sems)
         kv_rest.first()
         kv_cross.start(0)
@@ -757,14 +861,15 @@
         query_cross = Crossing(query_all, my_query, their_query, sems)
         query_rest.first()
         query_cross.start(0)
+        output_rest.relay()
+        output_rest.last()
+        output_y.first()
+        output_cross[0].start()
         down_ring.last()
-        output_ring.last()
         down_rest = ring_rest(down_out, whole_ref, sems, True)
-        output_rest = ring_rest(output_all, mine, sems)
         kv_rest.relay()
         kv_cross.start(3)
         kv_cross.start(1)
-        output_rest.first()
         collect(got_both, both_box, both_own)
         both_ring = ring_row(both_own, both_out, whole_ref, sems)
         both_ring.first()
@@ -775,7 +880,6 @@
         query_rest.relay()
         query_cross.start(3)
         query_cross.start(1)
-        output_rest.relay()
         down_rest.first()
         table = kv_all[:, :, 72:80, pl.ds(pl.multiple_of(c * 256, 128), 128)].reshape(128, 128)
         for g in range(4):
@@ -804,22 +908,12 @@
         kv[2, :, :HEAD_DIM] = key_turned.astype(jnp.bfloat16)
         kv[2, :, HEAD_DIM:] = key_value[:, HEAD_DIM:].astype(jnp.bfloat16)
         near.start()
+        output_y.relay()
+        output_cross[1].start()
+        output_cross[3].start()
         query_rest.last()
         query_cross.start(2)
         both_ring.relay()
-        output_rest.last()
-        other = device(x, y, z, 1 - c)
-        column = lambda k: output_all.at[:, :, k * 2 + c]
-        output_y = RingGather(
-            column(y), column, lambda k, h: output_all.at[pl.ds(2 * h, 2), :, k * 2 + c],
-            y, lambda k: device(x, k, z, c), sems,
-        )
-        output_cross = [
-            Push(column((y + d) % 4), column((y + d) % 4), sems, other, output_all.at[:, :, (y + d) % 4 * 2 + 1 - c])
-            for d in range(4)
-        ]
-        output_y.first()
-        output_cross[0].start()
         for src, dst in ((v.gains, saved.gains), (v.cosine, saved.cosine), (v.sine, saved.sine)):
             save(src, dst)
         query_cross.close()
@@ -843,9 +937,6 @@
         save(v.key, saved.key)
         near.arrived()
         far.start()
-        output_y.relay()
-        output_cross[1].start()
-        output_cross[3].start()
         both_rest.relay()
         output_y.last()
         output_cross[2].start()
@@ -931,8 +1022,11 @@
         ((8, tokens // SUBS, D), low),
     ]
     scratch = [pltpu.VMEM(shape, kind) for shape, kind in keep.values()] + [
+        pltpu.VMEM((72, 128), low),
+        pltpu.VMEM((40, 128), low),
         pltpu.VMEM((8, 72, 128), low),
         pltpu.VMEM((8, 40, 128), low),
+        pltpu.VMEM((8, 126, 128), low),
         pltpu.VMEM((8, 126, 128), low),
         pltpu.VMEM((128, 128), wide),
         pltpu.VMEM((80, 2 * WIDE), wide),
@@ -947,10 +1041,46 @@
         pltpu.VMEM((128, HEAD_DIM), wide),
     ]
     out = call(
-        kernel, "attend", number, outs, [stream, doc_starts, own_query, own_kv, own_output, own_both, own_down],
-        scratch, 3 * 7 + 11 * 4 + 2 * 4 + 4 + 2 + 4 + 4, in_specs=[VMEM] * 7, local=5 + 16,
+        kernel, "attend", number, outs,
+        [stream, doc_starts, own_query, own_key, own_value, own_output, own_gate, own_up, own_down, *norms],
+        scratch, 3 * 7 + 11 * 4 + 2 * 4 + 4 + 2 + 4 + 4, in_specs=[VMEM] * (9 + len(norms)), local=5 + 16,
     )
     return SimpleNamespace(**dict(zip(keep, out))), out[len(keep) :]
+
+
+def sum_row(total, boxes, sems, lean=False, kind=RingSum):
+    x, y, z, c = place()
+
+    def make(order):
+        if order == 0:
+            chunk, half = lambda k: total.at[:, k], lambda k, h: total.at[pl.ds(2 * h, 2), k]
+            if lean:
+                half = lambda k, h: None if h else chunk(k)
+            me, peer = z, lambda k: device(x, y, k, c)
+        else:
+            chunk, half = lambda k: total.at[k], lambda k, h: total.at[k, pl.ds(2 * h, 2)]
+            me, peer = x, lambda k: device(k, y, z, c)
+        own_boxes = list(boxes)
+        if order == 1 and lean:
+            own_boxes[0] = boxes[0].at[pl.ds(0, 2)]
+        return kind(chunk, half, own_boxes, me, peer, sems, add_into)
+
+    return Either(c, sems, make)
+
+
+def sum_rest(total, boxes, sems, kind=RingSum):
+    x, y, z, c = place()
+
+    def make(order):
+        if len(total.shape) == 3:
+            chunk = lambda k: total.at[k]
+        else:
+            chunk = (lambda k: total.at[k, z]) if order == 0 else (lambda k: total.at[x, k])
+        half = lambda k, h: split_lanes(chunk(k), h)
+        peer = (lambda k: device(k, y, z, c)) if order == 0 else (lambda k: device(x, y, k, c))
+        return kind(chunk, half, boxes, (x, z)[order], peer, sems, add_into)
+
+    return Either(c, sems, make)
 
 
 def norm_grad(values, gain, grad):
@@ -962,33 +1092,16 @@
     )
 
 
-def scatter_rings(total, boxes, sems):
-    x, y, z, c = place()
-    z_peer, x_peer = (lambda k: device(x, y, k, c)), (lambda k: device(k, y, z, c))
-
-    def one(order):
-        if order == 0:
-            chunk, half = lambda k: total.at[:, k], lambda k, h: total.at[pl.ds(2 * h, 2), k]
-        else:
-            chunk, half = lambda k: total.at[k], lambda k, h: total.at[k, pl.ds(2 * h, 2)]
-        return RingSum(chunk, half, boxes[:4], (z, x)[order], (z_peer, x_peer)[order], sems, add_into)
-
-    def two(order):
-        chunk = (lambda k: total.at[k, z]) if order == 0 else (lambda k: total.at[x, k])
-        half = lambda k, h: split_lanes(chunk(k), h)
-        return RingSum(chunk, half, boxes[4:], (x, z)[order], (x_peer, z_peer)[order], sems, add_into)
-
-    return Either(c, sems, one), Either(c, sems, two)
-
-
-def scatter_boxes(rows, width, kind):
+def scatter_boxes(rows, width, kind, row_only=False, lean=False):
     lanes = lane_halves(width)
+    rest = [pltpu.VMEM((rows, size), kind) for _, size in lanes] + [pltpu.VMEM((rows, width), kind)] * 2
+    if row_only:
+        return [pltpu.VMEM((4, rows, width), kind)] + rest
     return (
         [pltpu.VMEM((4, 4, rows, width), kind)]
-        + [pltpu.VMEM((2, rows, width), kind)] * 2
+        + [pltpu.VMEM((4 if lean else 2, rows, width), kind), pltpu.VMEM((2, rows, width), kind)]
         + [pltpu.VMEM((4, rows, width), kind)] * 2
-        + [pltpu.VMEM((rows, size), kind) for _, size in lanes]
-        + [pltpu.VMEM((rows, width), kind)] * 2
+        + rest
     )
 
 
@@ -1015,7 +1128,11 @@
     sizes = {BOTH: (72, 2 * WIDE), DOWN: (PIECE, D), OUTPUT: (64, 640), QUERY: (72, 512), KV: (72, 256)}
     stores = []
     for name, (rows, width) in sizes.items():
-        stores.append(scatter_boxes(rows, width, low))
+        if name == KV:
+            stores.append([pltpu.VMEM((4, 4, rows, width), low)] + [pltpu.VMEM((4, rows, width), low)] * 3)
+            stores[-1] += [pltpu.VMEM((rows, width), low)] * 5
+        else:
+            stores.append(scatter_boxes(rows, width, low, name == DOWN, name == BOTH))
         if name in SHARED:
             stores[-1] += [pltpu.VMEM((4, 4, rows, width), low)] * 2
     room = SimpleNamespace(
@@ -1064,7 +1181,16 @@
         sems = Sems(send, recv)
         other = device(x, y, z, 1 - c)
         after, before = {"seq": (q + 1) % 16, "shard": s}, {"seq": (q + 15) % 16, "shard": s}
-        rings = {n: scatter_rings(held[n][0], held[n][1:9], sems) for n in sizes}
+        rings = {}
+        for n in sizes:
+            if n == DOWN:
+                rings[n] = None, sum_rest(held[n][0], held[n][1:5], sems)
+            elif n == KV:
+                one = sum_row(held[n][0], held[n][1:4], sems, kind=DirectSum)
+                rings[n] = one, sum_rest(held[n][0], held[n][4:7], sems, kind=DirectSum)
+            else:
+                one = sum_row(held[n][0], held[n][1:5], sems, n == BOTH)
+                rings[n] = one, sum_rest(held[n][0], held[n][5:9], sems)
         cross = {n: Push(held[n][GIVE], held[n][TAKE], sems, other) for n in SHARED}
         loads = [
             pltpu.make_async_copy(given[names[-2]], held[BOTH][0], here.at[0]),
@@ -1080,9 +1206,10 @@
             + [device(x + d, y, z, c) for d in (1, 2, 3)]
             + [after, before]
         )
-        for n, load in zip((BOTH, DOWN), loads):
-            load.wait()
-            rings[n][0].first()
+        loads[0].wait()
+        rings[BOTH][0].first()
+        loads[1].wait()
+        rings[DOWN][1].first()
         for load in loads[2:]:
             load.wait()
         gains = a.gains
@@ -1171,8 +1298,8 @@
                         held[OUTPUT][GIVE][block] = value
 
         cross[OUTPUT].start()
-        for n in (BOTH, DOWN):
-            rings[n][0].second()
+        rings[BOTH][0].second()
+        rings[DOWN][1].second()
         halo_far.arrived()
         b.halo_out[1] = (b.kv_grad[tokens : 2 * tokens, :] + b.halo_in[0].astype(wide)).astype(low)
         halo_near.start()
@@ -1193,9 +1320,8 @@
         cross[KV].arrived()
         add_into(held[KV][0], held[KV][TAKE])
         rings[KV][0].first()
-        for n in (BOTH, DOWN):
-            rings[n][0].third()
-            rings[n][1].first()
+        rings[BOTH][0].third()
+        rings[BOTH][1].first()
         normed_grad = dot(b.qkv_low[...], a.qkv_weight[...], 1, 1)
         extra, own[0:1, :] = norm_grad(a.stream[...].astype(wide), gains[0:1, :], normed_grad)
         o.stream_grad[...] = (b.hidden_grad[...] + extra).astype(low)
@@ -1226,8 +1352,8 @@
         for n in (QUERY, OUTPUT):
             rings[n][0].third()
             rings[n][1].first()
-        for n in (BOTH, DOWN):
-            rings[n][1].second()
+        rings[BOTH][1].second()
+        rings[DOWN][1].third()
         b.own_sums[1] = finish()
         turns = lambda at: [((at + d) % 4, (at + 4 - d) % 4) for d in (1, 2, 3)]
         finish = all_sum(1, b.z_sums, z, turns(z), lambda t: device(x, y, t, c))
@@ -1263,8 +1389,7 @@
                 write(j, b.flat[pl.ds(j, 9, tiles), :])
 
         rings[KV][1].second()
-        for n in (BOTH, DOWN):
-            rings[n][1].third()
+        rings[BOTH][1].third()
         flatten(held[BOTH][0].at[x, z], b.both_give)
         got_both = spread(b.both_give, o.both_rows)
         for n in (QUERY, OUTPUT):
@@ -1279,7 +1404,7 @@
         rings[KV][1].third()
         flatten(held[KV][0].at[x, z], b.kv_give)
         got_kv = spread(b.kv_give, b.kv_take)
-        o.down_grad[...] = held[DOWN][0][x, z].astype(wide)
+        o.down_grad[...] = held[DOWN][0][x + c * (z + 4 - x) - 4 * c].astype(wide)
         o.sums[...] = finish()
 
         def over_y(box, core):
@@ -1307,21 +1432,55 @@
             push.arrived()
         for pair in rings.values():
             for ring in pair:
-                ring.close()
+                if ring is not None:
+                    ring.close()
         for push in list(cross.values()) + pending + [halo_far, halo_near]:
             push.sent()
 
     ins = list(arrays.values())
     out = call(
-        kernel, "attend_back", number, list(results.values()), ins, [pltpu.VMEM(arrays[n].shape, arrays[n].dtype) for n in held_names] + list(room.values()) + sum(stores, []), 5 * 8 + 3 + 2 + 13 + 28,
+        kernel, "attend_back", number, list(results.values()), ins, [pltpu.VMEM(arrays[n].shape, arrays[n].dtype) for n in held_names] + list(room.values()) + sum(stores, []), 4 * 8 + 4 + 3 + 2 + 13 + 28,
         out_specs=[VMEM] * len(results), local=len(ins),
     )
     return dict(zip(results, out))
 
 
-def split_hidden(weight):
-    parts = weight.reshape(9, 16, 8, PIECE).transpose(2, 0, 1, 3)
-    return jnp.pad(parts, ((0, 0), (0, 0), (0, 0), (0, SLOT - PIECE))).reshape(8, 9, WIDE)
+def finish(both_rows, sums, *arrays):
+    def kernel(rows, sums, *refs):
+        sources, refs = refs[: len(arrays)], refs[len(arrays) :]
+        gate, up, *small = refs[:9]
+        copies, (merge, flat) = refs[9:-2], refs[-2:]
+        own = lax.axis_index("seq") * 8 + lax.axis_index("shard")
+        for g in range(4):
+            small[g][...] = pltpu.roll(sums[...], D - 9 * own, 1)[g : g + 1, :9]
+        for g in range(2):
+            start = HEAD_DIM * g + 2 * own
+            small[4 + g][...] = pltpu.roll(sums[...], D - start, 1)[4:5, :2]
+        for at in range(3):
+            total = jnp.sum(sums[4:5, 512 + 128 * at : 640 + 128 * at], axis=1, keepdims=True)
+            small[6][:, at : at + 1] = jnp.sqrt(total / (32768 * D))
+        for source, copy in zip(sources, copies):
+            copy[...] = source[...]
+        for d in range(8):
+            flat[:126, :] = rows[d].astype(jnp.float32)
+            for j in range(14):
+                merge[0:9, 128 * j : 128 * (j + 1)] = flat[pl.ds(j, 9, 14), :]
+            for half, out in enumerate((gate, up)):
+                for i in range(16):
+                    start, to = WIDE * half + SLOT * i, 8 * PIECE * i + PIECE * d
+                    out[:, to : to + PIECE] = merge[0:9, start : start + PIECE]
+
+    return pl.pallas_call(
+        kernel,
+        name="finish",
+        out_shape=[jax.ShapeDtypeStruct((9, FF), jnp.float32)] * 2
+        + [jax.ShapeDtypeStruct((1, n), jnp.float32) for n in (9, 9, 9, 9, 2, 2, 3)]
+        + [jax.ShapeDtypeStruct(a.shape, a.dtype) for a in arrays],
+        in_specs=[VMEM] * (2 + len(arrays)),
+        out_specs=[VMEM] * (9 + len(arrays)),
+        scratch_shapes=[pltpu.VMEM((16, 2 * WIDE), jnp.float32), pltpu.VMEM((128, 128), jnp.float32)],
+        compiler_params=pltpu.CompilerParams(vmem_limit_bytes=60 * MIB),
+    )(both_rows, sums, *arrays)
 
 
 def local(
@@ -1329,16 +1488,12 @@
     output_weight, attention_post_norm, mlp_norm, gate_weight, up_weight, down_weight, mlp_post_norm,
 ):
     norms = (attention_norm, attention_post_norm, mlp_norm, mlp_post_norm, query_norm, key_norm)
-    own_gains = jnp.concatenate([jnp.pad(g, (0, 16 - g.shape[0])) for g in norms] + [jnp.zeros((32 + 3 * 128,), jnp.bfloat16)])
-    own_kv = jnp.concatenate([key_weight, value_weight], axis=1).reshape(36, 128)
-    own_kv = jnp.concatenate([own_kv, own_gains.reshape(4, 128)], axis=0)
-    own_both = jnp.concatenate([split_hidden(gate_weight), split_hidden(up_weight)], axis=2)
     ahead, (both16, down16, feeds_a) = attend(
-        0, stream[0], doc_starts, query_weight.reshape(72, 128), own_kv, output_weight,
-        own_both.reshape(8, 126, 128), down_weight,
+        0, stream[0], doc_starts, query_weight, key_weight, value_weight, output_weight, gate_weight, up_weight,
+        down_weight, [norm[None] for norm in norms],
     )
 
-    block_output, feed_grad, gain_mlp_post_grad, result_squares, both_term, down_term = feed_forward(
+    block_output, feed_grad, gain_mlp_post_grad, result_squares, both_term, down_row = feed_forward(
         1, ahead.feed, feeds_a, both16.reshape(D, 2 * WIDE), down16, ahead.hidden, cotangent[0], ahead.gains
     )
 
@@ -1350,37 +1505,32 @@
             **named, feed_grad=feed_grad, cotangent=cotangent[0], stream=stream[0],
             post_grad=gain_mlp_post_grad, result_squares=result_squares,
             both_term=both_term.reshape(4, 4, 72, 2 * WIDE),
-            down_term=down_term.reshape(16, SLOT, D)[:, :PIECE].reshape(4, 4, PIECE, D),
+            down_row=down_row,
         ),
     ))
 
-    def whole(rows):
-        parts = rows.reshape(8, 9, 16, SLOT)[..., :PIECE]
-        return parts.transpose(1, 2, 0, 3).reshape(9, FF).astype(jnp.float32)
-
-    both_rows = back.both_rows.reshape(8, 9, 2 * WIDE)
-    sums = back.sums
-    own = lax.axis_index("seq") * 8 + lax.axis_index("shard")
-    gain_grads = lax.dynamic_slice_in_dim(sums[:4], own * 9, 9, 1)
-    query_gain_grad = lax.dynamic_slice_in_dim(sums[4, :HEAD_DIM], own * 2, 2, 0)
-    key_gain_grad = lax.dynamic_slice_in_dim(sums[4, HEAD_DIM : 2 * HEAD_DIM], own * 2, 2, 0)
-    stream_rms = jnp.sqrt(jnp.sum(sums[4, 512:896].reshape(3, 128), axis=1) / (32768 * D))
+    gate_grad, up_grad, *rest = finish(
+        back.both_rows, back.sums, block_output, back.stream_grad, back.query_grad, back.key_grad, back.value_grad,
+        back.output_grad, back.down_grad,
+    )
+    small, (block_output, stream_grad, query_grad, key_grad, value_grad, output_grad, down_grad) = rest[:7], rest[7:]
+    input_gain, post_gain, mlp_gain, mlp_post_gain, query_gain, key_gain, stream_rms = [value[0] for value in small]
     return (
         block_output[None],
-        back.stream_grad[None],
-        gain_grads[0],
-        back.query_grad,
-        back.key_grad,
-        back.value_grad,
-        query_gain_grad,
-        key_gain_grad,
-        back.output_grad,
-        gain_grads[1],
-        gain_grads[2],
-        whole(both_rows[:, :, :WIDE]),
-        whole(both_rows[:, :, WIDE:]),
-        back.down_grad,
-        gain_grads[3],
+        stream_grad[None],
+        input_gain,
+        query_grad,
+        key_grad,
+        value_grad,
+        query_gain,
+        key_gain,
+        output_grad,
+        post_gain,
+        mlp_gain,
+        gate_grad,
+        up_grad,
+        down_grad,
+        mlp_post_gain,
         stream_rms,
     )
 

time: 283 us -> 262 us (0.926)
  local copies, waits for them, and re-layouts: 16.6 us -> 0 us
  Pallas kernels: 264 us -> 261 us
    pallas_call x3, Pallas kernels: 264 us -> 257 us  [call(): pl.pallas_call(kernel, name=name, out_shape=outs, in_specs=in_specs or [A...]
    reshape x11 -> x0, local copies, waits for them, and re-layouts: 6.35 us -> none  [the longest x4 3.39 us: split_hidden(): parts = weight.reshape(9, 16, 8, PIECE).transpose(2, 0, 1, 3)]
    unnamed x41 -> x0, local copies, waits for them, and re-layouts: 4.87 us -> none
    pallas_call x0 -> x1, Pallas kernels: none -> 3.81 us  [finish(): pl.pallas_call(kernel, name='finish', out_shape=[jax.ShapeDtypeStruct((9,...]
where the time goes in v6:
time: 262 us
  Pallas kernels  261 us (100%)
    pallas_call x3, Pallas kernels, call(): pl.pallas_call(kernel, name=name, out_shape=outs, in_specs=in_specs or [A...  257 us

profile of v6, /device:TPU:1, one launch (start us, length us, event | category | flops | bytes accessed | tf_op | source)
XLA Modules:
  0.0 261.5 jit_solution(7758949714307491671)
XLA Ops:
  0.7 85.4 %attend.1 = (bf16[256,1152]{1,0:T(8,128)(2,1)}, f32[1024,256]{1,0:T(8,128)}, f32[256,256]{1,0:T(8,128)}, bf16[1024,256]{1,0:T(8,128)(2,1)}, bf16[768,512]{1,0:T(...) custom-call(bf16[256,1152]{1,0:T(8,128)(2,1)} %bitcast.23, ...), custom_call_target="tpu_custom_call" | custom-call | tf_op jit(solution)/shard_map/attend/pallas_call | solution.py:211
  86.1 99.4 %feed_forward.1 = (bf16[256,1152]{1,0:T(8,128)(2,1)}, f32[256,1152]{1,0:T(8,128)}, f32[1,1152]{1,0:T(1,128)}, f32[1,1152]{1,0:T(1,128)}, bf16[1152,1792]{1,0:T(8,128)(2,1)}, /*index=5*/bf16[4,54,1152]{2,1,0:T(8,128)(2,1)}) custom-call(bf16[256,1152]{1,0:T(8,128)(2,1)} %get-tuple-element.78.feed_in, bf16[8,128,1152]{2,1,0:T(8,128)(2,1)} %get-tuple-element.79.feeds_in, ...), custom_call_target="tpu_custom_call" | custom-call | tf_op jit(solution)/shard_map/feed_forward/pallas_call | solution.py:211
  185.5 72.1 %attend_back.1 = (bf16[256,1152]{1,0:T(8,128)(2,1)}, bf16[8,126,128]{2,1,0:T(8,128)(2,1)}, f32[9,1024]{1,0:T(8,128)}, f32[9,256]{1,0:T(8,128)}, f32[9,256]{1,0:T...) custom-call(bf16[256,1152]{1,0:T(8,128)(2,1)} %get-tuple-element.64.refs_0_, ...), custom_call_target="tpu_custom_call" | custom-call | tf_op jit(solution)/shard_map/attend_back/pallas_call | solution.py:211
  257.6 3.8 %finish.1 = (f32[9,6912]{1,0:T(8,128)}, f32[9,6912]{1,0:T(8,128)}, f32[1,9]{1,0:T(1,128)}, f32[1,9]{1,0:T(1,128)}, f32[1,9]{1,0:T(1,128)}, /*index=5*/f32[1,9]{1...) custom-call(bf16[8,126,128]{2,1,0:T(8,128)(2,1)} %get-tuple-element., ...), custom_call_target="tpu_custom_call" | custom-call | tf_op jit(solution)/shard_map/finish/pallas_call | solution.py:1473

commit v7 on v6

--- a/solution.py
+++ b/solution.py
@@ -805,15 +805,7 @@
         pick9, owns9[...] = gain_picks(9, D)
         pick2, owns2[...] = gain_picks(2, HEAD_DIM)
         v.gains[...] = jnp.zeros_like(v.gains)
-        merge[...] = jnp.zeros_like(merge)
-        for d in range(8):
-            for half, source in enumerate((gate_in, up_in)):
-                for i in range(16):
-                    to, start = WIDE * half + SLOT * i, 8 * PIECE * i + PIECE * d
-                    merge[0:9, to : to + PIECE] = source[:, start : start + PIECE].astype(jnp.float32)
-            for j in range(14):
-                flat[pl.ds(j, 9, 14), :] = merge[0:9, 128 * j : 128 * (j + 1)]
-            both_give[d] = flat[:126, :].astype(jnp.bfloat16)
+        merge[72:80, :] = jnp.zeros((8, merge.shape[1]), jnp.float32)
 
         own = lambda src, dst, at: pltpu.make_async_copy(src, dst, here.at[at])
         collect(got_kv, kv_box, kv_own)
@@ -838,6 +830,15 @@
         own(output_in, output_all.at[x, z, s], 2).wait()
         output_rest = ring_rest(output_all, mine, sems, kind=DirectGather)
         output_rest.first()
+        merge[0:16, :] = jnp.zeros((16, merge.shape[1]), jnp.float32)
+        for d in range(8):
+            for half, source in enumerate((gate_in, up_in)):
+                for i in range(16):
+                    to, start = WIDE * half + SLOT * i, 8 * PIECE * i + PIECE * d
+                    merge[0:9, to : to + PIECE] = source[:, start : start + PIECE].astype(jnp.float32)
+            for j in range(14):
+                flat[pl.ds(j, 9, 14), :] = merge[0:9, 128 * j : 128 * (j + 1)]
+            both_give[d] = flat[:126, :].astype(jnp.bfloat16)
         got_both = spread(both_give, both_box, True)
         copies = [
             own(my_kv(kv_own), my_kv(kv_all.at[x, z]), 0),
@@ -899,15 +900,16 @@
         kv_cross.close()
         assemble(kv_all, slice(1024, 1536))
 
-        near = Push(kv.at[2], kv.at[1], sems, after)
-        far = Push(kv.at[1], kv.at[0], sems, after)
-        key_value = dot(normed, v.qkv_weight[:, 1024:], 1, 0)
-        key = key_value[:, :HEAD_DIM]
-        v.key[...] = key
+        piece = lambda at, i: kv.at[at, :, pl.ds(HEAD_DIM * i, HEAD_DIM)]
+        near = [Push(piece(2, i), piece(1, i), sems, after) for i in range(2)]
+        far = [Push(piece(1, i), piece(0, i), sems, after) for i in range(2)]
+        key = dot(normed, v.qkv_weight[:, 1024:1280], 1, 0)
         key_turned = turn(unit_rows(key)[0] * v.gains[5:6, :HEAD_DIM], v.cosine[...], v.sine[...])
         kv[2, :, :HEAD_DIM] = key_turned.astype(jnp.bfloat16)
-        kv[2, :, HEAD_DIM:] = key_value[:, HEAD_DIM:].astype(jnp.bfloat16)
-        near.start()
+        near[0].start()
+        v.key[...] = key
+        kv[2, :, HEAD_DIM:] = dot(normed, v.qkv_weight[:, 1280:], 1, 0).astype(jnp.bfloat16)
+        near[1].start()
         output_y.relay()
         output_cross[1].start()
         output_cross[3].start()
@@ -935,8 +937,9 @@
         save(v.turned, saved.turned)
         save(v.normed, saved.normed)
         save(v.key, saved.key)
-        near.arrived()
-        far.start()
+        for i in range(2):
+            near[i].arrived()
+            far[i].start()
         both_rest.relay()
         output_y.last()
         output_cross[2].start()
@@ -952,7 +955,8 @@
                 v.output_weight[rows, :] = jnp.concatenate(pair, axis=0).astype(jnp.bfloat16)
 
         save(v.output_weight, saved.output_weight)
-        far.arrived()
+        for push in far:
+            push.arrived()
         v.kv[...] = kv[...].reshape(span, 2 * HEAD_DIM)
         save(v.kv, saved.kv)
         allowed = allowed_keys(q * tokens, beginning, tokens, span)
@@ -1011,7 +1015,7 @@
         rings += [query_rest, kv_rest, down_rest, output_rest, both_rest, output_y, feed_y]
         for ring in rings:
             ring.close()
-        for push in sent + output_cross + feed_cross + [near, far]:
+        for push in sent + output_cross + feed_cross + near + far:
             push.sent()
         for copy in saves:
             copy.wait()
@@ -1043,7 +1047,7 @@
     out = call(
         kernel, "attend", number, outs,
         [stream, doc_starts, own_query, own_key, own_value, own_output, own_gate, own_up, own_down, *norms],
-        scratch, 3 * 7 + 11 * 4 + 2 * 4 + 4 + 2 + 4 + 4, in_specs=[VMEM] * (9 + len(norms)), local=5 + 16,
+        scratch, 3 * 7 + 11 * 4 + 2 * 4 + 4 + 4 + 4 + 4, in_specs=[VMEM] * (9 + len(norms)), local=5 + 16,
     )
     return SimpleNamespace(**dict(zip(keep, out))), out[len(keep) :]
 
@@ -1243,13 +1247,16 @@
             inner = jnp.sum(probs * prob_grad, axis=-1, keepdims=True)
             b.score_low[rows, :] = (probs * (prob_grad - inner) * HEAD_DIM ** (-0.5)).astype(low)
             b.probs_low[rows, :] = probs.astype(low)
-        b.kv_grad[:, :HEAD_DIM] = dot(b.score_low[...], a.turned[...], 0, 0)
-        b.kv_grad[:, HEAD_DIM:] = dot(b.probs_low[...], b.mixed_grad[...], 0, 0)
-
-        halo_far = Push(b.halo_out.at[0], b.halo_in.at[0], sems, before)
-        halo_near = Push(b.halo_out.at[1], b.halo_in.at[1], sems, before)
-        b.halo_out[0] = b.kv_grad[:tokens, :].astype(low)
-        halo_far.start()
+
+        lanes_of_kv = [slice(0, HEAD_DIM), slice(HEAD_DIM, 2 * HEAD_DIM)]
+        piece = lambda ref, at, i: ref.at[at, :, pl.ds(HEAD_DIM * i, HEAD_DIM)]
+        halo_far, halo_near = (
+            [Push(piece(b.halo_out, at, i), piece(b.halo_in, at, i), sems, before) for i in range(2)] for at in range(2)
+        )
+        for i, (left, right) in enumerate(((b.score_low, a.turned), (b.probs_low, b.mixed_grad))):
+            b.kv_grad[:, lanes_of_kv[i]] = dot(left[...], right[...], 0, 0)
+            b.halo_out[0, :, lanes_of_kv[i]] = b.kv_grad[:tokens, lanes_of_kv[i]].astype(low)
+            halo_far[i].start()
 
         gain_grad = jnp.zeros((1, HEAD_DIM), wide)
         for h in range(HEADS):
@@ -1278,6 +1285,8 @@
 
         term(0, 512, held[QUERY][GIVE], held[QUERY][0])
         cross[QUERY].start()
+        rings[BOTH][0].second()
+        rings[DOWN][1].second()
 
         @pl.loop(0, 8)
         def _(i):
@@ -1298,21 +1307,23 @@
                         held[OUTPUT][GIVE][block] = value
 
         cross[OUTPUT].start()
-        rings[BOTH][0].second()
-        rings[DOWN][1].second()
-        halo_far.arrived()
-        b.halo_out[1] = (b.kv_grad[tokens : 2 * tokens, :] + b.halo_in[0].astype(wide)).astype(low)
-        halo_near.start()
+        for i, lanes in enumerate(lanes_of_kv):
+            halo_far[i].arrived()
+            summed = b.kv_grad[tokens : 2 * tokens, lanes] + b.halo_in[0, :, lanes].astype(wide)
+            b.halo_out[1, :, lanes] = summed.astype(low)
+            halo_near[i].start()
         for n in (QUERY, OUTPUT):
             cross[n].arrived()
             add_into(held[n][0], held[n][TAKE])
             rings[n][0].first()
-        halo_near.arrived()
-        kv_grad = b.kv_grad[2 * tokens :, :] + b.halo_in[1].astype(wide)
-        back = turn(kv_grad[:, :HEAD_DIM], cosine[...], -sine[...])
+        halo_near[0].arrived()
+        key_back = b.kv_grad[2 * tokens :, :HEAD_DIM] + b.halo_in[1, :, :HEAD_DIM].astype(wide)
+        back = turn(key_back, cosine[...], -sine[...])
         grad, own[4:5, HEAD_DIM : 2 * HEAD_DIM] = norm_grad(a.key[...], gains[5:6, :HEAD_DIM], back)
         b.qkv_low[:, 1024:1280] = grad.astype(low)
-        b.qkv_low[:, 1280:] = kv_grad[:, HEAD_DIM:].astype(low)
+        halo_near[1].arrived()
+        value_back = b.kv_grad[2 * tokens :, HEAD_DIM:] + b.halo_in[1, :, HEAD_DIM:].astype(wide)
+        b.qkv_low[:, 1280:] = value_back.astype(low)
         term(1024, 256, held[KV][GIVE], held[KV][0])
         cross[KV].start()
         for n in (QUERY, OUTPUT):
@@ -1320,8 +1331,6 @@
         cross[KV].arrived()
         add_into(held[KV][0], held[KV][TAKE])
         rings[KV][0].first()
-        rings[BOTH][0].third()
-        rings[BOTH][1].first()
         normed_grad = dot(b.qkv_low[...], a.qkv_weight[...], 1, 1)
         extra, own[0:1, :] = norm_grad(a.stream[...].astype(wide), gains[0:1, :], normed_grad)
         o.stream_grad[...] = (b.hidden_grad[...] + extra).astype(low)
@@ -1348,6 +1357,8 @@
             there = (y + dy) % 4, (c + dc) % 2
             steps.append((there, (y + 4 - dy) % 4 * 2 + (c + 2 - dc) % 2))
         finish = all_sum(0, b.shard_sums, s, steps, lambda t: device(x, t[0], z, t[1]))
+        rings[BOTH][0].third()
+        rings[BOTH][1].first()
         rings[KV][0].second()
         for n in (QUERY, OUTPUT):
             rings[n][0].third()
@@ -1434,12 +1445,12 @@
             for ring in pair:
                 if ring is not None:
                     ring.close()
-        for push in list(cross.values()) + pending + [halo_far, halo_near]:
+        for push in list(cross.values()) + pending + halo_far + halo_near:
             push.sent()
 
     ins = list(arrays.values())
     out = call(
-        kernel, "attend_back", number, list(results.values()), ins, [pltpu.VMEM(arrays[n].shape, arrays[n].dtype) for n in held_names] + list(room.values()) + sum(stores, []), 4 * 8 + 4 + 3 + 2 + 13 + 28,
+        kernel, "attend_back", number, list(results.values()), ins, [pltpu.VMEM(arrays[n].shape, arrays[n].dtype) for n in held_names] + list(room.values()) + sum(stores, []), 4 * 8 + 4 + 3 + 4 + 13 + 28,
         out_specs=[VMEM] * len(results), local=len(ins),
     )
     return dict(zip(results, out))

time: 262 us -> 259 us (0.989)
  Pallas kernels: 261 us -> 258 us
where the time goes in v7:
time: 259 us
  Pallas kernels  258 us (100%)
    pallas_call x3, Pallas kernels, call(): pl.pallas_call(kernel, name=name, out_shape=outs, in_specs=in_specs or [A...  255 us

profile of v7, /device:TPU:1, one launch (start us, length us, event | category | flops | bytes accessed | tf_op | source)
XLA Modules:
  0.0 259.3 jit_solution(13786455926784166468)
XLA Ops:
  0.7 85.5 %attend.1 = (bf16[256,1152]{1,0:T(8,128)(2,1)}, f32[1024,256]{1,0:T(8,128)}, f32[256,256]{1,0:T(8,128)}, bf16[1024,256]{1,0:T(8,128)(2,1)}, bf16[768,512]{1,0:T(...) custom-call(bf16[256,1152]{1,0:T(8,128)(2,1)} %bitcast.23, ...), custom_call_target="tpu_custom_call" | custom-call | tf_op jit(solution)/shard_map/attend/pallas_call | solution.py:211
  86.1 99.4 %feed_forward.1 = (bf16[256,1152]{1,0:T(8,128)(2,1)}, f32[256,1152]{1,0:T(8,128)}, f32[1,1152]{1,0:T(1,128)}, f32[1,1152]{1,0:T(1,128)}, bf16[1152,1792]{1,0:T(8,128)(2,1)}, /*index=5*/bf16[4,54,1152]{2,1,0:T(8,128)(2,1)}) custom-call(bf16[256,1152]{1,0:T(8,128)(2,1)} %get-tuple-element.78.feed_in, bf16[8,128,1152]{2,1,0:T(8,128)(2,1)} %get-tuple-element.79.feeds_in, ...), custom_call_target="tpu_custom_call" | custom-call | tf_op jit(solution)/shard_map/feed_forward/pallas_call | solution.py:211
  185.5 69.8 %attend_back.1 = (bf16[256,1152]{1,0:T(8,128)(2,1)}, bf16[8,126,128]{2,1,0:T(8,128)(2,1)}, f32[9,1024]{1,0:T(8,128)}, f32[9,256]{1,0:T(8,128)}, f32[9,256]{1,0:T...) custom-call(bf16[256,1152]{1,0:T(8,128)(2,1)} %get-tuple-element.64.refs_0_, ...), custom_call_target="tpu_custom_call" | custom-call | tf_op jit(solution)/shard_map/attend_back/pallas_call | solution.py:211
  255.4 3.8 %finish.1 = (f32[9,6912]{1,0:T(8,128)}, f32[9,6912]{1,0:T(8,128)}, f32[1,9]{1,0:T(1,128)}, f32[1,9]{1,0:T(1,128)}, f32[1,9]{1,0:T(1,128)}, /*index=5*/f32[1,9]{1...) custom-call(bf16[8,126,128]{2,1,0:T(8,128)(2,1)} %get-tuple-element., ...), custom_call_target="tpu_custom_call" | custom-call | tf_op jit(solution)/shard_map/finish/pallas_call | solution.py:1484
